TPU v7x, 32 devices: a whole 2x2x4 slice. The times are simulated.
32 devices in a mesh: dp: 16 (over z, y, x), tensor: 2 (over core).
Axes of the slice: x: 2, y: 2, z: 4, core: 2. Of those that a mesh axis runs over, the one named last changes fastest.
Arguments:
- layer_input: bfloat16 [8192, 1536], P('dp'), may hold values from -6 to 6
- doc_lengths: int32 [16, 4], P('dp'), may hold values from 0 to 512, as said below
- routes: int32 [8192, 8], P('dp'), may hold values from 0 to 15, all different within a row; in each aligned block of 512 rows (0 to 511, 512 to 1023, ...) at most 288 rows name the same one
- norm1_gain: bfloat16 [1536], replicated, may hold values from 0.5 to 1.5
- w_query: bfloat16 [1536, 1536], P(None, 'tensor'), may hold values from -0.15625 to 0.15625
- w_key: bfloat16 [1536, 512], P(None, 'tensor'), may hold values from -0.15625 to 0.15625
- w_value: bfloat16 [1536, 512], P(None, 'tensor'), may hold values from -0.15625 to 0.15625
- w_out: bfloat16 [1536, 1536], P('tensor'), may hold values from -0.625 to 0.625
- norm2_gain: bfloat16 [1536], replicated, may hold values from 0.5 to 1.5
- w_router: bfloat16 [1536, 16], replicated, may hold values from -0.078125 to 0.078125
- w_gate: bfloat16 [16, 1536, 512], P('dp', None, 'tensor'), may hold values from -0.15625 to 0.15625
- w_up: bfloat16 [16, 1536, 512], P('dp', None, 'tensor'), may hold values from -0.15625 to 0.15625
- w_down: bfloat16 [16, 512, 1536], P('dp', 'tensor'), may hold values from -0.75 to 0.75
- cotangent: bfloat16 [8192, 1536], P('dp'), may hold values from -6 to 6
Outputs:
- layer_output: bfloat16 [8192, 1536], P('dp')
- grad_x: bfloat16 [8192, 1536], P('dp')
- grad_norm1: float32 [1536], replicated
- grad_query: float32 [1536, 1536], P(None, 'tensor')
- grad_key: float32 [1536, 512], P(None, 'tensor')
- grad_value: float32 [1536, 512], P(None, 'tensor')
- grad_out: float32 [1536, 1536], P('tensor')
- grad_norm2: float32 [1536], replicated
- grad_router: float32 [1536, 16], replicated
- grad_gate: float32 [16, 1536, 512], P('dp', None, 'tensor')
- grad_up: float32 [16, 1536, 512], P('dp', None, 'tensor')
- grad_down: float32 [16, 512, 1536], P('dp', 'tensor')
Inputs may be any that keep to these rules, and one draw needn't show every extreme that they name: `doc_lengths`: each index of dp has 4 lengths summing to 512; a length may be zero; some index holds one sequence of all 512 tokens. `routes`: A token's 8 experts differ. In the 512 rows of one index of dp no expert is named more than 288 times, a bound that some block reaches.
All inputs are finite; a program needn't handle non-finite values.
Results may differ from a plain program's by a relative error of at most 0.02.
Values may be sent and summed in bfloat16 or wider, within the bound.
No kernel may reach another device: no remote copies, remote signals or barrier semaphores. Data moves between devices by JAX's collectives and lax.ppermute only.
A program may use at most 320 MiB of HBM per device.

v0:
```python
import math

import jax
import jax.numpy as jnp
from jax import lax
from jax.sharding import PartitionSpec as P

HEADS = 24
KV_HEADS = 8
HEAD_DIM = 64


EPSILON = 1e-06
NEGATIVE = -1e30


def rms_norm(values, gain):
    return values * lax.rsqrt(jnp.mean(values * values, axis=-1, keepdims=True) + EPSILON) * gain


def rotate(values, cosine, sine_table):
    middle = values.shape[-1] // 2
    first_half = values[..., :middle]
    second_half = values[..., middle:]
    return jnp.concatenate(
        [
            first_half * cosine - second_half * sine_table,
            second_half * cosine + first_half * sine_table,
        ],
        axis=-1,
    )


def unrotate(values, cosine, sine_table):
    middle = values.shape[-1] // 2
    first_half = values[..., :middle]
    second_half = values[..., middle:]
    return jnp.concatenate(
        [
            first_half * cosine + second_half * sine_table,
            second_half * cosine - first_half * sine_table,
        ],
        axis=-1,
    )


def frequencies():
    return jnp.exp(
        jnp.arange(HEAD_DIM // 2, dtype=jnp.float32) * (-2.0 * math.log(10000.0) / HEAD_DIM)
    )


def contract_rows(left, right):
    return lax.dot_general(
        left, right, (((0,), (0,)), ((), ())), preferred_element_type=jnp.float32
    )


def contract_cols(left, right):
    return lax.dot_general(
        left, right, (((1,), (1,)), ((), ())), preferred_element_type=jnp.float32
    )


def on_device(
    layer_input,
    doc_lengths,
    routes,
    norm1_gain,
    w_query,
    w_key,
    w_value,
    w_out,
    norm2_gain,
    w_router,
    w_gate,
    w_up,
    w_down,
    cotangent,
):
    tokens_here = layer_input.shape[0]
    model_width = layer_input.shape[1]
    n_data = lax.axis_size("dp")
    expert_count = w_router.shape[1]
    split_count = n_data // expert_count
    top_count = routes.shape[1]
    capacity = 9 * tokens_here * top_count // (8 * expert_count)
    groups = HEADS // KV_HEADS
    local_kv = w_key.shape[1] // HEAD_DIM
    score_scale = HEAD_DIM ** (-0.5)
    lengths = doc_lengths[0]
    token_index = jnp.arange(tokens_here, dtype=jnp.int32)
    seq_ends = jnp.cumsum(lengths)
    seq_starts = seq_ends - lengths
    segment = jnp.sum((token_index[:, None] >= seq_ends[None, :]).astype(jnp.int32), axis=1)
    slot_ids = jnp.arange(lengths.shape[0], dtype=jnp.int32)
    seq_first = jnp.sum(
        jnp.where(segment[:, None] == slot_ids[None, :], seq_starts[None, :], 0), axis=1
    )
    position = (token_index - seq_first).astype(jnp.float32)
    angles = position[:, None] * frequencies()[None, :]
    cosine = jnp.cos(angles)[:, None, :]
    sine_table = jnp.sin(angles)[:, None, :]
    inputs_f = layer_input.astype(jnp.float32)
    gain_one = norm1_gain.astype(jnp.float32)
    gain_two = norm2_gain.astype(jnp.float32)
    normed = rms_norm(inputs_f, gain_one).astype(jnp.bfloat16)
    query_pre = jnp.dot(normed, w_query, preferred_element_type=jnp.float32).reshape(
        tokens_here, -1, HEAD_DIM
    )
    queries = (
        rotate(query_pre, cosine, sine_table)
        .astype(jnp.bfloat16)
        .reshape(tokens_here, local_kv, groups, HEAD_DIM)
    )
    key_pre = jnp.dot(normed, w_key, preferred_element_type=jnp.float32).reshape(
        tokens_here, local_kv, HEAD_DIM
    )
    key_rows = rotate(key_pre, cosine, sine_table).astype(jnp.bfloat16)
    values = (
        jnp.dot(normed, w_value, preferred_element_type=jnp.float32)
        .astype(jnp.bfloat16)
        .reshape(tokens_here, local_kv, HEAD_DIM)
    )
    block_rows = min(512, tokens_here)

    def block_scores(query_block, row_start):
        row_ids = row_start + jnp.arange(block_rows, dtype=jnp.int32)
        visible = (segment[:, None] == segment[None, :]) & (
            row_ids[:, None] >= token_index[None, :]
        )
        raw_scores = (
            jnp.einsum("qhgd,shd->hgqs", query_block, key_rows, preferred_element_type=jnp.float32)
            * score_scale
        )
        return jnp.where(visible[None, None], raw_scores, NEGATIVE)

    block_id = 0
    row_start = block_id * block_rows
    scores = block_scores(queries, row_start)
    row_peak = jnp.max(scores, axis=-1, keepdims=True)
    log_total = row_peak + jnp.log(jnp.sum(jnp.exp(scores - row_peak), axis=-1, keepdims=True))
    probabilities = jnp.exp(scores - log_total).astype(jnp.bfloat16)
    mixed_blocks = jnp.einsum(
        "hgqs,shd->qhgd", probabilities, values, preferred_element_type=jnp.float32
    ).astype(jnp.bfloat16)
    lse_blocks = [log_total]
    mixed_heads = mixed_blocks.reshape(tokens_here, -1)
    attention = lax.psum(
        jnp.dot(mixed_heads, w_out, preferred_element_type=jnp.float32).astype(jnp.bfloat16),
        "tensor",
    ).astype(jnp.float32)
    hidden = inputs_f + attention
    normed_two = rms_norm(hidden, gain_two).astype(jnp.bfloat16)
    logits = jnp.dot(normed_two, w_router, preferred_element_type=jnp.float32)
    picked = routes[:, :, None] == jnp.arange(expert_count, dtype=jnp.int32)[None, None, :]
    chosen = jnp.sum(jnp.where(picked, logits[:, None, :], 0.0), axis=-1)
    gate_probs = jax.nn.softmax(chosen, axis=-1)
    flat_routes = routes.reshape(-1)
    flat_pick = (flat_routes[:, None] == jnp.arange(expert_count, dtype=jnp.int32)[None, :]).astype(
        jnp.int32
    )
    ranking = jnp.sum(jnp.cumsum(flat_pick, axis=0) * flat_pick, axis=1) - 1
    slot_of = flat_routes * capacity + ranking
    token_of = jnp.arange(tokens_here * top_count, dtype=jnp.int32) // top_count
    send_rows = (
        jnp.zeros((expert_count * capacity, model_width), jnp.bfloat16)
        .at[slot_of]
        .set(normed_two[token_of])
    )
    send_rows = send_rows.reshape(expert_count, capacity, model_width)
    arrived = lax.all_to_all(
        jnp.repeat(send_rows, split_count, axis=0), "dp", split_axis=0, concat_axis=0, tiled=True
    )
    expert_in = arrived.reshape(-1, model_width)
    gate_w = w_gate[0]
    up_w = w_up[0]
    down_w = w_down[0]
    gate_pre = jnp.dot(expert_in, gate_w, preferred_element_type=jnp.float32)
    up_pre = jnp.dot(expert_in, up_w, preferred_element_type=jnp.float32)
    activated = (jax.nn.silu(gate_pre) * up_pre).astype(jnp.bfloat16)
    partial_out = jnp.dot(activated, down_w, preferred_element_type=jnp.float32).astype(
        jnp.bfloat16
    )
    returned = lax.all_to_all(
        partial_out.reshape(n_data, capacity, model_width),
        "dp",
        split_axis=0,
        concat_axis=0,
        tiled=True,
    )
    returned_sum = jnp.sum(
        returned.reshape(expert_count, split_count, capacity, model_width),
        axis=1,
        dtype=jnp.float32,
    )
    routed = returned_sum.reshape(expert_count * capacity, model_width)[slot_of].reshape(
        tokens_here, top_count, model_width
    )
    mixture_part = jnp.einsum("tk,tkd->td", gate_probs, routed, preferred_element_type=jnp.float32)
    mixture = lax.psum(mixture_part.astype(jnp.bfloat16), "tensor").astype(jnp.float32)
    result_out = (hidden + mixture).astype(jnp.bfloat16)
    grad_out_f = cotangent.astype(jnp.float32)
    gate_grad_part = jnp.einsum(
        "td,tkd->tk", grad_out_f, routed, preferred_element_type=jnp.float32
    )
    slot_grads = (
        (gate_probs[:, :, None] * grad_out_f[:, None, :])
        .astype(jnp.bfloat16)
        .reshape(-1, model_width)
    )
    send_grads = (
        jnp.zeros((expert_count * capacity, model_width), jnp.bfloat16).at[slot_of].set(slot_grads)
    )
    send_grads = send_grads.reshape(expert_count, capacity, model_width)
    arrived_grads = lax.all_to_all(
        jnp.repeat(send_grads, split_count, axis=0), "dp", split_axis=0, concat_axis=0, tiled=True
    )
    grad_rows = arrived_grads.reshape(-1, model_width)
    grad_down_w = contract_rows(activated, grad_rows)
    act_grad = contract_cols(grad_rows, down_w)
    sigmoid_val = jax.nn.sigmoid(gate_pre)
    silu_val = gate_pre * sigmoid_val
    gate_grad = (act_grad * up_pre * sigmoid_val * (1.0 + gate_pre * (1.0 - sigmoid_val))).astype(
        jnp.bfloat16
    )
    up_grad = (act_grad * silu_val).astype(jnp.bfloat16)
    grad_gate_w = contract_rows(expert_in, gate_grad)
    grad_up_w = contract_rows(expert_in, up_grad)
    rows_back = (contract_cols(gate_grad, gate_w) + contract_cols(up_grad, up_w)).astype(
        jnp.bfloat16
    )
    back_arrived = lax.all_to_all(
        rows_back.reshape(n_data, capacity, model_width),
        "dp",
        split_axis=0,
        concat_axis=0,
        tiled=True,
    )
    back_sum = jnp.sum(
        back_arrived.reshape(expert_count, split_count, capacity, model_width),
        axis=1,
        dtype=jnp.float32,
    )
    routed_back = back_sum.reshape(-1, model_width)[slot_of].reshape(
        tokens_here, top_count, model_width
    )
    normed_grad_part = jnp.sum(routed_back, axis=1)
    normed_grad_moe, gate_grad_sum = (
        lax.psum(normed_grad_part.astype(jnp.bfloat16), "tensor").astype(jnp.float32),
        lax.psum(gate_grad_part.astype(jnp.bfloat16), "tensor").astype(jnp.float32),
    )
    chosen_grad = gate_probs * (
        gate_grad_sum - jnp.sum(gate_probs * gate_grad_sum, axis=-1, keepdims=True)
    )
    logit_grad = jnp.sum(jnp.where(picked, chosen_grad[:, :, None], 0.0), axis=1).astype(
        jnp.bfloat16
    )
    grad_router_w = contract_rows(normed_two, logit_grad)
    normed_grad = normed_grad_moe + contract_cols(logit_grad, w_router)
    pull_two = jax.vjp(rms_norm, hidden, gain_two)[1]
    hidden_norm_grad, grad_gain_two = pull_two(normed_grad)
    hidden_grad = grad_out_f + hidden_norm_grad
    hidden_grad_low = hidden_grad.astype(jnp.bfloat16)
    grad_out_w = contract_rows(mixed_heads, hidden_grad_low)
    mixed_grad = (
        contract_cols(hidden_grad_low, w_out)
        .astype(jnp.bfloat16)
        .reshape(tokens_here, local_kv, groups, HEAD_DIM)
    )
    block_id = 0
    row_start = block_id * block_rows
    query_block = queries
    scores = block_scores(query_block, row_start)
    probabilities = jnp.exp(scores - lse_blocks[block_id])
    probs_low = probabilities.astype(jnp.bfloat16)
    prob_grad = jnp.einsum("qhgd,shd->hgqs", mixed_grad, values, preferred_element_type=jnp.float32)
    balance = jnp.sum(probabilities * prob_grad, axis=-1, keepdims=True)
    score_grad = (probabilities * (prob_grad - balance) * score_scale).astype(jnp.bfloat16)
    query_grads = jnp.einsum(
        "hgqs,shd->qhgd", score_grad, key_rows, preferred_element_type=jnp.float32
    )
    key_grad = jnp.einsum(
        "hgqs,qhgd->shd", score_grad, query_block, preferred_element_type=jnp.float32
    )
    value_grad = jnp.einsum(
        "hgqs,qhgd->shd", probs_low, mixed_grad, preferred_element_type=jnp.float32
    )
    query_grad = query_grads.reshape(tokens_here, -1, HEAD_DIM)
    query_pre_grad = (
        unrotate(query_grad, cosine, sine_table).astype(jnp.bfloat16).reshape(tokens_here, -1)
    )
    key_pre_grad = (
        unrotate(key_grad, cosine, sine_table).astype(jnp.bfloat16).reshape(tokens_here, -1)
    )
    value_pre_grad = value_grad.astype(jnp.bfloat16).reshape(tokens_here, -1)
    grad_query_w = contract_rows(normed, query_pre_grad)
    grad_key_w = contract_rows(normed, key_pre_grad)
    grad_value_w = contract_rows(normed, value_pre_grad)
    normed_grad_heads = (
        contract_cols(query_pre_grad, w_query)
        + contract_cols(key_pre_grad, w_key)
        + contract_cols(value_pre_grad, w_value)
    )
    normed_grad_one = lax.psum(normed_grad_heads.astype(jnp.bfloat16), "tensor").astype(jnp.float32)
    pull_one = jax.vjp(rms_norm, inputs_f, gain_one)[1]
    input_norm_grad, grad_gain_one = pull_one(normed_grad_one)
    grad_input = (hidden_grad + input_norm_grad).astype(jnp.bfloat16)
    summed = lax.psum(
        (
            grad_query_w,
            grad_key_w,
            grad_value_w,
            grad_out_w,
            grad_router_w,
            grad_gain_one,
            grad_gain_two,
        ),
        "dp",
    )
    return (
        result_out,
        grad_input,
        summed[5],
        summed[0],
        summed[1],
        summed[2],
        summed[3],
        summed[6],
        summed[4],
        grad_gate_w[None],
        grad_up_w[None],
        grad_down_w[None],
    )


def solution(mesh):
    in_specs = (
        P("dp", None),
        P("dp", None),
        P("dp", None),
        P(),
        P(None, "tensor"),
        P(None, "tensor"),
        P(None, "tensor"),
        P("tensor", None),
        P(),
        P(),
        P("dp", None, "tensor"),
        P("dp", None, "tensor"),
        P("dp", "tensor", None),
        P("dp", None),
    )
    out_specs = (
        P("dp", None),
        P("dp", None),
        P(),
        P(None, "tensor"),
        P(None, "tensor"),
        P(None, "tensor"),
        P("tensor", None),
        P(),
        P(),
        P("dp", None, "tensor"),
        P("dp", None, "tensor"),
        P("dp", "tensor", None),
    )
    return jax.shard_map(
        on_device, mesh=mesh, in_specs=in_specs, out_specs=out_specs, check_vma=False
    )
```

profile of v0, /device:TPU:0, one launch (start us, length us, event | category | flops | bytes accessed | tf_op | source)
XLA Modules:
  0.0 2131.4 jit_solution(8185825112179462870)
XLA Ops:
  9.5 1.8 fusion.27
  12.0 3.2 convolution_convert_fusion.4
  16.0 1.6 fusion.89
  18.6 2.0 fusion.18
  20.7 2.6 exponential_reduce_fusion
  23.3 1.9 copy-done.15
  25.2 3.7 convolution_convert_fusion.3
  29.8 2.6 convolution_convert_fusion.1
  32.7 4.6 reduce-window.11
  38.9 16.7 all-reduce.8.cloned.1.call-done
  55.7 2.6 multiply_reduce_fusion.2
  58.5 1.7 multiply_convert_fusion.3
  60.2 73.4 %scatter_custom_fusion = bf16[4608,1536]{1,0:T(8,128)(2,1)} fusion(s32[4096]{0:T(1024)S(1)} %bitcast.250, bf16[512,1536]{1,0:T(8,128)(2,1)} %multiply_convert_fusion.3, s32[4096]{0:T(1024)S(1)} %broadcast_clamp_fusion.1, bf16[]{:T(256)} %constant.52.clone.1), kind=kCustom, calls=%fused_computation.23 | custom fusion | bytes 14156288 | tf_op jit(solution)/shard_map/scatter | solution.py:169
  133.6 314.5 %all_to_all.20 = bf16[16,288,1536]{2,1,0:T(8,128)(2,1)S(1)} all-to-all(bf16[16,288,1536]{2,1,0:T(8,128)(2,1)} %bitcast.224), channel_id=1, replica_groups=mesh['dp'=16,'tensor'=2] {'dp'}, dimensions={0} | all-to-all | bytes 28311552 | tf_op jit(solution)/shard_map/all_to_all | solution.py:172
  448.1 6.1 fusion.45
  454.5 7.4 multiply_convert_fusion.2
  461.9 7.1 convolution_convert_fusion
  469.0 5.0 all-to-all-start.1
  474.1 3.5 convert_element_type.154
  478.3 257.7 %all-to-all-done.1 = bf16[16,288,1536]{2,1,0:T(8,128)(2,1)} async-done(((bf16[16,288,1536]{2,1,0:T(8,128)(2,1)}), bf16[16,288,1536]{2,1,0:T(8,128)(2,1)}, u32[]{:S(2)}, u32[]{:S(2)}) %all-to-all-start.1) | async-done | bytes 14155808 | tf_op jit(solution)/shard_map/all_to_all | solution.py:185
  736.0 32.1 %gather_fusion = bf16[4096,1536]{1,0:T(8,128)(2,1)} fusion(bf16[4608,1536]{1,0:T(8,128)(2,1)} %bitcast.27, s32[4096]{0:T(1024)S(1)} %broadcast_clamp_fusion), kind=kCustom, calls=%fused_computation.1 | custom fusion | bytes 25182208 | tf_op jit(solution)/shard_map/gather | solution.py:197
  768.1 8.5 fusion.7
  776.7 2.9 psum.87
  780.5 28.4 %scatter_custom_fusion.1 = bf16[4608,1536]{1,0:T(8,128)(2,1)} fusion(s32[4096]{0:T(1024)S(1)} %bitcast.252, f32[512,1536]{1,0:T(8,128)} %convert_element_type.154, f32[4096]{0:T(1024)S(1)} %div.61, bf16[]{:T(256)} %constant.52.clone.1), kind=kCustom, calls=%fused_computation.12 | custom fusion | flops 12582912 | bytes 17317890 | tf_op jit(solution)/shard_map/scatter | solution.py:213
  808.9 370.2 %all_to_all.21 = bf16[16,288,1536]{2,1,0:T(8,128)(2,1)S(1)} all-to-all(bf16[16,288,1536]{2,1,0:T(8,128)(2,1)} %bitcast.223), channel_id=1, replica_groups=mesh['dp'=16,'tensor'=2] {'dp'}, dimensions={0} | all-to-all | bytes 28311552 | tf_op jit(solution)/shard_map/all_to_all | solution.py:216
  1179.1 13.6 multiply_convert_fusion
  1192.8 15.1 fusion.43
  1207.8 17.1 add_convert_fusion
  1224.9 5.1 all-to-all-start.3
  1230.3 262.0 %all-to-all-done.3 = bf16[16,288,1536]{2,1,0:T(8,128)(2,1)} async-done(((bf16[16,288,1536]{2,1,0:T(8,128)(2,1)}), bf16[16,288,1536]{2,1,0:T(8,128)(2,1)}, u32[]{:S(2)}, u32[]{:S(2)}) %all-to-all-start.3) | async-done | bytes 14155808 | tf_op jit(solution)/shard_map/all_to_all | solution.py:233
  1492.3 16.1 bitcast_convert_fusion
  1508.4 36.2 %gather_fusion.1 = f32[4096,1536]{1,0:T(8,128)} fusion(f32[4608,1536]{1,0:T(8,128)} %bitcast_convert_fusion, s32[4096]{0:T(1024)S(1)} %broadcast_clamp_fusion), kind=kCustom, calls=%fused_computation.2 | custom fusion | bytes 50348032 | tf_op jit(solution)/shard_map/gather | solution.py:245
  1544.6 14.3 bitcast_reduce_fusion
  1559.2 6.4 fusion.9
  1565.7 1.5 copy.79
  1567.2 68.7 %all-reduce.10.cloned.1.call-done = bf16[512,1536]{1,0:T(8,128)(2,1)} async-done(((bf16[512,1536]{1,0:T(8,128)(2,1)}), bf16[512,1536]{1,0:T(8,128)(2,1)}) %all-reduce.10.cloned.1.call-update) | async-done | bytes 1572880 | tf_op jit(solution)/shard_map/psum | solution.py:250
  1636.0 4.5 multiply_reduce_fusion
  1640.5 1.1 fusion.24
  1641.5 1.6 copy-done.7
  1643.2 2.3 convolution_convert_fusion.2
  1645.5 1.4 copy.57
  1646.9 7.0 fusion.35
  1653.9 6.3 fusion.96
  1660.2 24.3 %fusion.34 = f32[512,4,64]{0,2,1:T(8,128)S(1)} fusion(f32[4,512,512,3]{2,1,3,0:T(8,128)} %fusion.96, f32[4,512,512,3]{2,1,3,0:T(8,128)} %copy-done.15, f32[4,3,512]{2,1,0:T(4,128)} %copy-done.55, pred[512,512]{0,1:T(8,128)(4,1)S(1)} %copy-done.26, bf16[512,4,3,32]{0,3,2,1:T(8,128)(2,1)} %bitcast.244, bf16[512,4,3,32]{0,3,2,1:T(8,128)(2,1)} %bitcast.242), kind=kOutput, calls=%fused_computation.77 | convolution fusion | flops 438835712 | bytes 26763264 | tf_op jit(solution)/shard_map/hgqs,qhgd->shd/dot_general | solution.py:283
  1684.6 20.4 fusion.33
  1705.1 1.8 add_convert_fusion.2
  1707.1 1.4 fusion.97
  1709.8 1.8 fusion.30
  1711.8 2.5 fusion.98
  1714.3 3.4 fusion.83
  1717.7 1.9 fusion.85
  1719.6 3.8 fusion.87
  1723.4 3.6 fusion.47
  1727.1 12.1 convolution_bitcast_fusion.1
  1739.1 8.6 convolution_bitcast_fusion.2
  1747.8 5.0 convolution_bitcast_fusion
  1752.8 3.2 fusion.23
  1756.0 81.4 %all-reduce = (f32[1536]{0:T(1024)}, f32[1536]{0:T(1024)}) all-reduce(f32[1536]{0:T(1024)S(1)} %get-tuple-element.14, f32[1536]{0:T(1024)S(1)} %copy-done.63), channel_id=1, replica_groups=mesh['dp'=16,'tensor'=2] {'dp'}, use_global_device_ids=true, to_apply=%region_27.28 | all-reduce | flops 3072 | bytes 24576 | tf_op jit(solution)/shard_map/psum | solution.py:309
  1837.4 6.8 fusion.26
  1844.2 269.5 %all-reduce.12.cloned.1.call-done = (f32[1536,768]{1,0:T(8,128)}, f32[1536,256]{1,0:T(8,128)}, f32[1536,256]{1,0:T(8,128)}, f32[768,1536]{1,0:T(8,128)}, f32[1536,16]{0,1:T(8,128)}) async-done(((f32[1536,768]{1,0:T(8,128)}, f32[1536,256]{1,0:T(8,128)}, f32[1536,256]{1,0:T(8,128)}, f32[768,1536]{1,0:T(8,128)}, f32[1536,16]{0,1:T(8,128)}), (f32[1536,768]{1,0:T(8,128)}, f32[1536,256]{1,0:T(8,128)}, ...) | async-done | bytes 12681232 | tf_op jit(solution)/shard_map/psum | solution.py:309
  2113.7 5.0 copy.89
  2118.7 1.1 copy.90
  2120.7 1.1 copy.91
  2121.8 2.2 copy.92
  (207 shorter events, 13.5 us)
Async XLA Ops:
  7.2 22.6 %copy-start = (bf16[768,1536]{1,0:T(8,128)(2,1)S(1)}, bf16[768,1536]{1,0:T(8,128)(2,1)}, u32[]{:S(2)}) copy-start(bf16[768,1536]{1,0:T(8,128)(2,1)} %param.21) | copy-start | bytes 7077892
  7.2 8.0 copy-start.28
  7.2 48.5 %all-reduce.8.cloned.1.call-start = ((), (), s32[]{:S(2)}) async-start(), calls=%async_computation.4 | async-start | bytes 3145728 | tf_op jit(solution)/shard_map/psum | solution.py:149
  8.3 6.9 copy-start.2
  9.4 13.9 copy-start.25
  11.3 3.9 copy-start.59
  11.3 4.7 copy-start.51
  12.0 4.0 copy-start.40
  12.0 4.0 copy-start.66
  18.0 2.6 copy-start.42
  18.0 2.6 copy-start.44
  20.6 4.6 copy-start.15
  20.6 4.6 copy-start.38
  23.3 5.7 copy-start.55
  29.8 2.6 copy-start.36
  32.4 6.0 copy-start.65
  38.3 21.9 %copy-start.49 = (f32[1536]{0:T(1024)}, f32[1536]{0:T(1024)S(1)}, u32[]{:S(2)}) copy-start(f32[1536]{0:T(1024)S(1)} %convert_element_type.146) | copy-start | bytes 18436
  55.7 2.6 copy-start.3
  55.7 2.8 copy-start.9
  58.3 75.3 %copy-start.61 = (f32[512]{0:T(512)}, f32[512]{0:T(512)S(1)}, u32[]{:S(2)}) copy-start(f32[512]{0:T(512)S(1)} %multiply_reduce_fusion.2) | copy-start | bytes 6148
  58.5 75.1 %copy-start.57 = (f32[512]{0:T(512)}, f32[512]{0:T(512)S(1)}, u32[]{:S(2)}) copy-start(f32[512]{0:T(512)S(1)} %fusion.64) | copy-start | bytes 6148
  133.6 314.5 %copy-start.32 = (bf16[1,1536,256]{2,1,0:T(8,128)(2,1)S(1)}, bf16[1,1536,256]{2,1,0:T(8,128)(2,1)}, u32[]{:S(2)}) copy-start(bf16[1,1536,256]{2,1,0:T(8,128)(2,1)} %param.24) | copy-start | bytes 2359300
  448.1 6.4 copy-start.1
  448.1 6.4 copy-start.27
  454.5 7.4 copy-start.31
  461.9 7.1 copy-start.11
  469.0 267.0 %all-to-all-start.1 = ((bf16[16,288,1536]{2,1,0:T(8,128)(2,1)}), bf16[16,288,1536]{2,1,0:T(8,128)(2,1)}, u32[]{:S(2)}, u32[]{:S(2)}) async-start(bf16[16,288,1536]{2,1,0:T(8,128)(2,1)} %bitcast.222), calls=%async_computation.1 | async-start | bytes 28311552 | tf_op jit(solution)/shard_map/all_to_all | solution.py:185
  474.1 3.6 copy-start.13
  474.1 3.6 copy-start.53
  1179.1 13.7 copy-start.6
  1224.9 267.4 %all-to-all-start.3 = ((bf16[16,288,1536]{2,1,0:T(8,128)(2,1)}), bf16[16,288,1536]{2,1,0:T(8,128)(2,1)}, u32[]{:S(2)}, u32[]{:S(2)}) async-start(bf16[16,288,1536]{2,1,0:T(8,128)(2,1)} %bitcast.217), calls=%async_computation.3 | async-start | bytes 28311552 | tf_op jit(solution)/shard_map/all_to_all | solution.py:233
  1230.0 405.9 %all-reduce.10.cloned.1.call-start = ((), (), s32[]{:S(2)}) async-start(), calls=%async_computation.5 | async-start | bytes 3145728 | tf_op jit(solution)/shard_map/psum | solution.py:250
  1558.9 193.9 %all-reduce.14.cloned.1.call-start = ((), (), s32[]{:S(2)}) async-start(), calls=%async_computation.7 | async-start | bytes 6291456 | tf_op jit(solution)/shard_map/psum | solution.py:201
  1565.6 70.3 %copy-start.50 = (f32[1536]{0:T(1024)S(1)}, f32[1536]{0:T(1024)}, u32[]{:S(2)}) copy-start(f32[1536]{0:T(1024)} %copy-done.49) | copy-start | bytes 18436
  1565.6 70.3 %copy-start.54 = (bf16[1536,16]{0,1:T(8,128)(2,1)S(1)}, bf16[1536,16]{0,1:T(8,128)(2,1)}, u32[]{:S(2)}) copy-start(bf16[1536,16]{0,1:T(8,128)(2,1)} %param.23) | copy-start | bytes 147460
  1565.7 70.3 %copy-start.58 = (f32[512]{0:T(512)S(1)}, f32[512]{0:T(512)}, u32[]{:S(2)}) copy-start(f32[512]{0:T(512)} %copy-done.57) | copy-start | bytes 6148
  1567.2 73.2 %copy-start.62 = (f32[512]{0:T(512)S(1)}, f32[512]{0:T(512)}, u32[]{:S(2)}) copy-start(f32[512]{0:T(512)} %copy-done.61) | copy-start | bytes 6148
  1635.9 4.5 copy-start.4
  1635.9 4.5 copy-start.10
  1635.9 4.5 copy-start.16
  1643.1 3.7 copy-start.26
  1643.1 3.7 copy-start.56
  1646.9 7.0 copy-start.39
  1660.2 24.3 %copy-start.43 = (bf16[512,4,32]{0,2,1:T(8,128)(2,1)S(1)}, bf16[512,4,32]{0,2,1:T(8,128)(2,1)}, u32[]{:S(2)}) copy-start(bf16[512,4,32]{0,2,1:T(8,128)(2,1)} %copy-done.42) | copy-start | bytes 393220
  1660.2 24.3 %copy-start.45 = (bf16[512,4,32]{0,2,1:T(8,128)(2,1)S(1)}, bf16[512,4,32]{0,2,1:T(8,128)(2,1)}, u32[]{:S(2)}) copy-start(bf16[512,4,32]{0,2,1:T(8,128)(2,1)} %copy-done.44) | copy-start | bytes 393220
  1684.6 20.4 copy-start.20
  1684.6 20.4 copy-start.22
  1711.6 2.8 copy-start.41
  1711.6 2.8 copy-start.52
  1711.6 402.1 %all-reduce.12.cloned.1.call-start = ((), (), s32[]{:S(2)}) async-start(), calls=%async_computation.6 | async-start | bytes 25362432 | tf_op jit(solution)/shard_map/psum | solution.py:309
  1711.8 5.9 copy-start.5
  1719.6 3.8 copy-start.8
  1719.6 3.8 copy-start.18
  1727.0 12.1 copy-start.14
  1727.1 20.7 slice-start
  1727.1 20.7 slice-start.1
  1739.1 8.6 slice-start.2
  1739.1 8.6 slice-start.3
  1739.1 8.7 copy-start.12
  1752.8 3.2 copy-start.63
  1752.8 84.6 %copy-start.60 = (f32[512]{0:T(512)S(1)}, f32[512]{0:T(512)}, u32[]{:S(2)}) copy-start(f32[512]{0:T(512)} %copy-done.59) | copy-start | bytes 6148
  2113.7 8.1 slice-start.4
  2113.7 5.0 copy-start.24
  2113.7 8.1 slice-start.5
  (16 other events, 23.8 us)
Sparse Core Ops, SparseCore 0:
  32.5 23.0 all-reduce.7
  1559.0 76.8 all-reduce.9
  1711.7 24.4 all-reduce.13
  1744.7 368.9 all-reduce.11
where the time goes:
time: 2140 us; the launch traced here: 2130 us
  waiting for transfers between devices  875 us (41%)
  blocking collectives  769 us (36%)
  matrix products  205 us (10%)
  local copies, waits for them, and re-layouts  163 us (8%)
  other arithmetic  93.6 us (4%)
    all_to_all x1, blocking collectives, on_device(): lax.all_to_all(jnp.repeat(send_grads, split_count, axis=0), 'dp', split_a...  370 us
    all_to_all x1, blocking collectives, on_device(): lax.all_to_all(jnp.repeat(send_rows, split_count, axis=0), 'dp', split_ax...  315 us
    psum x1, waiting for transfers between devices, on_device(): lax.psum((grad_query_w, grad_key_w, grad_value_w, grad_out_w, grad_router...  270 us
    all_to_all x1, waiting for transfers between devices, on_device(): lax.all_to_all(rows_back.reshape(n_data, capacity, model_width), 'dp', sp...  262 us
    all_to_all x1, waiting for transfers between devices, on_device(): lax.all_to_all(partial_out.reshape(n_data, capacity, model_width), 'dp',...  258 us
    psum x1, blocking collectives, on_device(): lax.psum((grad_query_w, grad_key_w, grad_value_w, grad_out_w, grad_router...  81.4 us
    scatter x1, local copies, waits for them, and re-layouts, on_device(): send_rows = jnp.zeros((expert_count * capacity, model_width), jnp.bfloat1...  73.4 us
    psum x1, waiting for transfers between devices, on_device(): lax.psum(normed_grad_part.astype(jnp.bfloat16), 'tensor')  68.7 us
  transfers between devices with their start and end apart: 6, of which 5 were waited for; matrix products, arithmetic and copies ran while one was open for 3% of the time, Pallas kernels for 0%

commit v1 on v0

v1 whole, which is shorter than its diff:
```python
import functools
import math

import jax
import jax.numpy as jnp
from jax import lax
from jax.experimental import pallas as pl
from jax.experimental.pallas import tpu as pltpu
from jax.sharding import PartitionSpec as P

HEAD_DIM = 64
HEADS = 24
KV_HEADS = 8
EPSILON = 1e-06
NEGATIVE = -1e30
BF16 = jnp.bfloat16
F32 = jnp.float32
NN = (((1,), (0,)), ((), ()))
NT = (((1,), (1,)), ((), ()))
TN = (((0,), (0,)), ((), ()))
VMEM_LIMIT = 56 * 1024 * 1024


def dot(left, right, dims=NN):
    return lax.dot_general(left, right, dims, preferred_element_type=F32)


def routed_kernel(*refs):
    hn, dy = refs[0:4], refs[4:8]
    mask, onehot, router = refs[8:11]
    wg, wu, wd = refs[11:13], refs[13:15], refs[15:17]
    dx, mix = refs[17:21], refs[21:25]
    dgate, pre, act = refs[25:28]
    hbuf, dbuf, xbuf, mbuf, in_sem, out_sem = refs[28:]
    step = pl.program_id(0)
    slot = lax.rem(step, 2)

    def fetch(s, to):
        return (
            pltpu.make_async_copy(hn[s], hbuf.at[to], in_sem.at[to, 0]),
            pltpu.make_async_copy(dy[s], dbuf.at[to], in_sem.at[to, 1]),
        )

    def put(s, at):
        return (
            pltpu.make_async_copy(xbuf.at[at], dx[s], out_sem.at[at, 0]),
            pltpu.make_async_copy(mbuf.at[at], mix[s], out_sem.at[at, 1]),
        )

    @pl.when(step == 0)
    def _():
        for copy in fetch(0, 0):
            copy.start()

    for s in range(1, 4):

        @pl.when(step == s - 1)
        def _():
            for copy in fetch(s, s % 2):
                copy.start()

    for copy in fetch(0, slot):
        copy.wait()
    for s in range(2, 4):

        @pl.when(step == s)
        def _():
            for copy in put(s - 2, s % 2):
                copy.wait()

    rows = hbuf[slot]
    grads = dbuf[slot]
    logits = dot(rows, router[...], NT) + mask[...]
    weights = jnp.exp(logits - jnp.max(logits, axis=1, keepdims=True))
    gate = jnp.sum(weights * onehot[...], axis=1, keepdims=True) / jnp.sum(
        weights, axis=1, keepdims=True
    )
    width = wg[0].shape[1]
    back = mixed = gate_grad = None
    for c in range(2):
        gu = dot(rows, wg[c][...])
        up = dot(rows, wu[c][...])
        da = dot(grads, wd[c][...], NT)
        sig = 1.0 / (1.0 + jnp.exp(-gu))
        silu = gu * sig
        value = silu * up
        own = jnp.sum(value * da, axis=1, keepdims=True)
        gate_grad = own if c == 0 else gate_grad + own
        low = (value * gate).astype(BF16)
        act[:, c * width : (c + 1) * width] = low
        own = dot(low, wd[c][...])
        mixed = own if c == 0 else mixed + own
        da = da * gate
        dgu = (da * up * sig * (1.0 + gu * (1.0 - sig))).astype(BF16)
        dup = (da * silu).astype(BF16)
        pre[:, 2 * c * width : (2 * c + 1) * width] = dgu
        pre[:, (2 * c + 1) * width : (2 * c + 2) * width] = dup
        own = dot(dgu, wg[c][...], NT) + dot(dup, wu[c][...], NT)
        back = own if c == 0 else back + own
    xbuf[slot] = back.astype(BF16)
    mbuf[slot] = mixed.astype(BF16)
    dgate[...] = jnp.broadcast_to(gate_grad, dgate.shape)
    for s in range(4):

        @pl.when(step == s)
        def _():
            for copy in put(s, s % 2):
                copy.start()

    @pl.when(step == 3)
    def _():
        for copy in put(2, 0) + put(3, 1):
            copy.wait()


def routed(hn, dy, mask, onehot, router, wg, wu, wd):
    rows, model = hn[0].shape
    width = wg[0].shape[1]
    hbm = pl.BlockSpec(memory_space=pl.ANY)

    def full(array):
        return pl.BlockSpec(array.shape, lambda i: (0, 0))

    def tile(columns):
        return pl.BlockSpec((rows, columns), lambda i: (i, 0))

    out = jax.ShapeDtypeStruct
    got = pl.pallas_call(
        routed_kernel,
        grid=(4,),
        in_specs=[hbm] * 8
        + [tile(mask.shape[1]), full(onehot), full(router)]
        + [full(array) for array in (*wg, *wu, *wd)],
        out_specs=[hbm] * 8 + [tile(128), tile(4 * width), tile(2 * width)],
        out_shape=[out((rows, model), BF16)] * 8
        + [
            out((4 * rows, 128), F32),
            out((4 * rows, 4 * width), BF16),
            out((4 * rows, 2 * width), BF16),
        ],
        scratch_shapes=[pltpu.VMEM((2, rows, model), BF16)] * 4
        + [pltpu.SemaphoreType.DMA((2, 2))] * 2,
        compiler_params=pltpu.CompilerParams(vmem_limit_bytes=VMEM_LIMIT),
        cost_estimate=pl.CostEstimate(
            flops=4 * 12 * rows * model * 2 * width,
            bytes_accessed=16 * rows * model * 2,
            transcendentals=0,
        ),
        name="routed_rows",
    )(*hn, *dy, mask, onehot, router, *wg, *wu, *wd)
    return got[0:4], got[4:8], got[8], got[9], got[10]


def expert_grads_kernel(count, *refs):
    hn, dy = refs[:count], refs[count : 2 * count]
    blocks = count // 4
    pre = refs[2 * count : 2 * count + blocks]
    act = refs[2 * count + blocks : 2 * count + 2 * blocks]
    gu, gd, hbuf, dbuf, pbuf, abuf, sem = refs[2 * count + 2 * blocks :]
    step = pl.program_id(0)
    slot = lax.rem(step, 2)
    rows = hbuf.shape[1]

    def fetch(s, to):
        piece = pl.ds((s % 4) * rows, rows)
        return (
            pltpu.make_async_copy(hn[s], hbuf.at[to], sem.at[to, 0]),
            pltpu.make_async_copy(dy[s], dbuf.at[to], sem.at[to, 1]),
            pltpu.make_async_copy(pre[s // 4].at[piece], pbuf.at[to], sem.at[to, 2]),
            pltpu.make_async_copy(act[s // 4].at[piece], abuf.at[to], sem.at[to, 3]),
        )

    @pl.when(step == 0)
    def _():
        for copy in fetch(0, 0):
            copy.start()
        gu[...] = jnp.zeros_like(gu)
        gd[...] = jnp.zeros_like(gd)

    for s in range(1, count):

        @pl.when(step == s - 1)
        def _():
            for copy in fetch(s, s % 2):
                copy.start()

    for copy in fetch(0, slot):
        copy.wait()
    gu[...] += dot(hbuf[slot], pbuf[slot], TN)
    gd[...] += dot(abuf[slot], dbuf[slot], TN)


def expert_grads(hn, dy, pre, act):
    count = len(hn)
    rows, model = hn[0].shape
    four, two = pre[0].shape[1], act[0].shape[1]
    hbm = pl.BlockSpec(memory_space=pl.ANY)
    out = jax.ShapeDtypeStruct
    return pl.pallas_call(
        functools.partial(expert_grads_kernel, count),
        grid=(count,),
        in_specs=[hbm] * (2 * count + len(pre) + len(act)),
        out_specs=[
            pl.BlockSpec((model, four), lambda i: (0, 0)),
            pl.BlockSpec((two, model), lambda i: (0, 0)),
        ],
        out_shape=[out((model, four), F32), out((two, model), F32)],
        scratch_shapes=[
            pltpu.VMEM((2, rows, model), BF16),
            pltpu.VMEM((2, rows, model), BF16),
            pltpu.VMEM((2, rows, four), BF16),
            pltpu.VMEM((2, rows, two), BF16),
            pltpu.SemaphoreType.DMA((2, 4)),
        ],
        compiler_params=pltpu.CompilerParams(vmem_limit_bytes=VMEM_LIMIT),
        cost_estimate=pl.CostEstimate(
            flops=4 * count * rows * model * (four + two),
            bytes_accessed=2 * count * rows * model * 2,
            transcendentals=0,
        ),
        name="expert_grads",
    )(*hn, *dy, *pre, *act)


class Places:
    def __init__(self):
        self.count = lax.axis_size("dp")
        self.ring = self.count // 4
        me = lax.axis_index("dp")
        self.z, self.y, self.x = me // 4, (me // 2) % 2, me % 2
        self.t = lax.axis_index("tensor")

    def by_x(self, array):
        return lax.ppermute(array, "dp", [(i, i ^ 1) for i in range(self.count)])

    def by_y(self, array):
        return lax.ppermute(array, "dp", [(i, i ^ 2) for i in range(self.count)])

    def by_z(self, array):
        return lax.ppermute(array, "dp", [(i, (i + 4) % self.count) for i in range(self.count)])

    def by_t(self, array):
        return lax.ppermute(array, "tensor", [(0, 1), (1, 0)])

    def spread(self, first, second):
        near_one = jnp.concatenate([first, self.by_x(first)], axis=0)
        near_two = jnp.concatenate([second, self.by_y(second)], axis=0)
        return near_one, self.by_y(near_one), near_two, self.by_x(near_two)

    def collect(self, near_one, far_one, near_two, far_two):
        half = near_one.shape[0] // 2
        one = add(near_one, self.by_y(far_one))
        two = add(near_two, self.by_x(far_two))
        return (
            add(one[:half], self.by_x(one[half:])),
            add(two[:half], self.by_y(two[half:])),
        )

    def absolute(self, relative):
        relative = jnp.where(self.y == 1, jnp.flip(relative, 1), relative)
        relative = jnp.where(self.x == 1, jnp.flip(relative, 2), relative)
        return jnp.roll(jnp.flip(relative, 0), self.z + 1, axis=0)

    def sum_all(self, array):
        rows, columns = array.shape
        part = rows // self.count
        grid = array.reshape(self.ring, 2, 2, part, columns)
        half = columns // 2

        def split(value, place, axis):
            keep = lax.dynamic_index_in_dim(value, place, axis, keepdims=False)
            send = lax.dynamic_index_in_dim(value, 1 - place, axis, keepdims=False)
            return keep, send

        def join(own, other, place, axis):
            return jnp.where(
                place == 0, jnp.stack([own, other], axis), jnp.stack([other, own], axis)
            )

        keep, send = split(grid[..., :half], self.x, 2)
        one = add(keep, self.by_x(send))
        keep, send = split(grid[..., half:], self.y, 1)
        two = add(keep, self.by_y(send))
        keep, send = split(one, self.y, 1)
        one = add(keep, self.by_y(send))
        keep, send = split(two, self.x, 1)
        two = add(keep, self.by_x(send))
        both = jnp.concatenate([one, two], axis=-1)

        def at(j):
            return lax.dynamic_index_in_dim(both, (self.z - j) % self.ring, 0, keepdims=False)

        total = at(1 % self.ring)
        for j in range(2, self.ring + 1):
            total = add(self.by_z(total), at(j % self.ring))
        got = [total]
        for _ in range(self.ring - 1):
            got.append(self.by_z(got[-1]))
        got = jnp.stack(got)
        got = jnp.stack(
            [
                lax.dynamic_index_in_dim(got, (self.z - i) % self.ring, 0, keepdims=False)
                for i in range(self.ring)
            ]
        )
        one, two = got[..., :half], got[..., half:]
        one = join(one, self.by_y(one), self.y, 1)
        two = join(two, self.by_x(two), self.x, 1)
        one = join(one, self.by_x(one), self.x, 2)
        two = join(two, self.by_y(two), self.y, 1)
        return jnp.concatenate([one, two], axis=-1).reshape(rows, columns)

    def sum_small(self, array):
        array = array + self.by_t(array)
        step = 1
        while step < self.count:
            array = array + lax.ppermute(
                array, "dp", [(i, i ^ step) for i in range(self.count)]
            )
            step *= 2
        return array

    def own_half(self, array):
        half = array.shape[0] // 2
        return lax.dynamic_slice_in_dim(array, self.t * half, half, 0)

    def other_half(self, array):
        half = array.shape[0] // 2
        return lax.dynamic_slice_in_dim(array, (1 - self.t) * half, half, 0)

    def sum_halves(self, array):
        return self.own_half(array).astype(F32) + self.by_t(self.other_half(array)).astype(F32)

    def both_halves(self, array):
        other = self.by_t(array)
        return jnp.where(
            self.t == 0,
            jnp.concatenate([array, other], axis=0),
            jnp.concatenate([other, array], axis=0),
        )


def add(left, right):
    return (left.astype(F32) + right.astype(F32)).astype(left.dtype)


def rotate(values, cosine, sine):
    middle = values.shape[-1] // 2
    first, second = values[..., :middle], values[..., middle:]
    return jnp.concatenate(
        [first * cosine - second * sine, second * cosine + first * sine], axis=-1
    )


def frequencies():
    return jnp.exp(
        jnp.arange(HEAD_DIM // 2, dtype=F32) * (-2.0 * math.log(10000.0) / HEAD_DIM)
    )


def norm_back(values, inverse, gain, grad):
    scaled = gain * grad
    mean = jnp.mean(scaled * values, axis=-1, keepdims=True)
    return inverse * scaled - values * (inverse * inverse * inverse * mean)


def inverse_rms(values):
    return lax.rsqrt(jnp.mean(values * values, axis=-1, keepdims=True) + EPSILON)


def on_device(
    layer_input,
    doc_lengths,
    routes,
    norm1_gain,
    w_query,
    w_key,
    w_value,
    w_out,
    norm2_gain,
    w_router,
    w_gate,
    w_up,
    w_down,
    cotangent,
):
    places = Places()
    ring, count = places.ring, places.count
    tokens, model = layer_input.shape
    half = tokens // 2
    quarter = half // 2
    experts = w_router.shape[1]
    splits = count // experts
    groups = HEADS // KV_HEADS
    local_kv = w_key.shape[1] // HEAD_DIM
    scale = HEAD_DIM ** (-0.5)
    gain_one = norm1_gain.astype(F32)
    gain_two = norm2_gain.astype(F32)

    dy = places.own_half(cotangent)
    current = (dy[:quarter], dy[quarter:])
    dy_blocks = []
    for j in range(ring):
        dy_blocks.append(places.spread(*current))
        if j < ring - 1:
            current = tuple(places.by_z(piece) for piece in current)

    wg = (w_gate[0], places.by_t(w_gate[0]))
    wu = (w_up[0], places.by_t(w_up[0]))
    wd = (w_down[0], places.by_t(w_down[0]))

    lengths = doc_lengths[0]
    index = jnp.arange(tokens, dtype=jnp.int32)
    ends = jnp.cumsum(lengths)
    starts = ends - lengths
    segment = jnp.sum((index[:, None] >= ends[None, :]).astype(jnp.int32), axis=1)
    slots = jnp.arange(lengths.shape[0], dtype=jnp.int32)
    first = jnp.sum(jnp.where(segment[:, None] == slots[None, :], starts[None, :], 0), axis=1)
    angles = (index - first).astype(F32)[:, None] * frequencies()[None, :]
    cosine = jnp.cos(angles)[:, None, :]
    sine = jnp.sin(angles)[:, None, :]
    inputs = layer_input.astype(F32)
    inverse_one = inverse_rms(inputs)
    normed = (inputs * inverse_one * gain_one).astype(BF16)
    queries = rotate(dot(normed, w_query).reshape(tokens, -1, HEAD_DIM), cosine, sine)
    queries = queries.astype(BF16).reshape(tokens, local_kv, groups, HEAD_DIM)
    keys = rotate(dot(normed, w_key).reshape(tokens, local_kv, HEAD_DIM), cosine, sine)
    keys = keys.astype(BF16)
    values = dot(normed, w_value).astype(BF16).reshape(tokens, local_kv, HEAD_DIM)
    visible = (segment[:, None] == segment[None, :]) & (index[:, None] >= index[None, :])

    def scores_of():
        raw = jnp.einsum("qhgd,shd->hgqs", queries, keys, preferred_element_type=F32)
        return jnp.where(visible[None, None], raw * scale, NEGATIVE)

    scores = scores_of()
    peak = jnp.max(scores, axis=-1, keepdims=True)
    log_total = peak + jnp.log(jnp.sum(jnp.exp(scores - peak), axis=-1, keepdims=True))
    probabilities = jnp.exp(scores - log_total).astype(BF16)
    mixed_heads = jnp.einsum(
        "hgqs,shd->qhgd", probabilities, values, preferred_element_type=F32
    )
    mixed_heads = mixed_heads.astype(BF16).reshape(tokens, -1)
    attention = places.sum_halves(dot(mixed_heads, w_out).astype(BF16))
    inputs_half = places.own_half(layer_input).astype(F32)
    hidden = inputs_half + attention
    inverse_two = inverse_rms(hidden)
    normed_two = (hidden * inverse_two * gain_two).astype(BF16)

    named = jnp.any(
        places.own_half(routes)[:, :, None] == jnp.arange(experts, dtype=jnp.int32), axis=1
    )
    bits = jnp.sum(
        jnp.where(named, jnp.left_shift(1, jnp.arange(experts, dtype=jnp.int32)), 0), axis=1
    )
    bits = lax.all_to_all(
        jnp.broadcast_to(bits[None], (count, half)), "dp", split_axis=0, concat_axis=0, tiled=True
    )
    bits = places.absolute(bits.reshape(ring, 2, 2, 2, quarter))
    order = ((0, 0, 0), (0, 1, 0), (1, 0, 0), (1, 1, 0), (0, 0, 1), (1, 0, 1), (0, 1, 1), (1, 1, 1))
    lanes = jnp.arange(experts, dtype=jnp.int32)
    router_rows = w_router.T
    expert = lax.axis_index("dp") // splits
    onehot = (lanes == expert).astype(F32)[None]

    current = (normed_two[:quarter], normed_two[quarter:])
    hn_blocks = [None] * ring
    results = [None] * ring
    for j in range(ring):
        hn_blocks[j] = places.spread(*current)
        if j < ring - 1:
            current = tuple(places.by_z(piece) for piece in current)
        flags = jnp.concatenate([bits[(j, *at)] for at in order])
        mask = jnp.where(
            jnp.bitwise_and(jnp.right_shift(flags[:, None], lanes), 1) == 1, 0.0, NEGATIVE
        )
        results[j] = routed(
            hn_blocks[j], dy_blocks[j], mask, onehot, router_rows, wg, wu, wd
        )

    def home(which):
        total = None
        for step in range(1, ring + 1):
            got = places.collect(*results[step % ring][which])
            if total is None:
                total = got
            else:
                total = tuple(add(places.by_z(a), b) for a, b in zip(total, got))
        return jnp.concatenate(total, axis=0)

    normed_grad = home(0)
    gate_grads = jnp.stack(
        [results[j][2][:, 0].reshape(len(order), quarter) for j in range(ring)]
    )
    inverse_order = {at: i for i, at in enumerate(order)}
    gate_grads = jnp.stack(
        [gate_grads[:, inverse_order[(y, x, h)]] for y in (0, 1) for x in (0, 1) for h in (0, 1)],
        axis=1,
    ).reshape(ring, 2, 2, half)
    gate_grads = places.absolute(gate_grads).reshape(count, half)
    gate_grads = lax.all_to_all(gate_grads, "dp", split_axis=0, concat_axis=0, tiled=True)
    gate_grads = jnp.sum(gate_grads.reshape(experts, splits, half), axis=1).T

    logits = jnp.where(named, dot(normed_two, w_router), NEGATIVE)
    gates = jax.nn.softmax(logits, axis=-1)
    logit_grad = gates * (gate_grads - jnp.sum(gates * gate_grads, axis=-1, keepdims=True))
    logit_grad = logit_grad.astype(BF16)
    grad_router = dot(logit_grad, normed_two, TN)
    normed_grad = normed_grad.astype(F32) + dot(logit_grad, w_router, NT)
    grad_gain_two = jnp.sum(normed_grad * hidden * inverse_two, axis=0)
    hidden_grad = dy.astype(F32) + norm_back(hidden, inverse_two, gain_two, normed_grad)
    hidden_low = places.both_halves(hidden_grad.astype(BF16))
    grad_out = places.sum_all(dot(mixed_heads, hidden_low, TN).astype(BF16))

    mixed_grad = dot(hidden_low, w_out, NT).astype(BF16)
    mixed_grad = mixed_grad.reshape(tokens, local_kv, groups, HEAD_DIM)
    probabilities = jnp.exp(scores_of() - log_total)
    prob_grad = jnp.einsum("qhgd,shd->hgqs", mixed_grad, values, preferred_element_type=F32)
    balance = jnp.sum(probabilities * prob_grad, axis=-1, keepdims=True)
    score_grad = (probabilities * (prob_grad - balance) * scale).astype(BF16)
    query_grad = jnp.einsum("hgqs,shd->qhgd", score_grad, keys, preferred_element_type=F32)
    key_grad = jnp.einsum("hgqs,qhgd->shd", score_grad, queries, preferred_element_type=F32)
    value_grad = jnp.einsum(
        "hgqs,qhgd->shd", probabilities.astype(BF16), mixed_grad, preferred_element_type=F32
    )
    query_grad = rotate(query_grad.reshape(tokens, -1, HEAD_DIM), cosine, -sine)
    query_grad = query_grad.astype(BF16).reshape(tokens, -1)
    key_grad = rotate(key_grad, cosine, -sine).astype(BF16).reshape(tokens, -1)
    value_grad = value_grad.astype(BF16).reshape(tokens, -1)
    grad_heads = jnp.concatenate([query_grad, key_grad, value_grad], axis=1)
    grad_heads_w = places.sum_all(dot(normed, grad_heads, TN).astype(BF16)).astype(F32)
    normed_grad_one = (
        dot(query_grad, w_query, NT) + dot(key_grad, w_key, NT) + dot(value_grad, w_value, NT)
    )
    normed_grad_one = places.sum_halves(normed_grad_one.astype(BF16))
    inverse_half = inverse_rms(inputs_half)
    grad_gain_one = jnp.sum(normed_grad_one * inputs_half * inverse_half, axis=0)
    grad_input = hidden_grad + norm_back(inputs_half, inverse_half, gain_one, normed_grad_one)
    grad_input = places.both_halves(grad_input.astype(BF16))

    small = places.sum_small(
        jnp.concatenate([grad_router, grad_gain_one[None], grad_gain_two[None]], axis=0)
    )
    mixture = home(1).astype(F32)
    output = places.both_halves((hidden + mixture).astype(BF16))

    grad_gu = grad_d = None
    for j in range(0, ring, 4):
        span = range(j, min(j + 4, ring))
        got = expert_grads(
            [piece for i in span for piece in hn_blocks[i]],
            [piece for i in span for piece in dy_blocks[i]],
            [results[i][3] for i in span],
            [results[i][4] for i in span],
        )
        grad_gu = got[0] if grad_gu is None else grad_gu + got[0]
        grad_d = got[1] if grad_d is None else grad_d + got[1]
    width = wg[0].shape[1]
    grad_gu = grad_gu[:, : 2 * width] + places.by_t(grad_gu[:, 2 * width :])
    grad_d = grad_d[:width] + places.by_t(grad_d[width:])
    query_width, key_width = w_query.shape[1], w_key.shape[1]
    return (
        output,
        grad_input,
        small[experts],
        grad_heads_w[:, :query_width],
        grad_heads_w[:, query_width : query_width + key_width],
        grad_heads_w[:, query_width + key_width :],
        grad_out.astype(F32),
        small[experts + 1],
        small[:experts].T,
        grad_gu[None, :, :width],
        grad_gu[None, :, width:],
        grad_d[None],
    )


def solution(mesh):
    in_specs = (
        P("dp", None),
        P("dp", None),
        P("dp", None),
        P(),
        P(None, "tensor"),
        P(None, "tensor"),
        P(None, "tensor"),
        P("tensor", None),
        P(),
        P(),
        P("dp", None, "tensor"),
        P("dp", None, "tensor"),
        P("dp", "tensor", None),
        P("dp", None),
    )
    out_specs = (
        P("dp", None),
        P("dp", None),
        P(),
        P(None, "tensor"),
        P(None, "tensor"),
        P(None, "tensor"),
        P("tensor", None),
        P(),
        P(),
        P("dp", None, "tensor"),
        P("dp", None, "tensor"),
        P("dp", "tensor", None),
    )
    return jax.shard_map(
        on_device, mesh=mesh, in_specs=in_specs, out_specs=out_specs, check_vma=False
    )
```

time: 2140 us -> 914 us (0.43)
  blocking collectives: 769 us -> 0 us
  waiting for transfers between devices: 875 us -> 459 us
  starting transfers between devices: 10.7 us -> 137 us
  matrix products: 205 us -> 81.9 us
  Pallas kernels: 0 us -> 108 us
  local copies, waits for them, and re-layouts: 163 us -> 62.7 us
  other arithmetic: 93.6 us -> 51 us
    all_to_all x2 -> x0, blocking collectives: 685 us -> none  [the longest x1 370 us: on_device(): lax.all_to_all(jnp.repeat(send_grads, split_count, axis=0), 'dp', split_a...]
    all_to_all x2, waiting for transfers between devices: 520 us -> 0.01 us  [the longest x1 0.01 us: on_device(): lax.all_to_all(jnp.broadcast_to(bits[None], (count, half)), 'dp', split_a...]
    ppermute x0 -> x131, waiting for transfers between devices: none -> 459 us  [the longest x36 194 us: by_z(): lax.ppermute(array, 'dp', [(i, (i + 4) % self.count) for i in range(self....]
    psum x4 -> x0, waiting for transfers between devices: 355 us -> none  [the longest x1 270 us: on_device(): lax.psum((grad_query_w, grad_key_w, grad_value_w, grad_out_w, grad_router...]
    ppermute x0 -> x131, starting transfers between devices: none -> 128 us  [the longest x40 57.5 us: by_y(): return lax.ppermute(array, 'dp', [(i, i ^ 2) for i in range(self.count)])]
    dot_general x31 -> x18, matrix products: 201 us -> 74 us  [the longest x1 20.8 us: on_device(): jnp.einsum('hgqs,shd->qhgd', score_grad, keys, preferred_element_type=F32)]
    pallas_call x0 -> x5, Pallas kernels: none -> 108 us  [the longest x4 78.8 us: routed(): pl.pallas_call(routed_kernel, grid=(4,), in_specs=[hbm] * 8 + [tile(mask....]
    psum x2 -> x0, blocking collectives: 84.3 us -> none  [the longest x1 81.4 us: on_device(): lax.psum((grad_query_w, grad_key_w, grad_value_w, grad_out_w, grad_router...]
  transfers between devices with their start and end apart: 6 -> 133, of which waited for: 5 -> 61; matrix products, arithmetic and copies ran while one was open for 3% -> 19% of each run, Pallas kernels for 0% -> 12%
where the time goes in v1:
time: 914 us; the launch traced here: 903 us
  waiting for transfers between devices  459 us (50%)
  starting transfers between devices  137 us (15%)
  Pallas kernels  108 us (12%)
  matrix products  81.9 us (9%)
  local copies, waits for them, and re-layouts  62.7 us (7%)
  other arithmetic  51 us (6%)
    ppermute x36, waiting for transfers between devices, by_z(): lax.ppermute(array, 'dp', [(i, (i + 4) % self.count) for i in range(self....  194 us
    ppermute x40, waiting for transfers between devices, by_y(): return lax.ppermute(array, 'dp', [(i, i ^ 2) for i in range(self.count)])  137 us
    ppermute x40, waiting for transfers between devices, by_x(): return lax.ppermute(array, 'dp', [(i, i ^ 1) for i in range(self.count)])  115 us
    pallas_call x4, Pallas kernels, routed(): pl.pallas_call(routed_kernel, grid=(4,), in_specs=[hbm] * 8 + [tile(mask....  78.8 us
    ppermute x40, starting transfers between devices, by_y(): return lax.ppermute(array, 'dp', [(i, i ^ 2) for i in range(self.count)])  57.5 us
    ppermute x40, starting transfers between devices, by_x(): return lax.ppermute(array, 'dp', [(i, i ^ 1) for i in range(self.count)])  46.7 us
    unnamed x305, local copies, waits for them, and re-layouts  29.7 us
    pallas_call x1, Pallas kernels, expert_grads(): pl.pallas_call(functools.partial(expert_grads_kernel, count), grid=(count...  29.5 us
  transfers between devices with their start and end apart: 133, of which 61 were waited for; matrix products, arithmetic and copies ran while one was open for 19% of the time, Pallas kernels for 12%

profile of v1, /device:TPU:0, one launch (start us, length us, event | category | flops | bytes accessed | tf_op | source)
XLA Modules:
  0.0 903.0 jit_solution(7161993996964561064)
XLA Ops:
  10.4 3.6 all-to-all-start
  30.8 7.8 convolution_convert_fusion.4
  66.7 13.3 %collective-permute-done.25 = bf16[128,1536]{1,0:T(8,128)(2,1)S(1)} collective-permute-done((bf16[128,1536]{1,0:T(8,128)(2,1)}, bf16[128,1536]{1,0:T(8,128)(2,1)S(1)}, u32[]{:S(2)}, u32[]{:S(2)}) %collective-permute-start.25) | collective-permute-done | bytes 393248 | tf_op jit(solution)/shard_map/ppermute | solution.py:240
  84.8 6.3 collective-permute-done.8
  96.5 16.8 %collective-permute-done.40 = bf16[128,1536]{1,0:T(8,128)(2,1)S(1)} collective-permute-done((bf16[128,1536]{1,0:T(8,128)(2,1)S(1)}, bf16[128,1536]{1,0:T(8,128)(2,1)S(1)}, u32[]{:S(2)}, u32[]{:S(2)}) %collective-permute-start.40) | collective-permute-done | bytes 393248 | tf_op jit(solution)/shard_map/ppermute | solution.py:240
  113.4 8.4 collective-permute-done.43
  123.4 4.7 collective-permute-done.1
  131.2 6.8 collective-permute-done.26
  142.8 9.1 %collective-permute-done.22 = bf16[128,1536]{1,0:T(8,128)(2,1)S(1)} collective-permute-done((bf16[128,1536]{1,0:T(8,128)(2,1)S(1)}, bf16[128,1536]{1,0:T(8,128)(2,1)S(1)}, u32[]{:S(2)}, u32[]{:S(2)}) %collective-permute-start.22) | collective-permute-done | bytes 393248 | tf_op jit(solution)/shard_map/ppermute | solution.py:240
  153.4 3.7 collective-permute-done.19
  168.9 12.0 %collective-permute-done.54.refs_5_.refs_17_ = bf16[256,1536]{1,0:T(8,128)(2,1)S(1)} collective-permute-done((bf16[256,1536]{1,0:T(8,128)(2,1)S(1)}, bf16[256,1536]{1,0:T(8,128)(2,1)S(1)}, u32[]{:S(2)}, u32[]{:S(2)}) %collective-permute-start.54) | collective-permute-done | bytes 786464 | tf_op jit(solution)/shard_map/ppermute | solution.py:237
  183.0 14.8 %collective-permute-done.50.refs_1_ = bf16[256,1536]{1,0:T(8,128)(2,1)S(1)} collective-permute-done((bf16[256,1536]{1,0:T(8,128)(2,1)S(1)}, bf16[256,1536]{1,0:T(8,128)(2,1)S(1)}, u32[]{:S(2)}, u32[]{:S(2)}) %collective-permute-start.50) | collective-permute-done | bytes 786464 | tf_op jit(solution)/shard_map/ppermute | solution.py:237
  202.4 19.9 %routed_rows.7 = (bf16[256,1536]{1,0:T(8,128)(2,1)}, bf16[256,1536]{1,0:T(8,128)(2,1)}, bf16[256,1536]{1,0:T(8,128)(2,1)}, bf16[256,1536]{1,0:T(8,128)(2,1)}, bf...) custom-call(bf16[256,1536]{1,0:T(8,128)(2,1)} %copy-done.46, ...), custom_call_target="tpu_custom_call" | custom-call | flops 9663676416 | bytes 12582912 | tf_op jit(solution)/shard_map/routed_rows/pallas_call | solution.py:128
  228.8 20.3 %collective-permute-done.23 = bf16[128,1536]{1,0:T(8,128)(2,1)S(1)} collective-permute-done((bf16[128,1536]{1,0:T(8,128)(2,1)S(1)}, bf16[128,1536]{1,0:T(8,128)(2,1)S(1)}, u32[]{:S(2)}, u32[]{:S(2)}) %collective-permute-start.23) | collective-permute-done | bytes 393248 | tf_op jit(solution)/shard_map/ppermute | solution.py:237
  255.7 19.5 %routed_rows.4 = (bf16[256,1536]{1,0:T(8,128)(2,1)}, bf16[256,1536]{1,0:T(8,128)(2,1)}, bf16[256,1536]{1,0:T(8,128)(2,1)}, bf16[256,1536]{1,0:T(8,128)(2,1)}, bf...) custom-call(bf16[256,1536]{1,0:T(8,128)(2,1)} %copy-done.88, ...), custom_call_target="tpu_custom_call" | custom-call | flops 9663676416 | bytes 12582912 | tf_op jit(solution)/shard_map/routed_rows/pallas_call | solution.py:128
  278.0 14.3 %collective-permute-done.38 = bf16[128,1536]{1,0:T(8,128)(2,1)S(1)} collective-permute-done((bf16[128,1536]{1,0:T(8,128)(2,1)S(1)}, bf16[128,1536]{1,0:T(8,128)(2,1)S(1)}, u32[]{:S(2)}, u32[]{:S(2)}) %collective-permute-start.38) | collective-permute-done | bytes 393248 | tf_op jit(solution)/shard_map/ppermute | solution.py:237
  296.3 15.9 %collective-permute-done.80 = bf16[256,1536]{1,0:T(8,128)(2,1)S(1)} collective-permute-done((bf16[256,1536]{1,0:T(8,128)(2,1)S(1)}, bf16[256,1536]{1,0:T(8,128)(2,1)S(1)}, u32[]{:S(2)}, u32[]{:S(2)}) %collective-permute-start.80) | collective-permute-done | bytes 786464 | tf_op jit(solution)/shard_map/ppermute | solution.py:237
  315.5 11.7 %collective-permute-done.91 = bf16[256,1536]{1,0:T(8,128)(2,1)S(1)} collective-permute-done((bf16[256,1536]{1,0:T(8,128)(2,1)S(1)}, bf16[256,1536]{1,0:T(8,128)(2,1)S(1)}, u32[]{:S(2)}, u32[]{:S(2)}) %collective-permute-start.91) | collective-permute-done | bytes 786464 | tf_op jit(solution)/shard_map/ppermute | solution.py:234
  334.8 19.9 %routed_rows.5 = (bf16[256,1536]{1,0:T(8,128)(2,1)}, bf16[256,1536]{1,0:T(8,128)(2,1)}, bf16[256,1536]{1,0:T(8,128)(2,1)}, bf16[256,1536]{1,0:T(8,128)(2,1)}, bf...) custom-call(bf16[256,1536]{1,0:T(8,128)(2,1)} %copy-done.82, ...), custom_call_target="tpu_custom_call" | custom-call | flops 9663676416 | bytes 12582912 | tf_op jit(solution)/shard_map/routed_rows/pallas_call | solution.py:128
  358.6 6.0 collective-permute-done.39.refs_3_.refs_15_
  368.5 19.6 %routed_rows.6 = (bf16[256,1536]{1,0:T(8,128)(2,1)}, bf16[256,1536]{1,0:T(8,128)(2,1)}, bf16[256,1536]{1,0:T(8,128)(2,1)}, bf16[256,1536]{1,0:T(8,128)(2,1)}, bf...) custom-call(bf16[256,1536]{1,0:T(8,128)(2,1)} %copy-done.93, ...), custom_call_target="tpu_custom_call" | custom-call | flops 9663676416 | bytes 12582912 | tf_op jit(solution)/shard_map/routed_rows/pallas_call | solution.py:128
  390.2 4.9 all-to-all-start.1
  395.1 29.5 %expert_grads.1 = (f32[1536,1024]{1,0:T(8,128)}, f32[512,1536]{1,0:T(8,128)}) custom-call(bf16[256,1536]{1,0:T(8,128)(2,1)} %copy-done.46, bf16[256,1536]{1,0:T(8,128)(2,1)} %copy-done.122, bf16[256,1536]{1,0:T(8,128)(2,1)} %copy-done.45, bf16[256,1536]{1,0:T(8,128)(2,1)} %copy-done.123, bf16[256,1536]{1,0:T(8,128)(2,1)} %copy-done.88, ...), custom_call_target="tpu_custom_call" | custom-call | flops 38654705664 | bytes 25165824 | tf_op jit(solution)/shard_map/expert_grads/pallas_call | solution.py:199
  443.6 10.4 %collective-permute-done.31 = bf16[256,1536]{1,0:T(8,128)(2,1)} collective-permute-done((bf16[256,1536]{1,0:T(8,128)(2,1)}, bf16[256,1536]{1,0:T(8,128)(2,1)}, u32[]{:S(2)}, u32[]{:S(2)}) %collective-permute-start.31) | collective-permute-done | bytes 786464 | tf_op jit(solution)/shard_map/ppermute | solution.py:237
  460.5 3.5 collective-permute-done.74
  469.8 15.8 %collective-permute-done.17 = bf16[128,1536]{1,0:T(8,128)(2,1)S(1)} collective-permute-done((bf16[128,1536]{1,0:T(8,128)(2,1)S(1)}, bf16[128,1536]{1,0:T(8,128)(2,1)S(1)}, u32[]{:S(2)}, u32[]{:S(2)}) %collective-permute-start.17) | collective-permute-done | bytes 393248 | tf_op jit(solution)/shard_map/ppermute | solution.py:234
  487.1 9.4 %collective-permute-done.60 = bf16[128,1536]{1,0:T(8,128)(2,1)S(1)} collective-permute-done((bf16[128,1536]{1,0:T(8,128)(2,1)S(1)}, bf16[128,1536]{1,0:T(8,128)(2,1)S(1)}, u32[]{:S(2)}, u32[]{:S(2)}) %collective-permute-start.60) | collective-permute-done | bytes 393248 | tf_op jit(solution)/shard_map/ppermute | solution.py:237
  496.9 11.7 %collective-permute-done.72 = bf16[128,1536]{1,0:T(8,128)(2,1)S(1)} collective-permute-done((bf16[128,1536]{1,0:T(8,128)(2,1)S(1)}, bf16[128,1536]{1,0:T(8,128)(2,1)S(1)}, u32[]{:S(2)}, u32[]{:S(2)}) %collective-permute-start.72) | collective-permute-done | bytes 393248 | tf_op jit(solution)/shard_map/ppermute | solution.py:234
  508.9 7.5 collective-permute-done.83
  518.2 10.1 %collective-permute-done.77 = bf16[256,1536]{1,0:T(8,128)(2,1)S(1)} collective-permute-done((bf16[256,1536]{1,0:T(8,128)(2,1)S(1)}, bf16[256,1536]{1,0:T(8,128)(2,1)S(1)}, u32[]{:S(2)}, u32[]{:S(2)}) %collective-permute-start.77) | collective-permute-done | bytes 786464 | tf_op jit(solution)/shard_map/ppermute | solution.py:237
  528.9 4.1 collective-permute-done.88
  539.0 4.6 collective-permute-done.18
  545.7 7.7 collective-permute-done.61
  555.3 8.6 collective-permute-done.73
  564.1 3.6 collective-permute-start.47
  567.7 7.6 collective-permute-done.84
  575.5 4.5 collective-permute-start.66
  580.0 7.8 collective-permute-done.33
  589.9 11.5 %collective-permute-done.64 = bf16[128,1536]{1,0:T(8,128)(2,1)S(1)} collective-permute-done((bf16[128,1536]{1,0:T(8,128)(2,1)S(1)}, bf16[128,1536]{1,0:T(8,128)(2,1)S(1)}, u32[]{:S(2)}, u32[]{:S(2)}) %collective-permute-start.64) | collective-permute-done | bytes 393248 | tf_op jit(solution)/shard_map/ppermute | solution.py:240
  601.6 4.5 collective-permute-start.89
  606.1 6.7 collective-permute-done.76
  614.1 8.3 collective-permute-done.87
  622.4 5.0 collective-permute-start.92
  629.1 10.9 %collective-permute-done.79 = bf16[128,1536]{1,0:T(8,128)(2,1)S(1)} collective-permute-done((bf16[128,1536]{1,0:T(8,128)(2,1)S(1)}, bf16[128,1536]{1,0:T(8,128)(2,1)S(1)}, u32[]{:S(2)}, u32[]{:S(2)}) %collective-permute-start.79) | collective-permute-done | bytes 393248 | tf_op jit(solution)/shard_map/ppermute | solution.py:240
  640.3 13.6 %collective-permute-done.90 = bf16[128,1536]{1,0:T(8,128)(2,1)S(1)} collective-permute-done((bf16[128,1536]{1,0:T(8,128)(2,1)S(1)}, bf16[128,1536]{1,0:T(8,128)(2,1)S(1)}, u32[]{:S(2)}, u32[]{:S(2)}) %collective-permute-start.90) | collective-permute-done | bytes 393248 | tf_op jit(solution)/shard_map/ppermute | solution.py:240
  659.4 4.1 collective-permute-done.67
  669.4 7.0 fusion.29
  676.4 6.4 fusion.114
  682.8 18.8 %fusion.28 = f32[512,4,64]{0,2,1:T(8,128)} fusion(f32[4,512,512,3]{2,1,3,0:T(8,128)} %fusion.114, f32[4,512,512,3]{2,1,3,0:T(8,128)} %copy-done.7, f32[4,3,512]{2,1,0:T(4,128)S(1)} %copy-done.102, pred[512,512]{0,1:T(8,128)(4,1)S(1)} %fusion.32, bf16[512,4,3,32]{0,3,2,1:T(8,128)(2,1)S(1)} %bitcast.443, bf16[512,4,3,32]{0,3,2,1:T(8,128)(2,1)S(1)} %bitcast.441), kind=kOutput, calls=%fused_computation.93 | convolution fusion | flops 438835712 | bytes 26763264 | tf_op jit(solution)/shard_map/hgqs,qhgd->shd/dot_general | solution.py:522
  701.6 20.8 %fusion.12 = f32[4,64,3,512]{3,1,2,0:T(8,128)} fusion(f32[4,512,512,3]{2,1,3,0:T(8,128)} %fusion.114, f32[4,512,512,3]{2,1,3,0:T(8,128)} %copy-done.7, f32[4,3,512]{2,1,0:T(4,128)S(1)} %copy-done.102, pred[512,512]{0,1:T(8,128)(4,1)S(1)} %fusion.32, bf16[512,4,32]{0,2,1:T(8,128)(2,1)S(1)} %copy-done.98, bf16[512,4,32]{0,2,1:T(8,128)(2,1)S(1)} %copy-done.96), kind=kOutput, calls=%fused_computation.32 | convolution fusion | flops 437787136 | bytes 27287552 | tf_op jit(solution)/shard_map/hgqs,shd->qhgd/dot_general | solution.py:521
  748.1 20.1 %collective-permute-done.118 = bf16[4,48,768]{2,1,0:T(8,128)(2,1)S(1)} collective-permute-done((bf16[4,48,768]{2,1,0:T(8,128)(2,1)S(1)}, bf16[4,48,768]{2,1,0:T(8,128)(2,1)S(1)}, u32[]{:S(2)}, u32[]{:S(2)}) %collective-permute-start.118) | collective-permute-done | bytes 294944 | tf_op jit(solution)/shard_map/ppermute | solution.py:234
  771.1 4.4 collective-permute-done.119
  778.3 4.6 collective-permute-done.98
  785.3 4.3 collective-permute-done.102
  795.8 6.5 collective-permute-done.122
  807.2 7.4 collective-permute-done.100
  815.6 7.6 collective-permute-done.124
  823.3 4.2 collective-permute-done.107
  827.9 8.7 collective-permute-done.108
  838.3 6.2 collective-permute-done.109
  848.5 4.0 collective-permute-done.110
  859.1 8.2 collective-permute-done.111
  869.7 9.8 %collective-permute-done.113 = bf16[4,96,640]{2,1,0:T(8,128)(2,1)S(1)} collective-permute-done((bf16[4,96,640]{2,1,0:T(8,128)(2,1)S(1)}, bf16[4,96,640]{2,1,0:T(8,128)(2,1)S(1)}, u32[]{:S(2)}, u32[]{:S(2)}) %collective-permute-start.113) | collective-permute-done | bytes 491552 | tf_op jit(solution)/shard_map/ppermute | solution.py:234
  884.1 12.4 %collective-permute-done.112 = bf16[4,2,96,640]{3,2,0,1:T(8,128)(2,1)S(1)} collective-permute-done((bf16[4,2,96,640]{3,2,0,1:T(8,128)(2,1)S(1)}, bf16[4,2,96,640]{3,2,0,1:T(8,128)(2,1)S(1)}, u32[]{:S(2)}, u32[]{:S(2)}) %collective-permute-start.112) | collective-permute-done | bytes 983072 | tf_op jit(solution)/shard_map/ppermute | solution.py:234
  (737 shorter events, 266.9 us)
Async XLA Ops:
  2.0 55.9 %collective-permute-start.55 = (bf16[128,1536]{1,0:T(8,128)(2,1)S(1)}, bf16[128,1536]{1,0:T(8,128)(2,1)}, u32[]{:S(2)}, u32[]{:S(2)}) collective-permute-start(bf16[128,1536]{1,0:T(8,128)(2,1)S(1)} %get-tuple-element.129), channel_id=1, source_target_pairs={{0,4},{2,6},{4,0},{6,2},{8,12},{10,14},{12,8},{14,10},{16,20},{18,... | collective-permute-start | bytes 1179656 | tf_op jit(solution)/shard_map/ppermute | solution.py:237
  5.1 51.0 %collective-permute-start.10 = (bf16[128,1536]{1,0:T(8,128)(2,1)S(1)}, bf16[128,1536]{1,0:T(8,128)(2,1)}, u32[]{:S(2)}, u32[]{:S(2)}) collective-permute-start(bf16[128,1536]{1,0:T(8,128)(2,1)S(1)} %get-tuple-element.129), channel_id=1, source_target_pairs={{0,8},{2,10},{4,12},{6,14},{8,16},{10,18},{12,20},{14,22},{16,24},... | collective-permute-start | bytes 1179656 | tf_op jit(solution)/shard_map/ppermute | solution.py:240
  6.6 54.2 %collective-permute-start.53 = (bf16[128,1536]{1,0:T(8,128)(2,1)S(1)}, bf16[128,1536]{1,0:T(8,128)(2,1)}, u32[]{:S(2)}, u32[]{:S(2)}) collective-permute-start(bf16[128,1536]{1,0:T(8,128)(2,1)S(1)} %get-tuple-element.130), channel_id=1, source_target_pairs={{0,2},{2,0},{4,6},{6,4},{8,10},{10,8},{12,14},{14,12},{16,18},{18,... | collective-permute-start | bytes 1179656 | tf_op jit(solution)/shard_map/ppermute | solution.py:234
  8.1 45.7 %collective-permute-start.7 = (bf16[128,1536]{1,0:T(8,128)(2,1)S(1)}, bf16[128,1536]{1,0:T(8,128)(2,1)}, u32[]{:S(2)}, u32[]{:S(2)}) collective-permute-start(bf16[128,1536]{1,0:T(8,128)(2,1)S(1)} %get-tuple-element.130), channel_id=1, source_target_pairs={{0,8},{2,10},{4,12},{6,14},{8,16},{10,18},{12,20},{14,22},{16,24},... | collective-permute-start | bytes 1179656 | tf_op jit(solution)/shard_map/ppermute | solution.py:240
  10.4 32.7 %all-to-all-start = ((s32[16,1,256]{2,1,0:T(1,128)}), s32[16,1,256]{2,1,0:T(1,128)S(1)}, u32[]{:S(2)}, u32[]{:S(2)}) async-start(s32[16,1,256]{2,1,0:T(1,128)} %broadcast_in_dim.75), calls=%async_computation | async-start | bytes 32768 | tf_op jit(solution)/shard_map/all_to_all | solution.py:456
  14.1 127.2 %collective-permute-start.13 = (bf16[1536,256]{1,0:T(8,128)(2,1)}, bf16[1536,256]{1,0:T(8,128)(2,1)}, u32[]{:S(2)}, u32[]{:S(2)}) collective-permute-start(bf16[1536,256]{1,0:T(8,128)(2,1)} %bitcast.464), channel_id=1, source_target_pairs={{0,1},{1,0},{2,3},{3,2},{4,5},{5,4},{6,7},{7,6},{8,9},{9,8},{10,11... | collective-permute-start | bytes 2359304 | tf_op jit(solution)/shard_map/ppermute | solution.py:243
  56.1 104.4 %collective-permute-start.14 = (bf16[1536,256]{1,0:T(8,128)(2,1)S(1)}, bf16[1536,256]{1,0:T(8,128)(2,1)S(1)}, u32[]{:S(2)}, u32[]{:S(2)}) collective-permute-start(bf16[1536,256]{1,0:T(8,128)(2,1)S(1)} %bitcast.473), channel_id=1, source_target_pairs={{0,1},{1,0},{2,3},{3,2},{4,5},{5,4},{6,7},{7,6},{8,9},{9,8},{10,11... | collective-permute-start | bytes 2359304 | tf_op jit(solution)/shard_map/ppermute | solution.py:243
  57.9 24.6 %collective-permute-start.28 = (bf16[128,1536]{1,0:T(8,128)(2,1)}, bf16[128,1536]{1,0:T(8,128)(2,1)S(1)}, u32[]{:S(2)}, u32[]{:S(2)}) collective-permute-start(bf16[128,1536]{1,0:T(8,128)(2,1)} %collective-permute-done.10), channel_id=1, source_target_pairs={{0,8},{2,10},{4,12},{6,14},{8,16},{10,18},{12,20},{14,22},{16,24},... | collective-permute-start | bytes 1179656 | tf_op jit(solution)/shard_map/ppermute | solution.py:240
  60.9 31.3 %collective-permute-start.11 = (bf16[128,1536]{1,0:T(8,128)(2,1)}, bf16[128,1536]{1,0:T(8,128)(2,1)S(1)}, u32[]{:S(2)}, u32[]{:S(2)}) collective-permute-start(bf16[128,1536]{1,0:T(8,128)(2,1)} %collective-permute-done.10), channel_id=1, source_target_pairs={{0,4},{2,6},{4,0},{6,2},{8,12},{10,14},{12,8},{14,10},{16,20},{18,... | collective-permute-start | bytes 1179656 | tf_op jit(solution)/shard_map/ppermute | solution.py:237
  91.1 38.5 %collective-permute-start.4 = (bf16[128,1536]{1,0:T(8,128)(2,1)S(1)}, bf16[128,1536]{1,0:T(8,128)(2,1)S(1)}, u32[]{:S(2)}, u32[]{:S(2)}) collective-permute-start(bf16[128,1536]{1,0:T(8,128)(2,1)S(1)} %get-tuple-element.143), channel_id=1, source_target_pairs={{0,8},{2,10},{4,12},{6,14},{8,16},{10,18},{12,20},{14,22},{16,24},... | collective-permute-start | bytes 1179656 | tf_op jit(solution)/shard_map/ppermute | solution.py:240
  92.2 21.1 %collective-permute-start.40 = (bf16[128,1536]{1,0:T(8,128)(2,1)S(1)}, bf16[128,1536]{1,0:T(8,128)(2,1)S(1)}, u32[]{:S(2)}, u32[]{:S(2)}) collective-permute-start(bf16[128,1536]{1,0:T(8,128)(2,1)S(1)} %collective-permute-done.25), channel_id=1, source_target_pairs={{0,8},{2,10},{4,12},{6,14},{8,16},{10,18},{12,20},{14,22},{16,24},... | collective-permute-start | bytes 1179656 | tf_op jit(solution)/shard_map/ppermute | solution.py:240
  94.9 26.9 %collective-permute-start.43 = (bf16[128,1536]{1,0:T(8,128)(2,1)S(1)}, bf16[128,1536]{1,0:T(8,128)(2,1)S(1)}, u32[]{:S(2)}, u32[]{:S(2)}) collective-permute-start(bf16[128,1536]{1,0:T(8,128)(2,1)S(1)} %collective-permute-done.28), channel_id=1, source_target_pairs={{0,8},{2,10},{4,12},{6,14},{8,16},{10,18},{12,20},{14,22},{16,24},... | collective-permute-start | bytes 1179656 | tf_op jit(solution)/shard_map/ppermute | solution.py:240
  139.6 21.0 %collective-permute-start.44 = (bf16[128,1536]{1,0:T(8,128)(2,1)S(1)}, bf16[128,1536]{1,0:T(8,128)(2,1)S(1)}, u32[]{:S(2)}, u32[]{:S(2)}) collective-permute-start(bf16[128,1536]{1,0:T(8,128)(2,1)S(1)} %collective-permute-done.43), channel_id=1, source_target_pairs={{0,4},{2,6},{4,0},{6,2},{8,12},{10,14},{12,8},{14,10},{16,20},{18,... | collective-permute-start | bytes 1179656 | tf_op jit(solution)/shard_map/ppermute | solution.py:237
  141.3 20.8 %collective-permute-start.41 = (bf16[128,1536]{1,0:T(8,128)(2,1)S(1)}, bf16[128,1536]{1,0:T(8,128)(2,1)S(1)}, u32[]{:S(2)}, u32[]{:S(2)}) collective-permute-start(bf16[128,1536]{1,0:T(8,128)(2,1)S(1)} %collective-permute-done.40), channel_id=1, source_target_pairs={{0,2},{2,0},{4,6},{6,4},{8,10},{10,8},{12,14},{14,12},{16,18},{18,... | collective-permute-start | bytes 1179656 | tf_op jit(solution)/shard_map/ppermute | solution.py:234
  160.6 20.4 %collective-permute-start.54 = (bf16[256,1536]{1,0:T(8,128)(2,1)S(1)}, bf16[256,1536]{1,0:T(8,128)(2,1)S(1)}, u32[]{:S(2)}, u32[]{:S(2)}) collective-permute-start(bf16[256,1536]{1,0:T(8,128)(2,1)S(1)} %pad_maximum_fusion.5.refs_4_.refs_16_), channel_id=1, source_target_pairs={{0,4},{2,6},{4,0},{6,2},{8,12},{10,14},{12,8},{14,10},{16,20},{18,... | collective-permute-start | bytes 2359304 | tf_op jit(solution)/shard_map/ppermute | solution.py:237
  162.1 20.9 %collective-permute-start.56 = (bf16[256,1536]{1,0:T(8,128)(2,1)S(1)}, bf16[256,1536]{1,0:T(8,128)(2,1)S(1)}, u32[]{:S(2)}, u32[]{:S(2)}) collective-permute-start(bf16[256,1536]{1,0:T(8,128)(2,1)S(1)} %pad_maximum_fusion.6.refs_6_.refs_18_), channel_id=1, source_target_pairs={{0,2},{2,0},{4,6},{6,4},{8,10},{10,8},{12,14},{14,12},{16,18},{18,... | collective-permute-start | bytes 2359304 | tf_op jit(solution)/shard_map/ppermute | solution.py:234
  162.7 35.2 %collective-permute-start.50 = (bf16[256,1536]{1,0:T(8,128)(2,1)S(1)}, bf16[256,1536]{1,0:T(8,128)(2,1)S(1)}, u32[]{:S(2)}, u32[]{:S(2)}) collective-permute-start(bf16[256,1536]{1,0:T(8,128)(2,1)S(1)} %pad_maximum_fusion.3.refs_0_), channel_id=1, source_target_pairs={{0,4},{2,6},{4,0},{6,2},{8,12},{10,14},{12,8},{14,10},{16,20},{18,... | collective-permute-start | bytes 2359304 | tf_op jit(solution)/shard_map/ppermute | solution.py:237
  166.2 33.7 %collective-permute-start.52 = (bf16[256,1536]{1,0:T(8,128)(2,1)S(1)}, bf16[256,1536]{1,0:T(8,128)(2,1)S(1)}, u32[]{:S(2)}, u32[]{:S(2)}) collective-permute-start(bf16[256,1536]{1,0:T(8,128)(2,1)S(1)} %pad_maximum_fusion.4.refs_2_), channel_id=1, source_target_pairs={{0,2},{2,0},{4,6},{6,4},{8,10},{10,8},{12,14},{14,12},{16,18},{18,... | collective-permute-start | bytes 2359304 | tf_op jit(solution)/shard_map/ppermute | solution.py:234
  168.9 82.1 %collective-permute-start.12 = (bf16[256,1536]{1,0:T(8,128)(2,1)}, bf16[256,1536]{1,0:T(8,128)(2,1)}, u32[]{:S(2)}, u32[]{:S(2)}) collective-permute-start(bf16[256,1536]{1,0:T(8,128)(2,1)} %constant_dynamic-update-slice_fusion.6.refs_6_.refs_22_), channel_id=1, source_target_pairs={{0,2},{2,0},{4,6},{6,4},{8,10},{10,8},{12,14},{14,12},{16,18},{18,... | collective-permute-start | bytes 2359304 | tf_op jit(solution)/shard_map/ppermute | solution.py:234
  181.0 70.5 %collective-permute-start.9 = (bf16[256,1536]{1,0:T(8,128)(2,1)}, bf16[256,1536]{1,0:T(8,128)(2,1)}, u32[]{:S(2)}, u32[]{:S(2)}) collective-permute-start(bf16[256,1536]{1,0:T(8,128)(2,1)} %constant_dynamic-update-slice_fusion.4.refs_4_.refs_20_), channel_id=1, source_target_pairs={{0,4},{2,6},{4,0},{6,2},{8,12},{10,14},{12,8},{14,10},{16,20},{18,... | collective-permute-start | bytes 2359304 | tf_op jit(solution)/shard_map/ppermute | solution.py:237
  183.0 41.0 %collective-permute-start.37 = (bf16[128,1536]{1,0:T(8,128)(2,1)S(1)}, bf16[128,1536]{1,0:T(8,128)(2,1)S(1)}, u32[]{:S(2)}, u32[]{:S(2)}) collective-permute-start(bf16[128,1536]{1,0:T(8,128)(2,1)S(1)} %collective-permute-done.22), channel_id=1, source_target_pairs={{0,8},{2,10},{4,12},{6,14},{8,16},{10,18},{12,20},{14,22},{16,24},... | collective-permute-start | bytes 1179656 | tf_op jit(solution)/shard_map/ppermute | solution.py:240
  197.8 24.5 %collective-permute-start.34 = (bf16[128,1536]{1,0:T(8,128)(2,1)S(1)}, bf16[128,1536]{1,0:T(8,128)(2,1)S(1)}, u32[]{:S(2)}, u32[]{:S(2)}) collective-permute-start(bf16[128,1536]{1,0:T(8,128)(2,1)S(1)} %collective-permute-done.19), channel_id=1, source_target_pairs={{0,8},{2,10},{4,12},{6,14},{8,16},{10,18},{12,20},{14,22},{16,24},... | collective-permute-start | bytes 1179656 | tf_op jit(solution)/shard_map/ppermute | solution.py:240
  199.9 26.7 %collective-permute-start.20 = (bf16[128,1536]{1,0:T(8,128)(2,1)S(1)}, bf16[128,1536]{1,0:T(8,128)(2,1)S(1)}, u32[]{:S(2)}, u32[]{:S(2)}) collective-permute-start(bf16[128,1536]{1,0:T(8,128)(2,1)S(1)} %collective-permute-done.19), channel_id=1, source_target_pairs={{0,2},{2,0},{4,6},{6,4},{8,10},{10,8},{12,14},{14,12},{16,18},{18,... | collective-permute-start | bytes 1179656 | tf_op jit(solution)/shard_map/ppermute | solution.py:234
  222.4 30.7 %collective-permute-start.6 = (bf16[256,1536]{1,0:T(8,128)(2,1)S(1)}, bf16[256,1536]{1,0:T(8,128)(2,1)S(1)}, u32[]{:S(2)}, u32[]{:S(2)}) collective-permute-start(bf16[256,1536]{1,0:T(8,128)(2,1)S(1)} %copy-done.91), channel_id=1, source_target_pairs={{0,2},{2,0},{4,6},{6,4},{8,10},{10,8},{12,14},{14,12},{16,18},{18,... | collective-permute-start | bytes 2359304 | tf_op jit(solution)/shard_map/ppermute | solution.py:234
  224.0 29.6 %collective-permute-start.3 = (bf16[256,1536]{1,0:T(8,128)(2,1)S(1)}, bf16[256,1536]{1,0:T(8,128)(2,1)S(1)}, u32[]{:S(2)}, u32[]{:S(2)}) collective-permute-start(bf16[256,1536]{1,0:T(8,128)(2,1)S(1)} %copy-done.89), channel_id=1, source_target_pairs={{0,4},{2,6},{4,0},{6,2},{8,12},{10,14},{12,8},{14,10},{16,20},{18,... | collective-permute-start | bytes 2359304 | tf_op jit(solution)/shard_map/ppermute | solution.py:237
  226.6 22.4 %collective-permute-start.23 = (bf16[128,1536]{1,0:T(8,128)(2,1)S(1)}, bf16[128,1536]{1,0:T(8,128)(2,1)S(1)}, u32[]{:S(2)}, u32[]{:S(2)}) collective-permute-start(bf16[128,1536]{1,0:T(8,128)(2,1)S(1)} %collective-permute-done.22), channel_id=1, source_target_pairs={{0,4},{2,6},{4,0},{6,2},{8,12},{10,14},{12,8},{14,10},{16,20},{18,... | collective-permute-start | bytes 1179656 | tf_op jit(solution)/shard_map/ppermute | solution.py:237
  249.0 81.3 %collective-permute-start.30 = (bf16[256,1536]{1,0:T(8,128)(2,1)}, bf16[256,1536]{1,0:T(8,128)(2,1)}, u32[]{:S(2)}, u32[]{:S(2)}) collective-permute-start(bf16[256,1536]{1,0:T(8,128)(2,1)} %constant_dynamic-update-slice_fusion.15.refs_6_.refs_26_), channel_id=1, source_target_pairs={{0,2},{2,0},{4,6},{6,4},{8,10},{10,8},{12,14},{14,12},{16,18},{18,... | collective-permute-start | bytes 2359304 | tf_op jit(solution)/shard_map/ppermute | solution.py:234
  250.9 80.0 %collective-permute-start.27 = (bf16[256,1536]{1,0:T(8,128)(2,1)}, bf16[256,1536]{1,0:T(8,128)(2,1)}, u32[]{:S(2)}, u32[]{:S(2)}) collective-permute-start(bf16[256,1536]{1,0:T(8,128)(2,1)} %constant_dynamic-update-slice_fusion.13.refs_4_.refs_24_), channel_id=1, source_target_pairs={{0,4},{2,6},{4,0},{6,2},{8,12},{10,14},{12,8},{14,10},{16,20},{18,... | collective-permute-start | bytes 2359304 | tf_op jit(solution)/shard_map/ppermute | solution.py:237
  251.5 43.0 %collective-permute-start.57 = (bf16[256,1536]{1,0:T(8,128)(2,1)}, bf16[256,1536]{1,0:T(8,128)(2,1)S(1)}, u32[]{:S(2)}, u32[]{:S(2)}) collective-permute-start(bf16[256,1536]{1,0:T(8,128)(2,1)} %get-tuple-element.65), channel_id=1, source_target_pairs={{0,4},{2,6},{4,0},{6,2},{8,12},{10,14},{12,8},{14,10},{16,20},{18,... | collective-permute-start | bytes 2359304 | tf_op jit(solution)/shard_map/ppermute | solution.py:237
  253.0 39.3 %collective-permute-start.38 = (bf16[128,1536]{1,0:T(8,128)(2,1)S(1)}, bf16[128,1536]{1,0:T(8,128)(2,1)S(1)}, u32[]{:S(2)}, u32[]{:S(2)}) collective-permute-start(bf16[128,1536]{1,0:T(8,128)(2,1)S(1)} %collective-permute-done.37), channel_id=1, source_target_pairs={{0,4},{2,6},{4,0},{6,2},{8,12},{10,14},{12,8},{14,10},{16,20},{18,... | collective-permute-start | bytes 1179656 | tf_op jit(solution)/shard_map/ppermute | solution.py:237
  254.8 20.5 %collective-permute-start.35 = (bf16[128,1536]{1,0:T(8,128)(2,1)S(1)}, bf16[128,1536]{1,0:T(8,128)(2,1)S(1)}, u32[]{:S(2)}, u32[]{:S(2)}) collective-permute-start(bf16[128,1536]{1,0:T(8,128)(2,1)S(1)} %collective-permute-done.34), channel_id=1, source_target_pairs={{0,2},{2,0},{4,6},{6,4},{8,10},{10,8},{12,14},{14,12},{16,18},{18,... | collective-permute-start | bytes 1179656 | tf_op jit(solution)/shard_map/ppermute | solution.py:234
  292.4 39.3 %collective-permute-start.24 = (bf16[256,1536]{1,0:T(8,128)(2,1)}, bf16[256,1536]{1,0:T(8,128)(2,1)S(1)}, u32[]{:S(2)}, u32[]{:S(2)}) collective-permute-start(bf16[256,1536]{1,0:T(8,128)(2,1)} %constant_dynamic-update-slice_fusion.11.refs_2_.refs_10_), channel_id=1, source_target_pairs={{0,2},{2,0},{4,6},{6,4},{8,10},{10,8},{12,14},{14,12},{16,18},{18,... | collective-permute-start | bytes 2359304 | tf_op jit(solution)/shard_map/ppermute | solution.py:234
  295.4 31.8 %collective-permute-start.91 = (bf16[256,1536]{1,0:T(8,128)(2,1)S(1)}, bf16[256,1536]{1,0:T(8,128)(2,1)S(1)}, u32[]{:S(2)}, u32[]{:S(2)}) collective-permute-start(bf16[256,1536]{1,0:T(8,128)(2,1)S(1)} %copy-done.134), channel_id=1, source_target_pairs={{0,2},{2,0},{4,6},{6,4},{8,10},{10,8},{12,14},{14,12},{16,18},{18,... | collective-permute-start | bytes 2359304 | tf_op jit(solution)/shard_map/ppermute | solution.py:234
  312.3 20.9 %collective-permute-start.21 = (bf16[256,1536]{1,0:T(8,128)(2,1)S(1)}, bf16[256,1536]{1,0:T(8,128)(2,1)S(1)}, u32[]{:S(2)}, u32[]{:S(2)}) collective-permute-start(bf16[256,1536]{1,0:T(8,128)(2,1)S(1)} %copy-done.83), channel_id=1, source_target_pairs={{0,4},{2,6},{4,0},{6,2},{8,12},{10,14},{12,8},{14,10},{16,20},{18,... | collective-permute-start | bytes 2359304 | tf_op jit(solution)/shard_map/ppermute | solution.py:237
  327.1 28.8 %collective-permute-start.45 = (bf16[256,1536]{1,0:T(8,128)(2,1)S(1)}, bf16[256,1536]{1,0:T(8,128)(2,1)}, u32[]{:S(2)}, u32[]{:S(2)}) collective-permute-start(bf16[256,1536]{1,0:T(8,128)(2,1)S(1)} %copy-done.87), channel_id=1, source_target_pairs={{0,2},{2,0},{4,6},{6,4},{8,10},{10,8},{12,14},{14,12},{16,18},{18,... | collective-permute-start | bytes 2359304 | tf_op jit(solution)/shard_map/ppermute | solution.py:234
  330.4 27.0 %collective-permute-start.42 = (bf16[256,1536]{1,0:T(8,128)(2,1)S(1)}, bf16[256,1536]{1,0:T(8,128)(2,1)S(1)}, u32[]{:S(2)}, u32[]{:S(2)}) collective-permute-start(bf16[256,1536]{1,0:T(8,128)(2,1)S(1)} %copy-done.85), channel_id=1, source_target_pairs={{0,4},{2,6},{4,0},{6,2},{8,12},{10,14},{12,8},{14,10},{16,20},{18,... | collective-permute-start | bytes 2359304 | tf_op jit(solution)/shard_map/ppermute | solution.py:237
  331.0 33.6 %collective-permute-start.39 = (bf16[256,1536]{1,0:T(8,128)(2,1)S(1)}, bf16[256,1536]{1,0:T(8,128)(2,1)}, u32[]{:S(2)}, u32[]{:S(2)}) collective-permute-start(bf16[256,1536]{1,0:T(8,128)(2,1)S(1)} %copy-done.94), channel_id=1, source_target_pairs={{0,2},{2,0},{4,6},{6,4},{8,10},{10,8},{12,14},{14,12},{16,18},{18,... | collective-permute-start | bytes 2359304 | tf_op jit(solution)/shard_map/ppermute | solution.py:234
  331.6 36.2 %collective-permute-start.36 = (bf16[256,1536]{1,0:T(8,128)(2,1)S(1)}, bf16[256,1536]{1,0:T(8,128)(2,1)}, u32[]{:S(2)}, u32[]{:S(2)}) collective-permute-start(bf16[256,1536]{1,0:T(8,128)(2,1)S(1)} %constant_dynamic-update-slice_fusion.18.refs_0_.refs_12_), channel_id=1, source_target_pairs={{0,4},{2,6},{4,0},{6,2},{8,12},{10,14},{12,8},{14,10},{16,20},{18,... | collective-permute-start | bytes 2359304 | tf_op jit(solution)/shard_map/ppermute | solution.py:237
  334.0 90.6 %collective-permute-start.16 = (bf16[256,1536]{1,0:T(8,128)(2,1)}, bf16[256,1536]{1,0:T(8,128)(2,1)}, u32[]{:S(2)}, u32[]{:S(2)}) collective-permute-start(bf16[256,1536]{1,0:T(8,128)(2,1)} %get-tuple-element.59), channel_id=1, source_target_pairs={{0,4},{2,6},{4,0},{6,2},{8,12},{10,14},{12,8},{14,10},{16,20},{18,... | collective-permute-start | bytes 2359304 | tf_op jit(solution)/shard_map/ppermute | solution.py:237
  356.0 72.1 %collective-permute-start.59 = (bf16[256,1536]{1,0:T(8,128)(2,1)}, bf16[256,1536]{1,0:T(8,128)(2,1)}, u32[]{:S(2)}, u32[]{:S(2)}) collective-permute-start(bf16[256,1536]{1,0:T(8,128)(2,1)} %get-tuple-element.67), channel_id=1, source_target_pairs={{0,2},{2,0},{4,6},{6,4},{8,10},{10,8},{12,14},{14,12},{16,18},{18,... | collective-permute-start | bytes 2359304 | tf_op jit(solution)/shard_map/ppermute | solution.py:234
  357.4 72.3 %collective-permute-start.71 = (bf16[256,1536]{1,0:T(8,128)(2,1)}, bf16[256,1536]{1,0:T(8,128)(2,1)}, u32[]{:S(2)}, u32[]{:S(2)}) collective-permute-start(bf16[256,1536]{1,0:T(8,128)(2,1)} %get-tuple-element.75), channel_id=1, source_target_pairs={{0,4},{2,6},{4,0},{6,2},{8,12},{10,14},{12,8},{14,10},{16,20},{18,... | collective-permute-start | bytes 2359304 | tf_op jit(solution)/shard_map/ppermute | solution.py:237
  364.6 68.5 %collective-permute-start.82 = (bf16[256,1536]{1,0:T(8,128)(2,1)}, bf16[256,1536]{1,0:T(8,128)(2,1)}, u32[]{:S(2)}, u32[]{:S(2)}) collective-permute-start(bf16[256,1536]{1,0:T(8,128)(2,1)} %get-tuple-element.83), channel_id=1, source_target_pairs={{0,2},{2,0},{4,6},{6,4},{8,10},{10,8},{12,14},{14,12},{16,18},{18,... | collective-permute-start | bytes 2359304 | tf_op jit(solution)/shard_map/ppermute | solution.py:234
  367.8 288.3 %collective-permute-start.58 = (bf16[128,1536]{1,0:T(8,128)(2,1)}, bf16[128,1536]{1,0:T(8,128)(2,1)}, u32[]{:S(2)}, u32[]{:S(2)}) collective-permute-start(bf16[128,1536]{1,0:T(8,128)(2,1)} %slice.477), channel_id=1, source_target_pairs={{0,2},{2,0},{4,6},{6,4},{8,10},{10,8},{12,14},{14,12},{16,18},{18,... | collective-permute-start | bytes 1179656 | tf_op jit(solution)/shard_map/ppermute | solution.py:234
  390.2 52.3 %all-to-all-start.1 = ((f32[16,1,256]{2,1,0:T(1,128)}), f32[16,1,256]{2,1,0:T(1,128)S(1)}, u32[]{:S(2)}, u32[]{:S(2)}) async-start(f32[16,1,256]{2,1,0:T(1,128)} %all_to_all.11), calls=%async_computation.1 | async-start | bytes 32768 | tf_op jit(solution)/shard_map/all_to_all | solution.py:501
  424.6 234.8 %collective-permute-start.69 = (bf16[128,1536]{1,0:T(8,128)(2,1)}, bf16[128,1536]{1,0:T(8,128)(2,1)}, u32[]{:S(2)}, u32[]{:S(2)}) collective-permute-start(bf16[128,1536]{1,0:T(8,128)(2,1)} %slice.485), channel_id=1, source_target_pairs={{0,4},{2,6},{4,0},{6,2},{8,12},{10,14},{12,8},{14,10},{16,20},{18,... | collective-permute-start | bytes 1179656 | tf_op jit(solution)/shard_map/ppermute | solution.py:237
  428.0 25.9 %collective-permute-start.31 = (bf16[256,1536]{1,0:T(8,128)(2,1)}, bf16[256,1536]{1,0:T(8,128)(2,1)}, u32[]{:S(2)}, u32[]{:S(2)}) collective-permute-start(bf16[256,1536]{1,0:T(8,128)(2,1)} %get-tuple-element.61), channel_id=1, source_target_pairs={{0,4},{2,6},{4,0},{6,2},{8,12},{10,14},{12,8},{14,10},{16,20},{18,... | collective-permute-start | bytes 2359304 | tf_op jit(solution)/shard_map/ppermute | solution.py:237
  429.7 27.7 %collective-permute-start.62 = (bf16[256,1536]{1,0:T(8,128)(2,1)}, bf16[256,1536]{1,0:T(8,128)(2,1)}, u32[]{:S(2)}, u32[]{:S(2)}) collective-permute-start(bf16[256,1536]{1,0:T(8,128)(2,1)} %get-tuple-element.69), channel_id=1, source_target_pairs={{0,2},{2,0},{4,6},{6,4},{8,10},{10,8},{12,14},{14,12},{16,18},{18,... | collective-permute-start | bytes 2359304 | tf_op jit(solution)/shard_map/ppermute | solution.py:234
  433.1 30.9 %collective-permute-start.74 = (bf16[256,1536]{1,0:T(8,128)(2,1)}, bf16[256,1536]{1,0:T(8,128)(2,1)}, u32[]{:S(2)}, u32[]{:S(2)}) collective-permute-start(bf16[256,1536]{1,0:T(8,128)(2,1)} %get-tuple-element.77), channel_id=1, source_target_pairs={{0,4},{2,6},{4,0},{6,2},{8,12},{10,14},{12,8},{14,10},{16,20},{18,... | collective-permute-start | bytes 2359304 | tf_op jit(solution)/shard_map/ppermute | solution.py:237
  457.4 59.2 %collective-permute-start.46 = (bf16[256,1536]{1,0:T(8,128)(2,1)S(1)}, bf16[256,1536]{1,0:T(8,128)(2,1)S(1)}, u32[]{:S(2)}, u32[]{:S(2)}) collective-permute-start(bf16[256,1536]{1,0:T(8,128)(2,1)S(1)} %copy-done.130), channel_id=1, source_target_pairs={{0,4},{2,6},{4,0},{6,2},{8,12},{10,14},{12,8},{14,10},{16,20},{18,... | collective-permute-start | bytes 2359304 | tf_op jit(solution)/shard_map/ppermute | solution.py:237
  464.0 53.2 %collective-permute-start.65 = (bf16[256,1536]{1,0:T(8,128)(2,1)S(1)}, bf16[256,1536]{1,0:T(8,128)(2,1)S(1)}, u32[]{:S(2)}, u32[]{:S(2)}) collective-permute-start(bf16[256,1536]{1,0:T(8,128)(2,1)S(1)} %copy-done.129), channel_id=1, source_target_pairs={{0,2},{2,0},{4,6},{6,4},{8,10},{10,8},{12,14},{14,12},{16,18},{18,... | collective-permute-start | bytes 2359304 | tf_op jit(solution)/shard_map/ppermute | solution.py:234
  517.7 109.8 %collective-permute-start.130 = (f32[256,1536]{1,0:T(8,128)S(1)}, f32[256,1536]{1,0:T(8,128)S(1)}, u32[]{:S(2)}, u32[]{:S(2)}) collective-permute-start(f32[256,1536]{1,0:T(8,128)S(1)} %copy-done.35), channel_id=1, source_target_pairs={{0,1},{1,0},{2,3},{3,2},{4,5},{5,4},{6,7},{7,6},{8,9},{9,8},{10,11... | collective-permute-start | bytes 4718600 | tf_op jit(solution)/shard_map/ppermute | solution.py:243
  629.1 112.5 %collective-permute-start.129 = (f32[1536,512]{1,0:T(8,128)}, f32[1536,512]{1,0:T(8,128)}, u32[]{:S(2)}, u32[]{:S(2)}) collective-permute-start(f32[1536,512]{1,0:T(8,128)} %slice.427), channel_id=1, source_target_pairs={{0,1},{1,0},{2,3},{3,2},{4,5},{5,4},{6,7},{7,6},{8,9},{9,8},{10,11... | collective-permute-start | bytes 9437192 | tf_op jit(solution)/shard_map/ppermute | solution.py:243
  738.2 32.2 %collective-permute-start.103 = (bf16[4,2,96,640]{3,2,1,0:T(8,128)(2,1)S(1)}, bf16[4,2,96,640]{3,2,1,0:T(8,128)(2,1)S(1)}, u32[]{:S(2)}, u32[]{:S(2)}) collective-permute-start(bf16[4,2,96,640]{3,2,1,0:T(8,128)(2,1)S(1)} %dynamic-slice_bitcast_fusion), channel_id=1, source_target_pairs={{0,4},{2,6},{4,0},{6,2},{8,12},{10,14},{12,8},{14,10},{16,20},{18,... | collective-permute-start | bytes 2949128 | tf_op jit(solution)/shard_map/ppermute | solution.py:237
  739.0 36.7 %collective-permute-start.101 = (bf16[4,2,96,640]{3,2,0,1:T(8,128)(2,1)S(1)}, bf16[4,2,96,640]{3,2,0,1:T(8,128)(2,1)S(1)}, u32[]{:S(2)}, u32[]{:S(2)}) collective-permute-start(bf16[4,2,96,640]{3,2,0,1:T(8,128)(2,1)S(1)} %bitcast.427), channel_id=1, source_target_pairs={{0,2},{2,0},{4,6},{6,4},{8,10},{10,8},{12,14},{14,12},{16,18},{18,... | collective-permute-start | bytes 2949128 | tf_op jit(solution)/shard_map/ppermute | solution.py:234
  741.3 27.0 %collective-permute-start.118 = (bf16[4,48,768]{2,1,0:T(8,128)(2,1)S(1)}, bf16[4,48,768]{2,1,0:T(8,128)(2,1)S(1)}, u32[]{:S(2)}, u32[]{:S(2)}) collective-permute-start(bf16[4,48,768]{2,1,0:T(8,128)(2,1)S(1)} %dynamic-slice_bitcast_fusion.4), channel_id=1, source_target_pairs={{0,2},{2,0},{4,6},{6,4},{8,10},{10,8},{12,14},{14,12},{16,18},{18,... | collective-permute-start | bytes 884744 | tf_op jit(solution)/shard_map/ppermute | solution.py:234
  741.5 26.8 %collective-permute-start.116 = (bf16[4,48,768]{2,1,0:T(8,128)(2,1)S(1)}, bf16[4,48,768]{2,1,0:T(8,128)(2,1)S(1)}, u32[]{:S(2)}, u32[]{:S(2)}) collective-permute-start(bf16[4,48,768]{2,1,0:T(8,128)(2,1)S(1)} %dynamic-slice_bitcast_fusion.5), channel_id=1, source_target_pairs={{0,4},{2,6},{4,0},{6,2},{8,12},{10,14},{12,8},{14,10},{16,20},{18,... | collective-permute-start | bytes 884744 | tf_op jit(solution)/shard_map/ppermute | solution.py:237
  748.0 20.5 %collective-permute-start.96 = (f32[18,1536]{1,0:T(8,128)S(1)}, f32[18,1536]{1,0:T(8,128)S(1)}, u32[]{:S(2)}, u32[]{:S(2)}) collective-permute-start(f32[18,1536]{1,0:T(8,128)S(1)} %pad_maximum_fusion.13), channel_id=1, source_target_pairs={{0,1},{1,0},{2,3},{3,2},{4,5},{5,4},{6,7},{7,6},{8,9},{9,8},{10,11... | collective-permute-start | bytes 331784 | tf_op jit(solution)/shard_map/ppermute | solution.py:243
  792.7 21.9 %collective-permute-start.100 = (f32[18,1536]{1,0:T(8,128)S(1)}, f32[18,1536]{1,0:T(8,128)S(1)}, u32[]{:S(2)}, u32[]{:S(2)}) collective-permute-start(f32[18,1536]{1,0:T(8,128)S(1)} %add.471), channel_id=1, source_target_pairs={{0,16},{2,18},{4,20},{6,22},{8,24},{10,26},{12,28},{14,30},{16,0},... | collective-permute-start | bytes 331784 | tf_op jit(solution)/shard_map/ppermute | solution.py:317
  806.7 37.9 %collective-permute-start.95 = (bf16[256,1536]{1,0:T(8,128)(2,1)S(1)}, bf16[256,1536]{1,0:T(8,128)(2,1)S(1)}, u32[]{:S(2)}, u32[]{:S(2)}) collective-permute-start(bf16[256,1536]{1,0:T(8,128)(2,1)S(1)} %get-tuple-element.126), channel_id=1, source_target_pairs={{0,1},{1,0},{2,3},{3,2},{4,5},{5,4},{6,7},{7,6},{8,9},{9,8},{10,11... | collective-permute-start | bytes 2359304 | tf_op jit(solution)/shard_map/ppermute | solution.py:243
  806.7 47.4 %collective-permute-start.70 = (bf16[256,1536]{1,0:T(8,128)(2,1)S(1)}, bf16[256,1536]{1,0:T(8,128)(2,1)S(1)}, u32[]{:S(2)}, u32[]{:S(2)}) collective-permute-start(bf16[256,1536]{1,0:T(8,128)(2,1)S(1)} %get-tuple-element.127), channel_id=1, source_target_pairs={{0,1},{1,0},{2,3},{3,2},{4,5},{5,4},{6,7},{7,6},{8,9},{9,8},{10,11... | collective-permute-start | bytes 2359304 | tf_op jit(solution)/shard_map/ppermute | solution.py:243
  848.2 21.2 %collective-permute-start.126 = (bf16[4,2,48,768]{3,2,0,1:T(8,128)(2,1)S(1)}, bf16[4,2,48,768]{3,2,0,1:T(8,128)(2,1)S(1)}, u32[]{:S(2)}, u32[]{:S(2)}) collective-permute-start(bf16[4,2,48,768]{3,2,0,1:T(8,128)(2,1)S(1)} %maximum_select_fusion.12), channel_id=1, source_target_pairs={{0,2},{2,0},{4,6},{6,4},{8,10},{10,8},{12,14},{14,12},{16,18},{18,... | collective-permute-start | bytes 1769480 | tf_op jit(solution)/shard_map/ppermute | solution.py:234
  856.4 24.3 %collective-permute-start.128 = (bf16[4,2,48,768]{3,2,0,1:T(8,128)(2,1)S(1)}, bf16[4,2,48,768]{3,2,0,1:T(8,128)(2,1)S(1)}, u32[]{:S(2)}, u32[]{:S(2)}) collective-permute-start(bf16[4,2,48,768]{3,2,0,1:T(8,128)(2,1)S(1)} %maximum_select_fusion.14), channel_id=1, source_target_pairs={{0,4},{2,6},{4,0},{6,2},{8,12},{10,14},{12,8},{14,10},{16,20},{18,... | collective-permute-start | bytes 1769480 | tf_op jit(solution)/shard_map/ppermute | solution.py:237
  857.4 22.1 %collective-permute-start.113 = (bf16[4,96,640]{2,1,0:T(8,128)(2,1)S(1)}, bf16[4,96,640]{2,1,0:T(8,128)(2,1)S(1)}, u32[]{:S(2)}, u32[]{:S(2)}) collective-permute-start(bf16[4,96,640]{2,1,0:T(8,128)(2,1)S(1)} %get-tuple-element.137), channel_id=1, source_target_pairs={{0,2},{2,0},{4,6},{6,4},{8,10},{10,8},{12,14},{14,12},{16,18},{18,... | collective-permute-start | bytes 1474568 | tf_op jit(solution)/shard_map/ppermute | solution.py:234
  867.6 29.0 %collective-permute-start.112 = (bf16[4,2,96,640]{3,2,0,1:T(8,128)(2,1)S(1)}, bf16[4,2,96,640]{3,2,0,1:T(8,128)(2,1)S(1)}, u32[]{:S(2)}, u32[]{:S(2)}) collective-permute-start(bf16[4,2,96,640]{3,2,0,1:T(8,128)(2,1)S(1)} %maximum_select_fusion.8), channel_id=1, source_target_pairs={{0,2},{2,0},{4,6},{6,4},{8,10},{10,8},{12,14},{14,12},{16,18},{18,... | collective-permute-start | bytes 2949128 | tf_op jit(solution)/shard_map/ppermute | solution.py:234
  (211 other events, 3176.7 us)

commit v2 on v1

v2 whole, which is shorter than its diff:
```python
import functools
import math

import jax
import jax.numpy as jnp
from jax import lax
from jax.experimental import pallas as pl
from jax.experimental.pallas import tpu as pltpu
from jax.sharding import PartitionSpec as P

HEAD_DIM = 64
HEADS = 24
KV_HEADS = 8
EPSILON = 1e-06
NEGATIVE = -1e30
BF16 = jnp.bfloat16
F32 = jnp.float32
NN = (((1,), (0,)), ((), ()))
NT = (((1,), (1,)), ((), ()))
TN = (((0,), (0,)), ((), ()))
VMEM_LIMIT = 56 * 1024 * 1024
SMALL = pl.CostEstimate(flops=0, bytes_accessed=1024 * 1024, transcendentals=0)


def dot(left, right, dims=NN):
    return lax.dot_general(left, right, dims, preferred_element_type=F32)


LABELS = [(0, 0, 0), (0, 0, 1), (0, 1, 0), (0, 1, 1), (1, 0, 0), (1, 0, 1), (1, 1, 0), (1, 1, 1)]
SPREAD = [
    [(0, 0, 0), (0, 0, 1)],
    [(0, 1, 0), (0, 1, 1)],
    [(1, 0, 0), (1, 0, 1)],
    [(1, 1, 0)],
    [(1, 1, 1)],
]
WIDE = [(0, 0, 0), (0, 1, 0), (1, 0, 0), (1, 1, 0)]
SPLIT = [WIDE, [(0, 0, 1)], [(0, 1, 1)], [(1, 0, 1)], [(1, 1, 1)]]


def near_far(order, half):
    if order == "xy":
        return [[(0, 0, half), (0, 1, half)], [(1, 0, half), (1, 1, half)]]
    return [[(0, 0, half), (1, 0, half)], [(0, 1, half), (1, 1, half)]]


def places_of(tables):
    return {label: (a, i) for a, table in enumerate(tables) for i, label in enumerate(table)}


def piece_of(refs, where, label, rows):
    array, at = where[label]
    return refs[array].at[pl.ds(at * rows, rows)]


def routed_kernel(tables, fresh, *refs):
    counts = [len(table) for table in tables]
    groups, at = [], 2
    for size in (counts[0], counts[1], 1, 1, 1, 1, 1, 0 if fresh else 1, counts[2], 1, 1, 1, 1, 1, 6):
        groups.append(refs[at : at + size])
        at += size
    numbers, bits = refs[0], refs[1]
    hn, dy, (seed,), (router,), (wg,), (wu,), (wd,), _, dx, (wide,), (mix,), *rest = groups
    (dgate,), (pre,), (act,), scratch = rest
    hbuf, dbuf, xbuf, mbuf, in_sem, out_sem = scratch
    where = [places_of(table) for table in tables]
    rows = hbuf.shape[1] // 2
    step = pl.program_id(0)
    slot = lax.rem(step, 2)

    def fetch(s, to):
        return [
            pltpu.make_async_copy(
                piece_of(source, where[n], LABELS[2 * s + i], rows),
                buffer.at[to, pl.ds(i * rows, rows)],
                in_sem.at[to, 2 * n + i],
            )
            for n, (source, buffer) in enumerate(((hn, hbuf), (dy, dbuf)))
            for i in range(2)
        ]

    def put(s, at):
        copies = []
        for i in range(2):
            p, span = 2 * s + i, pl.ds(i * rows, rows)
            target = piece_of(dx, where[2], LABELS[p], rows)
            copies.append(
                pltpu.make_async_copy(xbuf.at[at, span], target, out_sem.at[at, i])
            )
            target = wide.at[pl.ds(s * rows, rows)]
            if i == 1:
                at_row = pl.multiple_of((numbers[p] // 2) * rows, rows)
                target = mix.at[pl.ds(at_row, rows)]
            copies.append(
                pltpu.make_async_copy(mbuf.at[at, span], target, out_sem.at[at, 2 + i])
            )
        return copies

    @pl.when(step == 0)
    def _():
        for copy in fetch(0, 0):
            copy.start()
        dgate[...] = seed[...]

    for s in range(1, 4):

        @pl.when(step == s - 1)
        def _():
            for copy in fetch(s, s % 2):
                copy.start()

    for copy in fetch(0, slot):
        copy.wait()
    for s in range(2, 4):

        @pl.when(step == s)
        def _():
            for copy in put(s - 2, s % 2):
                copy.wait()

    tokens = hbuf[slot]
    grads = dbuf[slot]
    experts = router.shape[0]
    columns = jnp.transpose(bits[...])
    lane = lax.broadcasted_iota(jnp.int32, columns.shape, 1)
    ids = [numbers[2 * step], numbers[2 * step + 1]]
    flags = jnp.concatenate(
        [jnp.sum(jnp.where(lane == i, columns, 0), axis=1, keepdims=True) for i in ids], axis=0
    )
    lane = lax.broadcasted_iota(jnp.int32, (2 * rows, experts), 1)
    named = jnp.bitwise_and(lax.shift_right_logical(flags + jnp.zeros_like(lane), lane), 1) == 1
    logits = jnp.where(named, dot(tokens, router[...], NT), NEGATIVE)
    weights = jnp.exp(logits - jnp.max(logits, axis=1, keepdims=True))
    gate = jnp.sum(jnp.where(lane == numbers[8], weights, 0.0), axis=1, keepdims=True)
    gate = gate / jnp.sum(weights, axis=1, keepdims=True)
    width = wg.shape[2]
    back = mixed = gate_grad = None
    for c in range(2):
        gu = dot(tokens, wg[c])
        up = dot(tokens, wu[c])
        da = dot(grads, wd[c], NT)
        sig = 1.0 / (1.0 + jnp.exp(-gu))
        silu = gu * sig
        value = silu * up
        own = jnp.sum(value * da, axis=1, keepdims=True)
        gate_grad = own if c == 0 else gate_grad + own
        low = (value * gate).astype(BF16)
        act[:, c * width : (c + 1) * width] = low
        own = dot(low, wd[c])
        mixed = own if c == 0 else mixed + own
        da = da * gate
        dgu = (da * up * sig * (1.0 + gu * (1.0 - sig))).astype(BF16)
        dup = (da * silu).astype(BF16)
        pre[:, 2 * c * width : (2 * c + 1) * width] = dgu
        pre[:, (2 * c + 1) * width : (2 * c + 2) * width] = dup
        own = dot(dgu, wg[c], NT) + dot(dup, wu[c], NT)
        back = own if c == 0 else back + own
    xbuf[slot] = back.astype(BF16)
    mbuf[slot] = mixed.astype(BF16)
    for i in range(2):
        piece = jnp.broadcast_to(gate_grad[i * rows : (i + 1) * rows], (rows, rows))
        dgate[pl.ds(ids[i], 1), :] = jnp.transpose(piece)[:1]
    for s in range(4):

        @pl.when(step == s)
        def _():
            for copy in put(s, s % 2):
                copy.start()

    @pl.when(step == 3)
    def _():
        for copy in put(2, 0) + put(3, 1):
            copy.wait()


def routed(numbers, bits, hn, dy, mix, seed, router, wg, wu, wd, tables):
    model = hn[0].shape[1]
    rows = bits.shape[1]
    width = wg.shape[2]
    hbm = pl.BlockSpec(memory_space=pl.ANY)

    def full(array):
        return pl.BlockSpec(array.shape, lambda i: (0,) * array.ndim)

    def tile(columns):
        return pl.BlockSpec((2 * rows, columns), lambda i: (i, 0))

    out = jax.ShapeDtypeStruct
    outs = [out((len(table) * rows, model), BF16) for table in tables[2]]
    outs.append(out((4 * rows, model), BF16))
    outs.append(out((bits.shape[0] // 2 * rows, model), BF16))
    mix = [] if mix is None else [mix]
    before = 2 + len(hn) + len(dy)
    got = pl.pallas_call(
        functools.partial(routed_kernel, tables, not mix),
        grid=(4,),
        in_specs=[pl.BlockSpec(memory_space=pltpu.SMEM), full(bits)]
        + [hbm] * (len(hn) + len(dy))
        + [full(array) for array in (seed, router, wg, wu, wd)]
        + [hbm] * len(mix),
        out_specs=[hbm] * len(outs) + [full(seed), tile(4 * width), tile(2 * width)],
        out_shape=outs
        + [
            out(seed.shape, F32),
            out((8 * rows, 4 * width), BF16),
            out((8 * rows, 2 * width), BF16),
        ],
        scratch_shapes=[pltpu.VMEM((2, 2 * rows, model), BF16)] * 4
        + [pltpu.SemaphoreType.DMA((2, 4))] * 2,
        input_output_aliases={before: len(outs)}
        | ({before + 5: len(outs) - 1} if mix else {}),
        compiler_params=pltpu.CompilerParams(vmem_limit_bytes=VMEM_LIMIT),
        cost_estimate=SMALL,
        name="routed_rows",
    )(numbers, bits, *hn, *dy, seed, router, wg, wu, wd, *mix)
    split = len(tables[2])
    return got[:split], *got[split:]


def expert_grads_kernel(tables, fresh, *refs):
    blocks = len(tables)
    at, hn, dy = 0, [], []
    for into, n in ((hn, 0), (dy, 1)):
        for table in tables:
            into.append(refs[at : at + len(table[n])])
            at += len(table[n])
    pre, act = refs[at : at + blocks], refs[at + blocks : at + 2 * blocks]
    at += 2 * blocks
    if not fresh:
        gu_before, gd_before = refs[at : at + 2]
        at += 2
    gu, gd, hbuf, dbuf, pbuf, abuf, sem = refs[at:]
    step = pl.program_id(0)
    slot = lax.rem(step, 2)
    rows = hbuf.shape[1] // 2

    def fetch(s, to):
        j, s = s // 4, s % 4
        copies = [
            pltpu.make_async_copy(
                piece_of(source[j], places_of(tables[j][n]), LABELS[2 * s + i], rows),
                buffer.at[to, pl.ds(i * rows, rows)],
                sem.at[to, 2 * n + i],
            )
            for n, (source, buffer) in enumerate(((hn, hbuf), (dy, dbuf)))
            for i in range(2)
        ]
        span = pl.ds(2 * s * rows, 2 * rows)
        return copies + [
            pltpu.make_async_copy(pre[j].at[span], pbuf.at[to], sem.at[to, 4]),
            pltpu.make_async_copy(act[j].at[span], abuf.at[to], sem.at[to, 5]),
        ]

    @pl.when(step == 0)
    def _():
        for copy in fetch(0, 0):
            copy.start()
        gu[...] = jnp.zeros_like(gu) if fresh else gu_before[...]
        gd[...] = jnp.zeros_like(gd) if fresh else gd_before[...]

    for s in range(1, 4 * blocks):

        @pl.when(step == s - 1)
        def _():
            for copy in fetch(s, s % 2):
                copy.start()

    for copy in fetch(0, slot):
        copy.wait()
    width = gu.shape[2]
    for c in range(2):
        gu[c] += dot(hbuf[slot], pbuf[slot, :, c * width : (c + 1) * width], TN)
    gd[...] += dot(abuf[slot], dbuf[slot], TN)


def expert_grads(hn, dy, pre, act, tables, before):
    blocks = len(pre)
    rows, model = pre[0].shape[0] // 8, hn[0][0].shape[1]
    four, two = pre[0].shape[1], act[0].shape[1]
    hbm = pl.BlockSpec(memory_space=pl.ANY)
    out = jax.ShapeDtypeStruct
    flat = [array for group in (*hn, *dy) for array in group]
    sums = [
        pl.BlockSpec((2, model, two), lambda i: (0, 0, 0)),
        pl.BlockSpec((two, model), lambda i: (0, 0)),
    ]
    fixed = len(flat) + 2 * blocks
    return pl.pallas_call(
        functools.partial(expert_grads_kernel, tables, not before),
        grid=(4 * blocks,),
        in_specs=[hbm] * fixed + (sums if before else []),
        out_specs=sums,
        out_shape=[out((2, model, two), F32), out((two, model), F32)],
        scratch_shapes=[
            pltpu.VMEM((2, 2 * rows, model), BF16),
            pltpu.VMEM((2, 2 * rows, model), BF16),
            pltpu.VMEM((2, 2 * rows, four), BF16),
            pltpu.VMEM((2, 2 * rows, two), BF16),
            pltpu.SemaphoreType.DMA((2, 6)),
        ],
        input_output_aliases={fixed: 0, fixed + 1: 1} if before else {},
        compiler_params=pltpu.CompilerParams(vmem_limit_bytes=VMEM_LIMIT),
        cost_estimate=SMALL,
        name="expert_grads",
    )(*flat, *pre, *act, *before)


def spin(values, cosine, sine):
    lane = lax.broadcasted_iota(jnp.int32, cosine.shape, 1) % HEAD_DIM
    parts = []
    for at in range(0, values.shape[1], 128):
        part = values[:, at : at + 128]
        other = jnp.where(
            lane < HEAD_DIM // 2,
            pltpu.roll(part, 128 - HEAD_DIM // 2, 1),
            pltpu.roll(part, HEAD_DIM // 2, 1),
        )
        parts.append(part * cosine + other * sine)
    return parts


def head(ref, rows, h):
    return ref[rows, h * HEAD_DIM : (h + 1) * HEAD_DIM]


def attend_kernel(
    x, gain, wq, wk, wv, wo, cosine, sine, seg_col, seg_row, normed, q, k, v, o, sums, part, stat
):
    tokens = x.shape[0]
    groups = HEADS // KV_HEADS
    inputs = x[...].astype(F32)
    inverse = lax.rsqrt(jnp.mean(inputs * inputs, axis=1, keepdims=True) + EPSILON)
    low = (inputs * inverse * gain[...].astype(F32)).astype(BF16)
    normed[...] = low
    for ref, weight in ((q, wq), (k, wk)):
        for i, piece in enumerate(spin(dot(low, weight[...]), cosine[...], sine[...])):
            ref[:, i * 128 : (i + 1) * 128] = piece.astype(BF16)
    v[...] = dot(low, wv[...]).astype(BF16)
    stat[...] = jnp.zeros_like(stat)
    step = tokens // 2
    for c in range(2):
        rows, seen = slice(c * step, (c + 1) * step), slice(0, (c + 1) * step)
        row_id = lax.broadcasted_iota(jnp.int32, (step, (c + 1) * step), 0) + c * step
        key_id = lax.broadcasted_iota(jnp.int32, (step, (c + 1) * step), 1)
        visible = (seg_col[rows, :] == seg_row[:, seen]) & (row_id >= key_id)
        for g in range(k.shape[1] // HEAD_DIM):
            keys, values = head(k, seen, g), head(v, seen, g)
            for h in range(g * groups, (g + 1) * groups):
                s = dot(head(q, rows, h), keys, NT) * HEAD_DIM**-0.5
                s = jnp.where(visible, s, NEGATIVE)
                peak = jnp.max(s, axis=1, keepdims=True)
                e = jnp.exp(s - peak)
                total = jnp.sum(e, axis=1, keepdims=True)
                p = (e * (1.0 / total)).astype(BF16)
                o[rows, h * HEAD_DIM : (h + 1) * HEAD_DIM] = dot(p, values).astype(BF16)
                stat[rows, h : h + 1] = peak + jnp.log(total)
    sums[...] = jnp.transpose(stat[...])[: sums.shape[0]]
    part[...] = dot(o[...], wo[...]).astype(BF16)


def attend(x, gain, wq, wk, wv, wo, cosine, sine, seg_col, seg_row):
    tokens, model = x.shape
    out = jax.ShapeDtypeStruct
    heads = wq.shape[1] // HEAD_DIM
    return pl.pallas_call(
        attend_kernel,
        out_shape=[
            out((tokens, model), BF16),
            out((tokens, wq.shape[1]), BF16),
            out((tokens, wk.shape[1]), BF16),
            out((tokens, wv.shape[1]), BF16),
            out((tokens, wq.shape[1]), BF16),
            out((-(-heads // 8) * 8, tokens), F32),
            out((tokens, model), BF16),
        ],
        scratch_shapes=[pltpu.VMEM((tokens, 128), F32)],
        compiler_params=pltpu.CompilerParams(vmem_limit_bytes=VMEM_LIMIT),
        cost_estimate=SMALL,
        name="attend",
    )(x, gain, wq, wk, wv, wo, cosine, sine, seg_col, seg_row)


def attend_back_kernel(
    dh, wq, wk, wv, wo, cosine, sine, seg_col, seg_row, normed, q, k, v, sums,
    weights, back, dout, dq, dk, dv, low,
):
    tokens = dh.shape[0]
    groups = HEADS // KV_HEADS
    scale = HEAD_DIM**-0.5
    dout[...] = dot(dh[...], wo[...], NT).astype(BF16)
    dk[...] = jnp.zeros_like(dk)
    dv[...] = jnp.zeros_like(dv)
    step = tokens // 2
    for c in range(2):
        rows, seen = slice(c * step, (c + 1) * step), slice(0, (c + 1) * step)
        key_id = lax.broadcasted_iota(jnp.int32, ((c + 1) * step, step), 0)
        row_id = lax.broadcasted_iota(jnp.int32, ((c + 1) * step, step), 1) + c * step
        visible = (seg_col[seen, :] == seg_row[:, rows]) & (row_id >= key_id)
        for g in range(k.shape[1] // HEAD_DIM):
            keys, values = head(k, seen, g), head(v, seen, g)
            key_sum = value_sum = None
            for h in range(g * groups, (g + 1) * groups):
                query, grad = head(q, rows, h), head(dout, rows, h)
                s = jnp.where(visible, dot(keys, query, NT) * scale, NEGATIVE)
                p = jnp.exp(s - sums[h : h + 1, rows])
                dp = dot(values, grad, NT)
                balance = jnp.sum(p * dp, axis=0, keepdims=True)
                ds = (p * (dp - balance) * scale).astype(BF16)
                dq[rows, h * HEAD_DIM : (h + 1) * HEAD_DIM] = dot(ds, keys, TN)
                own = dot(ds, query)
                key_sum = own if key_sum is None else key_sum + own
                own = dot(p.astype(BF16), grad)
                value_sum = own if value_sum is None else value_sum + own
            dk[seen, g * HEAD_DIM : (g + 1) * HEAD_DIM] += key_sum
            dv[seen, g * HEAD_DIM : (g + 1) * HEAD_DIM] += value_sum
    at = 0
    for ref in (dq, dk):
        for piece in spin(ref[...], cosine[...], -sine[...]):
            low[:, at : at + 128] = piece.astype(BF16)
            at += 128
    low[:, at:] = dv[...].astype(BF16)
    one, two = wq.shape[1], wq.shape[1] + wk.shape[1]
    total = dot(low[:, :one], wq[...], NT) + dot(low[:, one:two], wk[...], NT)
    back[...] = (total + dot(low[:, two:], wv[...], NT)).astype(BF16)
    weights[...] = dot(normed[...], low[...], TN).astype(BF16)


def attend_back(dh, wq, wk, wv, wo, cosine, sine, seg_col, seg_row, normed, q, k, v, sums):
    tokens, model = dh.shape
    out = jax.ShapeDtypeStruct
    columns = wq.shape[1] + wk.shape[1] + wv.shape[1]
    return pl.pallas_call(
        attend_back_kernel,
        out_shape=[out((model, columns), BF16), out((tokens, model), BF16)],
        scratch_shapes=[
            pltpu.VMEM((tokens, wq.shape[1]), BF16),
            pltpu.VMEM((tokens, wq.shape[1]), F32),
            pltpu.VMEM((tokens, wk.shape[1]), F32),
            pltpu.VMEM((tokens, wk.shape[1]), F32),
            pltpu.VMEM((tokens, columns), BF16),
        ],
        compiler_params=pltpu.CompilerParams(vmem_limit_bytes=VMEM_LIMIT),
        cost_estimate=SMALL,
        name="attend_back",
    )(dh, wq, wk, wv, wo, cosine, sine, seg_col, seg_row, normed, q, k, v, sums)


class Places:
    def __init__(self):
        self.count = lax.axis_size("dp")
        self.ring = self.count // 4
        me = lax.axis_index("dp")
        self.z, self.y, self.x = me // 4, (me // 2) % 2, me % 2
        self.t = lax.axis_index("tensor")
        self.sent = {"x": [], "y": [], "z": []}
        self.after = None

    def send(self, axis, array, pairs):
        sent = self.sent[axis]
        first = sent[-2:-1]
        if self.after is not None:
            first.append(self.after)
        if first:
            array = lax.optimization_barrier((array, *first))[0]
        got = lax.ppermute(array, "dp", pairs)
        sent.append(got)
        return got

    def by_x(self, array):
        return self.send("x", array, [(i, i ^ 1) for i in range(self.count)])

    def by_y(self, array):
        return self.send("y", array, [(i, i ^ 2) for i in range(self.count)])

    def by_z(self, array, step=1):
        return self.send(
            "z", array, [(i, (i + 4 * step) % self.count) for i in range(self.count)]
        )

    def by_ring(self, array, step):
        return lax.ppermute(
            array, "dp", [(i, (i + 4 * step) % self.count) for i in range(self.count)]
        )

    def by_t(self, array):
        return lax.ppermute(array, "tensor", [(0, 1), (1, 0)])

    def by(self, axis, array):
        return self.by_x(array) if axis == "x" else self.by_y(array)

    def spread_near(self, block):
        return block, self.by_x(block), self.by_y(block)

    def spread_far(self, own, beside_x, beside_y):
        half = own.shape[0] // 2
        return (
            own, beside_x, beside_y, self.by_y(beside_x[:half]), self.by_x(beside_y[half:])
        )

    def collect_far(self, near, far, order):
        return add(near, self.by(order[1], far))

    def collect_near(self, near, order):
        half = near.shape[0] // 2
        return add(near[:half], self.by(order[0], near[half:]))

    def number(self, j, label):
        y, x, half = label
        device = ((self.z - j) % self.ring) * 4 + (self.y ^ y) * 2 + (self.x ^ x)
        return device * 2 + half

    def sum_all(self, array):
        rows, columns = array.shape
        part = rows // self.count
        grid = array.reshape(self.ring, 2, 2, part, columns)
        half = columns // 2

        def split(value, place, axis):
            keep = lax.dynamic_index_in_dim(value, place, axis, keepdims=False)
            send = lax.dynamic_index_in_dim(value, 1 - place, axis, keepdims=False)
            return keep, send

        def join(own, other, place, axis):
            return jnp.where(
                place == 0, jnp.stack([own, other], axis), jnp.stack([other, own], axis)
            )

        keep_one, one = split(grid[..., :half], self.x, 2)
        keep_two, two = split(grid[..., half:], self.y, 1)
        one, two = add(keep_one, self.by_x(one)), add(keep_two, self.by_y(two))
        yield one
        keep_one, one = split(one, self.y, 1)
        keep_two, two = split(two, self.x, 1)
        got = self.by_y(one), self.by_x(two)
        one, two = add(keep_one, got[0]), add(keep_two, got[1])
        both = jnp.concatenate([one, two], axis=-1)
        yield got[0]

        def at(j):
            return lax.dynamic_index_in_dim(both, (self.z - j) % self.ring, 0, keepdims=False)

        got = [self.by_ring(at(j), -j) for j in range(1, self.ring)]
        total = sum((value.astype(F32) for value in got), at(0).astype(F32)).astype(BF16)
        got = [total]
        for j in range(1, self.ring):
            got.append(self.by_ring(total, j))
        got = jnp.stack(got)
        got = jnp.stack(
            [
                lax.dynamic_index_in_dim(got, (self.z - i) % self.ring, 0, keepdims=False)
                for i in range(self.ring)
            ]
        )
        one, two = got[..., :half], got[..., half:]
        yield
        other_one, other_two = self.by_y(one), self.by_x(two)
        one, two = join(one, other_one, self.y, 1), join(two, other_two, self.x, 1)
        yield
        other_one, other_two = self.by_x(one), self.by_y(two)
        one, two = join(one, other_one, self.x, 2), join(two, other_two, self.y, 1)
        yield jnp.concatenate([one, two], axis=-1).reshape(rows, columns)

    def own_half(self, array):
        half = array.shape[0] // 2
        return lax.dynamic_slice_in_dim(array, self.t * half, half, 0)

    def other_half(self, array):
        half = array.shape[0] // 2
        return lax.dynamic_slice_in_dim(array, (1 - self.t) * half, half, 0)

    def sum_halves(self, array):
        return self.own_half(array).astype(F32) + self.by_t(self.other_half(array)).astype(F32)

    def both_halves(self, array):
        other = self.by_t(array)
        return jnp.where(
            self.t == 0,
            jnp.concatenate([array, other], axis=0),
            jnp.concatenate([other, array], axis=0),
        )


def add(left, right):
    return (left.astype(F32) + right.astype(F32)).astype(left.dtype)


def frequencies():
    index = jnp.arange(128) % (HEAD_DIM // 2)
    return jnp.exp(index.astype(F32) * (-2.0 * math.log(10000.0) / HEAD_DIM))


def norm_back(values, inverse, gain, grad):
    scaled = gain * grad
    mean = jnp.mean(scaled * values, axis=-1, keepdims=True)
    return inverse * scaled - values * (inverse * inverse * inverse * mean)


def inverse_rms(values):
    return lax.rsqrt(jnp.mean(values * values, axis=-1, keepdims=True) + EPSILON)


def on_device(
    layer_input,
    doc_lengths,
    routes,
    norm1_gain,
    w_query,
    w_key,
    w_value,
    w_out,
    norm2_gain,
    w_router,
    w_gate,
    w_up,
    w_down,
    cotangent,
):
    places = Places()
    ring, count = places.ring, places.count
    tokens, model = layer_input.shape
    half = tokens // 2
    quarter = half // 2
    experts = w_router.shape[1]
    splits = count // experts
    gain_one = norm1_gain.astype(F32)
    gain_two = norm2_gain.astype(F32)

    dy = places.own_half(cotangent)
    block = places.spread_near(dy)
    ring_piece = dy[quarter:]
    pieces = [places.by_z(ring_piece)]
    block = places.spread_far(*block)
    wide = jnp.concatenate([piece[:quarter] for piece in block[:4]], axis=0)
    dy_second = [tuple(block[i][quarter:] for i in range(3)) + (block[4],)]
    for j in range(1, ring):
        if j + 1 < ring:
            pieces.append(places.by_z(pieces[-1]))
        beside = places.by_x(pieces[j - 1]), places.by_y(pieces[j - 1])
        far = places.by_y(beside[0]) if j % 2 else places.by_x(beside[1])
        dy_second.append((pieces[j - 1], *beside, far))
    dy_first = [wide, places.by_z(wide)]

    wg = lax.all_gather(w_gate[0], "tensor")
    wu = lax.all_gather(w_up[0], "tensor")
    wd = lax.all_gather(w_down[0], "tensor")

    lengths = doc_lengths[0]
    index = jnp.arange(tokens, dtype=jnp.int32)
    ends = jnp.cumsum(lengths)
    starts = ends - lengths
    segment = jnp.sum((index[:, None] >= ends[None, :]).astype(jnp.int32), axis=1)
    slots = jnp.arange(lengths.shape[0], dtype=jnp.int32)
    first = jnp.sum(jnp.where(segment[:, None] == slots[None, :], starts[None, :], 0), axis=1)
    angles = (index - first).astype(F32)[:, None] * frequencies()[None, :]
    cosine = jnp.cos(angles)
    sine = jnp.sin(angles) * jnp.where(jnp.arange(128) % HEAD_DIM < HEAD_DIM // 2, -1.0, 1.0)
    around = (cosine, sine, segment[:, None], segment[None, :])
    normed, queries, keys, values, mixed_heads, sums, part = attend(
        layer_input, norm1_gain[None], w_query, w_key, w_value, w_out, *around
    )
    attention = places.sum_halves(part)
    inputs_half = places.own_half(layer_input).astype(F32)
    hidden = inputs_half + attention
    inverse_two = inverse_rms(hidden)
    normed_two = (hidden * inverse_two * gain_two).astype(BF16)

    named = jnp.any(
        places.own_half(routes)[:, :, None] == jnp.arange(experts, dtype=jnp.int32), axis=1
    )
    bits = jnp.sum(
        jnp.where(named, jnp.left_shift(1, jnp.arange(experts, dtype=jnp.int32)), 0), axis=1
    )
    bits = lax.all_to_all(
        jnp.broadcast_to(bits[None], (count, half)), "dp", split_axis=0, concat_axis=0, tiled=True
    ).reshape(2 * count, quarter)
    router_rows = w_router.T
    expert = lax.axis_index("dp") // splits
    gate_grads = jnp.zeros((2 * count, quarter), F32)

    tables = (SPREAD, SPLIT, near_far("xy", 0) + near_far("yx", 1))
    dy_blocks, results, kept = [], [], []

    def run(j):
        numbers = jnp.stack([places.number(j, label) for label in LABELS] + [expert])
        dy_blocks.append((dy_first[j], *dy_second[j]))
        mix, seed = results[-1][2:4] if results else (None, gate_grads)
        results.append(
            routed(
                numbers.astype(jnp.int32), bits, hn_blocks[j], dy_blocks[j], mix, seed, router_rows,
                wg, wu, wd, tables,
            )
        )
        places.after = results[-1][3]
        kept.append(results[-1][4:6])

    def near(j):
        hn_blocks[j] = places.spread_near(ring_blocks[j])

    def far(j):
        hn_blocks[j] = places.spread_far(*hn_blocks[j])

    def back_far(j):
        parts = results[j][0]
        back[j] = [
            places.collect_far(*parts[0:2], "xy"), places.collect_far(*parts[2:4], "yx")
        ]

    def back_near(j):
        parts = [places.collect_near(part, order) for part, order in zip(back[j], ("xy", "yx"))]
        back[j] = jnp.concatenate(parts, axis=0)

    def back_ring(j):
        back[j] = places.by_z(back[j], -j)

    def onward(running, value):
        return value if running is None else add(places.by_z(running), value)

    def grads_of(blocks, before):
        per = 2 if ring < 8 else 4
        for at in range(0, len(blocks), per):
            span = blocks[at : at + per]
            before = expert_grads(
                [hn_blocks[i] for i in span],
                [dy_blocks[i] for i in span],
                [kept[i][0] for i in span],
                [kept[i][1] for i in span],
                [tables[:2] for i in span],
                before,
            )
        return before

    ring_blocks = [normed_two, places.by_z(normed_two)]
    hn_blocks, back = [None] * ring, [None] * ring
    near(0)
    near(1)
    far(0)
    for j in range(ring):
        if j + 2 < ring:
            ring_blocks.append(places.by_z(ring_blocks[-1]))
            dy_first.append(places.by_z(dy_first[-1]))
            near(j + 2)
        if j + 1 < ring:
            far(j + 1)
        if j == 3:
            first = places.by_z(results[1][1])
        if j > 2:
            back_near(j - 2)
            back_ring(j - 2)
        if j > 1:
            back_far(j - 1)
        run(j)
    last = ring - 1
    places.after = None
    back_far(last)
    if last > 1:
        back_near(last - 1)
        back_ring(last - 1)
    kept[: ring // 2] = lax.optimization_barrier((kept[: ring // 2], results[last][3]))[0]
    expert_sums = grads_of(range(ring // 2), ())
    places.after = expert_sums[1]
    back_near(last)
    places.after = None
    for j in range(2, last):
        first = places.by_z(add(first, results[j][1]))
    back_ring(last)
    moved = first
    back_far(0)
    kept[ring // 2 :] = lax.optimization_barrier((kept[ring // 2 :], back[last]))[0]
    expert_sums = grads_of(range(ring // 2, ring), expert_sums)
    back_near(0)
    second = lax.optimization_barrier((results[-1][2], back[last]))[0]
    second = lax.psum_scatter(second, "dp", scatter_dimension=0, tiled=True)
    normed_grad = sum(part.astype(F32) for part in back)
    gate_grads = lax.all_to_all(
        results[-1][3].reshape(count, half), "dp", split_axis=0, concat_axis=0, tiled=True
    )
    gate_grads = jnp.sum(gate_grads.reshape(experts, splits, half), axis=1).T

    logits = jnp.where(named, dot(normed_two, w_router), NEGATIVE)
    gates = jax.nn.softmax(logits, axis=-1)
    logit_grad = gates * (gate_grads - jnp.sum(gates * gate_grads, axis=-1, keepdims=True))
    logit_grad = logit_grad.astype(BF16)
    grad_router = dot(logit_grad, normed_two, TN)
    normed_grad = normed_grad + dot(logit_grad, w_router, NT)
    grad_gain_two = jnp.sum(normed_grad * hidden * inverse_two, axis=0)
    hidden_grad = dy.astype(F32) + norm_back(hidden, inverse_two, gain_two, normed_grad)
    hidden_low = places.both_halves(hidden_grad.astype(BF16))
    hidden_low = lax.optimization_barrier((hidden_low, moved, expert_sums[1]))[0]
    moved = places.by_z(add(moved, results[last][1]))
    first = add(moved, results[0][1])
    grad_out = dot(mixed_heads, hidden_low, TN).astype(BF16)

    grad_heads_w, part = attend_back(
        hidden_low, w_query, w_key, w_value, w_out, *around, normed, queries, keys, values, sums
    )
    grad_heads_w = places.sum_all(grad_heads_w)
    places.after = moved
    next(grad_heads_w)
    places.after = None
    first = places.collect_far(first[:half], first[half:], "xy")
    first = places.collect_near(first, "xy")
    normed_grad_one = places.sum_halves(part)
    inverse_half = inverse_rms(inputs_half)
    grad_gain_one = jnp.sum(normed_grad_one * inputs_half * inverse_half, axis=0)
    grad_input = hidden_grad + norm_back(inputs_half, inverse_half, gain_one, normed_grad_one)
    grad_input = places.both_halves(grad_input.astype(BF16))

    small = jnp.concatenate([grad_router, grad_gain_one[None], grad_gain_two[None]], axis=0)
    small = (small + places.by_t(small)).astype(BF16)
    rows, columns = grad_out.shape
    spare = 256 * (-(-small.size // (256 * rows)))
    small = jnp.pad(small.reshape(-1), (0, rows * spare - small.size)).reshape(rows, spare)
    grad_out = places.sum_all(jnp.concatenate([grad_out, small], axis=1))
    next(grad_out)
    next(grad_heads_w)
    next(grad_out)
    next(grad_heads_w)
    next(grad_out)
    next(grad_heads_w)
    next(grad_out)
    mixture = jnp.concatenate([first, second], axis=0).astype(F32)
    grad_heads_w = next(grad_heads_w).astype(F32)
    grad_out = next(grad_out).astype(F32)
    small = grad_out[:, columns:].reshape(-1)[: (experts + 2) * model].reshape(-1, model)
    grad_out = grad_out[:, :columns]
    output = places.both_halves((hidden + mixture).astype(BF16))

    grad_gu = lax.psum_scatter(expert_sums[0], "tensor", scatter_dimension=0)
    grad_d = lax.psum_scatter(expert_sums[1], "tensor", scatter_dimension=0, tiled=True)
    width = w_gate.shape[2]
    query_width, key_width = w_query.shape[1], w_key.shape[1]
    return (
        output,
        grad_input,
        small[experts],
        grad_heads_w[:, :query_width],
        grad_heads_w[:, query_width : query_width + key_width],
        grad_heads_w[:, query_width + key_width :],
        grad_out,
        small[experts + 1],
        small[:experts].T,
        grad_gu[None, :, :width],
        grad_gu[None, :, width:],
        grad_d[None],
    )


def solution(mesh):
    in_specs = (
        P("dp", None),
        P("dp", None),
        P("dp", None),
        P(),
        P(None, "tensor"),
        P(None, "tensor"),
        P(None, "tensor"),
        P("tensor", None),
        P(),
        P(),
        P("dp", None, "tensor"),
        P("dp", None, "tensor"),
        P("dp", "tensor", None),
        P("dp", None),
    )
    out_specs = (
        P("dp", None),
        P("dp", None),
        P(),
        P(None, "tensor"),
        P(None, "tensor"),
        P(None, "tensor"),
        P("tensor", None),
        P(),
        P(),
        P("dp", None, "tensor"),
        P("dp", None, "tensor"),
        P("dp", "tensor", None),
    )
    return jax.shard_map(
        on_device, mesh=mesh, in_specs=in_specs, out_specs=out_specs, check_vma=False
    )
```

time: 914 us -> 760 us (0.83)
  waiting for transfers between devices: 459 us -> 349 us
  matrix products: 81.9 us -> 4.38 us
  Pallas kernels: 108 us -> 159 us
  starting transfers between devices: 137 us -> 110 us
  between operations: 4.01 us -> 16 us
  local copies, waits for them, and re-layouts: 62.7 us -> 53.5 us
    ppermute x120 -> x90, waiting for transfers between devices: 459 us -> 322 us  [the longest x78 281 us: send(): got = lax.ppermute(array, 'dp', pairs)]
    dot_general x6 -> x0, matrix products: 62.8 us -> none  [the longest x1 20.8 us: on_device(): jnp.einsum('hgqs,shd->qhgd', score_grad, keys, preferred_element_type=F32)]
    pallas_call x5 -> x8, Pallas kernels: 108 us -> 159 us  [the longest x4 78.9 us: routed(): pl.pallas_call(functools.partial(routed_kernel, tables, not mix), grid=(4...]
    all_to_all x1, waiting for transfers between devices: 0.01 us -> 26.1 us  [on_device(): lax.all_to_all(jnp.broadcast_to(bits[None], (count, half)), 'dp', split_a...]
    ppermute x120 -> x90, starting transfers between devices: 127 us -> 102 us  [the longest x78 83.3 us: send(): got = lax.ppermute(array, 'dp', pairs)]
    unnamed x305 -> x185, local copies, waits for them, and re-layouts: 29.7 us -> 12.1 us
    dot_general x13 -> x4, matrix products: 19 us -> 4.38 us  [dot(): return lax.dot_general(left, right, dims, preferred_element_type=F32)]
    convert_element_type x46 -> x29, other arithmetic: 17.6 us -> 20.5 us  [add(): return (left.astype(F32) + right.astype(F32)).astype(left.dtype)]
  transfers between devices with their start and end apart: 133 -> 104, of which waited for: 61 -> 37; matrix products, arithmetic and copies ran while one was open for 19% -> 14% of each run, Pallas kernels for 12% -> 21%
where the time goes in v2:
time: 760 us; the launch traced here: 750 us
  waiting for transfers between devices  349 us (46%)
  Pallas kernels  159 us (21%)
  starting transfers between devices  110 us (14%)
  other arithmetic  58.7 us (8%)
  local copies, waits for them, and re-layouts  53.5 us (7%)
  between operations  16 us (2%)
    ppermute x78, waiting for transfers between devices, send(): got = lax.ppermute(array, 'dp', pairs)  281 us
    ppermute x78, starting transfers between devices, send(): got = lax.ppermute(array, 'dp', pairs)  83.3 us
    pallas_call x4, Pallas kernels, routed(): pl.pallas_call(functools.partial(routed_kernel, tables, not mix), grid=(4...  78.9 us
    ppermute x12, waiting for transfers between devices, by_ring(): lax.ppermute(array, 'dp', [(i, (i + 4 * step) % self.count) for i in rang...  40.5 us
    pallas_call x2, Pallas kernels, expert_grads(): pl.pallas_call(functools.partial(expert_grads_kernel, tables, not before)...  38.3 us
    all_to_all x1, waiting for transfers between devices, on_device(): lax.all_to_all(jnp.broadcast_to(bits[None], (count, half)), 'dp', split_a...  26.1 us
    pallas_call x1, Pallas kernels, attend_back(): pl.pallas_call(attend_back_kernel, out_shape=[out((model, columns), BF16)...  24.5 us
    convert_element_type x29, other arithmetic, add(): return (left.astype(F32) + right.astype(F32)).astype(left.dtype)  20.5 us
  transfers between devices with their start and end apart: 104, of which 37 were waited for; matrix products, arithmetic and copies ran while one was open for 14% of the time, Pallas kernels for 21%

profile of v2, /device:TPU:0, one launch (start us, length us, event | category | flops | bytes accessed | tf_op | source)
XLA Modules:
  0.0 750.1 jit_solution(3972610737520783271)
XLA Ops:
  8.0 2.1 constant_dynamic-slice_fusion.15
  10.1 3.0 collective-permute-start.5
  18.1 8.8 %collective-permute-done.1.refs_8_.refs_16_ = bf16[128,1536]{1,0:T(8,128)(2,1)} collective-permute-done((bf16[128,1536]{1,0:T(8,128)(2,1)S(1)}, bf16[128,1536]{1,0:T(8,128)(2,1)}, u32[]{:S(2)}, u32[]{:S(2)}) %collective-permute-start.1) | collective-permute-done | bytes 393248 | tf_op jit(solution)/shard_map/ppermute | solution.py:465
  28.8 17.0 %attend.1 = (bf16[512,1536]{1,0:T(8,128)(2,1)}, bf16[512,768]{1,0:T(8,128)(2,1)}, bf16[512,256]{1,0:T(8,128)(2,1)}, bf16[512,256]{1,0:T(8,128)(2,1)}, bf16[512,7...) custom-call(bf16[512,1536]{1,0:T(8,128)(2,1)} %x.3, bf16[1,1536]{1,0:T(2,128)(2,1)} %broadcast_in_dim.87.gain, ...), custom_call_target="tpu_custom_call" | custom-call | bytes 1048576 | tf_op jit(solution)/shard_map/attend/pallas_call | solution.py:365
  54.4 14.1 %collective-permute-done.18 = bf16[128,1536]{1,0:T(8,128)(2,1)S(1)} collective-permute-done((bf16[128,1536]{1,0:T(8,128)(2,1)S(1)}, bf16[128,1536]{1,0:T(8,128)(2,1)S(1)}, u32[]{:S(2)}, u32[]{:S(2)}) %collective-permute-start.18) | collective-permute-done | bytes 393248 | tf_op jit(solution)/shard_map/ppermute | solution.py:465
  71.9 2.2 multiply_reduce_fusion.2
  76.5 4.3 collective-permute-done.15.refs_9_.refs_17_
  81.3 6.3 collective-permute-done.7.refs_9_.refs_12_
  93.0 6.8 collective-permute-done.8.refs_9_.refs_17_
  100.4 5.2 collective-permute-done.16.refs_11_.refs_14_
  107.1 17.6 %collective-permute-done.4.refs_2_.refs_5_ = bf16[256,1536]{1,0:T(8,128)(2,1)} collective-permute-done((bf16[256,1536]{1,0:T(8,128)(2,1)S(1)}, bf16[256,1536]{1,0:T(8,128)(2,1)}, u32[]{:S(2)}, u32[]{:S(2)}) %collective-permute-start.4) | collective-permute-done | bytes 786464 | tf_op jit(solution)/shard_map/ppermute | solution.py:465
  130.7 13.0 %collective-permute-done.13.refs_4_.refs_7_ = bf16[256,1536]{1,0:T(8,128)(2,1)S(1)} collective-permute-done((bf16[256,1536]{1,0:T(8,128)(2,1)}, bf16[256,1536]{1,0:T(8,128)(2,1)S(1)}, u32[]{:S(2)}, u32[]{:S(2)}) %collective-permute-start.13) | collective-permute-done | bytes 786464 | tf_op jit(solution)/shard_map/ppermute | solution.py:465
  144.6 3.2 collective-permute-done.27.refs_2_.refs_0_
  150.1 3.5 all-to-all-start
  154.4 26.1 %all-to-all-done = s32[16,1,256]{2,1,0:T(1,128)S(1)} async-done(((s32[16,1,256]{2,1,0:T(1,128)}), s32[16,1,256]{2,1,0:T(1,128)S(1)}, u32[]{:S(2)}, u32[]{:S(2)}) %all-to-all-start) | async-done | bytes 16416 | tf_op jit(solution)/shard_map/all_to_all | solution.py:673
  181.2 19.7 %routed_rows.4 = (bf16[256,1536]{1,0:T(8,128)(2,1)}, bf16[256,1536]{1,0:T(8,128)(2,1)}, bf16[256,1536]{1,0:T(8,128)(2,1)}, bf16[256,1536]{1,0:T(8,128)(2,1)}, bf...) custom-call(s32[9]{0:T(128)} %stack.312.refs_0_, ...), custom_call_target="tpu_custom_call", output_to_operand_aliasing={{6}: (12, {})} | custom-call | bytes 1048576 | tf_op jit(solution)/shard_map/routed_rows/pallas_call | solution.py:194
  206.8 20.4 %collective-permute-done.25.refs_6_.refs_9_ = bf16[128,1536]{1,0:T(8,128)(2,1)} collective-permute-done((bf16[128,1536]{1,0:T(8,128)(2,1)S(1)}, bf16[128,1536]{1,0:T(8,128)(2,1)}, u32[]{:S(2)}, u32[]{:S(2)}) %collective-permute-start.25) | collective-permute-done | bytes 393248 | tf_op jit(solution)/shard_map/ppermute | solution.py:465
  230.6 19.7 %routed_rows.5 = (bf16[256,1536]{1,0:T(8,128)(2,1)}, bf16[256,1536]{1,0:T(8,128)(2,1)}, bf16[256,1536]{1,0:T(8,128)(2,1)}, bf16[256,1536]{1,0:T(8,128)(2,1)}, bf...) custom-call(s32[9]{0:T(128)} %stack.303.refs_0_, ...), custom_call_target="tpu_custom_call", output_to_operand_aliasing={{6}: (12, {}), {5}: (17, {})} | custom-call | bytes 1048576 | tf_op jit(solution)/shard_map/routed_rows/pallas_call | solution.py:194
  252.3 9.7 %collective-permute-done.31.refs_5_.refs_3_ = bf16[128,1536]{1,0:T(8,128)(2,1)S(1)} collective-permute-done((bf16[128,1536]{1,0:T(8,128)(2,1)S(1)}, bf16[128,1536]{1,0:T(8,128)(2,1)S(1)}, u32[]{:S(2)}, u32[]{:S(2)}) %collective-permute-start.31) | collective-permute-done | bytes 393248 | tf_op jit(solution)/shard_map/ppermute | solution.py:465
  262.8 2.0 collective-permute-start.35
  270.9 19.7 %routed_rows.6 = (bf16[256,1536]{1,0:T(8,128)(2,1)}, bf16[256,1536]{1,0:T(8,128)(2,1)}, bf16[256,1536]{1,0:T(8,128)(2,1)}, bf16[256,1536]{1,0:T(8,128)(2,1)}, bf...) custom-call(s32[9]{0:T(128)} %stack.321.refs_0_, ...), custom_call_target="tpu_custom_call", output_to_operand_aliasing={{6}: (12, {}), {5}: (17, {})} | custom-call | bytes 1048576 | tf_op jit(solution)/shard_map/routed_rows/pallas_call | solution.py:194
  301.8 19.7 %routed_rows.7 = (bf16[256,1536]{1,0:T(8,128)(2,1)}, bf16[256,1536]{1,0:T(8,128)(2,1)}, bf16[256,1536]{1,0:T(8,128)(2,1)}, bf16[256,1536]{1,0:T(8,128)(2,1)}, bf...) custom-call(s32[9]{0:T(128)} %stack.330.refs_0_, ...), custom_call_target="tpu_custom_call", output_to_operand_aliasing={{6}: (12, {}), {5}: (17, {})} | custom-call | bytes 1048576 | tf_op jit(solution)/shard_map/routed_rows/pallas_call | solution.py:194
  321.4 17.3 %expert_grads.2 = (f32[2,1536,512]{2,1,0:T(8,128)}, f32[512,1536]{1,0:T(8,128)}) custom-call(bf16[256,1536]{1,0:T(8,128)(2,1)} %copy-done.3, bf16[256,1536]{1,0:T(8,128)(2,1)} %copy-done.20, bf16[256,1536]{1,0:T(8,128)(2,1)} %copy-done.21, bf16[128,1536]{1,0:T(8,128)(2,1)} %collective-permute-done.22.refs_5_.refs_3_, ...), custom_call_target="tpu_custom_call" | custom-call | bytes 1048576 | tf_op jit(solution)/shard_map/expert_grads/pallas_call | solution.py:288
  345.8 14.9 %collective-permute-done.49 = bf16[128,1536]{1,0:T(8,128)(2,1)S(1)} collective-permute-done((bf16[128,1536]{1,0:T(8,128)(2,1)S(1)}, bf16[128,1536]{1,0:T(8,128)(2,1)S(1)}, u32[]{:S(2)}, u32[]{:S(2)}) %collective-permute-start.49) | collective-permute-done | bytes 393248 | tf_op jit(solution)/shard_map/ppermute | solution.py:465
  361.0 2.7 collective-permute-start.61
  365.5 6.4 collective-permute-done.53
  373.1 17.8 %collective-permute-done.61 = bf16[256,1536]{1,0:T(8,128)(2,1)} collective-permute-done((bf16[256,1536]{1,0:T(8,128)(2,1)S(1)}, bf16[256,1536]{1,0:T(8,128)(2,1)}, u32[]{:S(2)}, u32[]{:S(2)}) %collective-permute-start.61) | collective-permute-done | bytes 786464 | tf_op jit(solution)/shard_map/ppermute | solution.py:465
  390.9 13.9 %collective-permute-done.62 = bf16[256,1536]{1,0:T(8,128)(2,1)} collective-permute-done((bf16[256,1536]{1,0:T(8,128)(2,1)S(1)}, bf16[256,1536]{1,0:T(8,128)(2,1)}, u32[]{:S(2)}, u32[]{:S(2)}) %collective-permute-start.62) | collective-permute-done | bytes 786464 | tf_op jit(solution)/shard_map/ppermute | solution.py:465
  405.1 21.1 %expert_grads.3 = (f32[2,1536,512]{2,1,0:T(8,128)}, f32[512,1536]{1,0:T(8,128)}) custom-call(bf16[256,1536]{1,0:T(8,128)(2,1)} %collective-permute-done.27.refs_2_.refs_0_, bf16[256,1536]{1,0:T(8,128)(2,1)} %copy-done.17, bf16[256,1536]{1,0:T(8,128)(2,1)} %copy-done.16, ...), custom_call_target="tpu_custom_call", output_to_operand_aliasing={{0}: (24, {}), {1}: (25, {})} | custom-call | bytes 1048576 | tf_op jit(solution)/shard_map/expert_grads/pallas_call | solution.py:288
  427.6 3.5 all-to-all-start.1
  434.4 3.7 collective-permute-start.44
  441.2 2.3 add_convert_fusion.2
  443.5 25.1 %collective-permute-done.44 = bf16[256,1536]{1,0:T(8,128)(2,1)S(1)} collective-permute-done((bf16[256,1536]{1,0:T(8,128)(2,1)}, bf16[256,1536]{1,0:T(8,128)(2,1)S(1)}, u32[]{:S(2)}, u32[]{:S(2)}) %collective-permute-start.44) | collective-permute-done | bytes 786464 | tf_op jit(solution)/shard_map/ppermute | solution.py:465
  473.9 6.9 collective-permute-done.54
  482.3 2.4 multiply_reduce_fusion
  485.9 15.9 %collective-permute-done.45 = bf16[512,1536]{1,0:T(8,128)(2,1)S(1)} collective-permute-done((bf16[512,1536]{1,0:T(8,128)(2,1)S(1)}, bf16[512,1536]{1,0:T(8,128)(2,1)S(1)}, u32[]{:S(2)}, u32[]{:S(2)}) %collective-permute-start.45) | collective-permute-done | bytes 1572896 | tf_op jit(solution)/shard_map/ppermute | solution.py:465
  504.3 3.0 maximum_select_fusion.3.dh
  507.2 24.5 %attend_back.1 = (bf16[1536,1280]{1,0:T(8,128)(2,1)}, bf16[512,1536]{1,0:T(8,128)(2,1)}) custom-call(bf16[512,1536]{1,0:T(8,128)(2,1)} %maximum_select_fusion.3.dh, bf16[1536,768]{1,0:T(8,128)(2,1)} %wq.3, bf16[1536,256]{1,0:T(8,128)(2,1)} %wk.3, bf16[1536,256]{1,0:T(8,128)(2,1)} %wv.3, bf16[768,1536]{1,0:T(8,128)(2,1)} %wo.3, ...), custom_call_target="tpu_custom_call" | custom-call | bytes 1048576 | tf_op jit(solution)/shard_map/attend_back/pallas_call | solution.py:432
  539.2 10.1 %collective-permute-done.46 = bf16[512,1536]{1,0:T(8,128)(2,1)} collective-permute-done((bf16[512,1536]{1,0:T(8,128)(2,1)}, bf16[512,1536]{1,0:T(8,128)(2,1)}, u32[]{:S(2)}, u32[]{:S(2)}) %collective-permute-start.46) | collective-permute-done | bytes 1572896 | tf_op jit(solution)/shard_map/ppermute | solution.py:465
  556.1 15.7 %collective-permute-done.55 = bf16[256,1536]{1,0:T(8,128)(2,1)S(1)} collective-permute-done((bf16[256,1536]{1,0:T(8,128)(2,1)S(1)}, bf16[256,1536]{1,0:T(8,128)(2,1)S(1)}, u32[]{:S(2)}, u32[]{:S(2)}) %collective-permute-start.55) | collective-permute-done | bytes 786464 | tf_op jit(solution)/shard_map/ppermute | solution.py:465
  575.7 14.9 %collective-permute-done.70 = bf16[4,2,96,640]{3,2,1,0:T(8,128)(2,1)S(1)} collective-permute-done((bf16[4,2,96,640]{3,2,1,0:T(8,128)(2,1)S(1)}, bf16[4,2,96,640]{3,2,1,0:T(8,128)(2,1)S(1)}, u32[]{:S(2)}, u32[]{:S(2)}) %collective-permute-start.70) | collective-permute-done | bytes 983072 | tf_op jit(solution)/shard_map/ppermute | solution.py:465
  605.2 3.4 collective-permute-start.86
  608.8 1.9 collective-permute-start.88
  610.8 4.7 collective-permute-done.68
  618.8 15.2 %collective-permute-done.87 = bf16[96,1280]{1,0:T(8,128)(2,1)S(1)} collective-permute-done((bf16[96,1280]{1,0:T(8,128)(2,1)S(1)}, bf16[96,1280]{1,0:T(8,128)(2,1)S(1)}, u32[]{:S(2)}, u32[]{:S(2)}) %collective-permute-start.87) | collective-permute-done | bytes 245792 | tf_op jit(solution)/shard_map/ppermute | solution.py:481
  634.2 3.4 collective-permute-start.90
  637.6 1.9 collective-permute-start.89
  639.8 1.9 collective-permute-start.74
  642.5 7.1 collective-permute-done.90
  650.0 13.4 %collective-permute-done.75 = bf16[48,1792]{1,0:T(8,128)(2,1)S(1)} collective-permute-done((bf16[48,1792]{1,0:T(8,128)(2,1)S(1)}, bf16[48,1792]{1,0:T(8,128)(2,1)S(1)}, u32[]{:S(2)}, u32[]{:S(2)}) %collective-permute-start.75) | collective-permute-done | bytes 172064 | tf_op jit(solution)/shard_map/ppermute | solution.py:481
  663.7 2.8 collective-permute-start.78
  666.5 1.9 collective-permute-start.77
  670.6 4.8 collective-permute-done.78
  678.6 2.5 collective-permute-done.92
  682.2 6.4 collective-permute-done.81
  688.7 2.0 collective-permute-start.83
  696.6 10.0 %collective-permute-done.83 = bf16[4,2,48,896]{3,2,0,1:T(8,128)(2,1)S(1)} collective-permute-done((bf16[4,2,48,896]{3,2,0,1:T(8,128)(2,1)S(1)}, bf16[4,2,48,896]{3,2,0,1:T(8,128)(2,1)S(1)}, u32[]{:S(2)}, u32[]{:S(2)}) %collective-permute-start.83) | collective-permute-done | bytes 688160 | tf_op jit(solution)/shard_map/ppermute | solution.py:465
  712.4 2.8 slice.261
  715.2 2.1 collective-permute-done.95
  723.8 2.5 slice.260
  726.3 4.6 fusion.6
  733.4 3.7 slice_bitcast_fusion
  737.1 3.0 maximum_select_fusion.4
  740.1 2.9 maximum_select_fusion.2
  (495 shorter events, 162.8 us)
Async XLA Ops:
  7.2 173.3 %all-gather.4.cloned.1.call-start = ((), (), s32[]{:S(2)}) async-start(), calls=%async_computation.5 | async-start | bytes 2359296 | tf_op jit(solution)/shard_map/all_gather | solution.py:643
  7.9 172.6 %all-gather.6.cloned.1.call-start = ((), (), s32[]{:S(2)}) async-start(), calls=%async_computation.6 | async-start | bytes 2359296 | tf_op jit(solution)/shard_map/all_gather | solution.py:644
  10.1 38.6 %collective-permute-start.5 = (bf16[256,1536]{1,0:T(8,128)(2,1)}, bf16[256,1536]{1,0:T(8,128)(2,1)}, u32[]{:S(2)}, u32[]{:S(2)}) collective-permute-start(bf16[256,1536]{1,0:T(8,128)(2,1)} %constant_dynamic-slice_fusion.15), channel_id=1, source_target_pairs={{0,4},{2,6},{4,0},{6,2},{8,12},{10,14},{12,8},{14,10},{16,20},{18,... | collective-permute-start | bytes 2359304 | tf_op jit(solution)/shard_map/ppermute | solution.py:465
  13.1 36.1 %collective-permute-start.14 = (bf16[256,1536]{1,0:T(8,128)(2,1)}, bf16[256,1536]{1,0:T(8,128)(2,1)}, u32[]{:S(2)}, u32[]{:S(2)}) collective-permute-start(bf16[256,1536]{1,0:T(8,128)(2,1)} %constant_dynamic-slice_fusion.15), channel_id=1, source_target_pairs={{0,2},{2,0},{4,6},{6,4},{8,10},{10,8},{12,14},{14,12},{16,18},{18,... | collective-permute-start | bytes 2359304 | tf_op jit(solution)/shard_map/ppermute | solution.py:465
  46.9 23.4 %collective-permute-start = (bf16[256,1536]{1,0:T(8,128)(2,1)S(1)}, bf16[256,1536]{1,0:T(8,128)(2,1)}, u32[]{:S(2)}, u32[]{:S(2)}) collective-permute-start(bf16[256,1536]{1,0:T(8,128)(2,1)S(1)} %constant_dynamic-slice_fusion.17), channel_id=1, source_target_pairs={{0,1},{1,0},{2,3},{3,2},{4,5},{5,4},{6,7},{7,6},{8,9},{9,8},{10,11... | collective-permute-start | bytes 2359304 | tf_op jit(solution)/shard_map/ppermute | solution.py:486
  47.0 133.5 %all-gather.8.cloned.1.call-start = ((), (), s32[]{:S(2)}) async-start(), calls=%async_computation.7 | async-start | bytes 2359296 | tf_op jit(solution)/shard_map/all_gather | solution.py:645
  47.3 34.0 %collective-permute-start.3 = (bf16[128,1536]{1,0:T(8,128)(2,1)S(1)}, bf16[128,1536]{1,0:T(8,128)(2,1)S(1)}, u32[]{:S(2)}, u32[]{:S(2)}) collective-permute-start(bf16[128,1536]{1,0:T(8,128)(2,1)S(1)} %collective-permute-done.2.refs_8_.refs_11_), channel_id=1, source_target_pairs={{0,8},{2,10},{4,12},{6,14},{8,16},{10,18},{12,20},{14,22},{16,24},... | collective-permute-start | bytes 1179656 | tf_op jit(solution)/shard_map/ppermute | solution.py:465
  48.7 25.5 %collective-permute-start.10 = (bf16[128,1536]{1,0:T(8,128)(2,1)}, bf16[128,1536]{1,0:T(8,128)(2,1)S(1)}, u32[]{:S(2)}, u32[]{:S(2)}) collective-permute-start(bf16[128,1536]{1,0:T(8,128)(2,1)} %collective-permute-done.1.refs_8_.refs_16_), channel_id=1, source_target_pairs={{0,4},{2,6},{4,0},{6,2},{8,12},{10,14},{12,8},{14,10},{16,20},{18,... | collective-permute-start | bytes 1179656 | tf_op jit(solution)/shard_map/ppermute | solution.py:465
  53.9 20.9 %collective-permute-start.6 = (bf16[128,1536]{1,0:T(8,128)(2,1)S(1)}, bf16[128,1536]{1,0:T(8,128)(2,1)S(1)}, u32[]{:S(2)}, u32[]{:S(2)}) collective-permute-start(bf16[128,1536]{1,0:T(8,128)(2,1)S(1)} %get-tuple-element.311.refs_10_.refs_13_), channel_id=1, source_target_pairs={{0,2},{2,0},{4,6},{6,4},{8,10},{10,8},{12,14},{14,12},{16,18},{18,... | collective-permute-start | bytes 1179656 | tf_op jit(solution)/shard_map/ppermute | solution.py:465
  70.3 54.9 %collective-permute-start.26 = (bf16[512,1536]{1,0:T(8,128)(2,1)}, bf16[512,1536]{1,0:T(8,128)(2,1)}, u32[]{:S(2)}, u32[]{:S(2)}) collective-permute-start(bf16[512,1536]{1,0:T(8,128)(2,1)} %pad_maximum_fusion.refs_7_.refs_10_), channel_id=1, source_target_pairs={{0,8},{2,10},{4,12},{6,14},{8,16},{10,18},{12,20},{14,22},{16,24},... | collective-permute-start | bytes 4718600 | tf_op jit(solution)/shard_map/ppermute | solution.py:465
  88.1 36.6 %collective-permute-start.4 = (bf16[256,1536]{1,0:T(8,128)(2,1)S(1)}, bf16[256,1536]{1,0:T(8,128)(2,1)}, u32[]{:S(2)}, u32[]{:S(2)}) collective-permute-start(bf16[256,1536]{1,0:T(8,128)(2,1)S(1)} %multiply_convert_fusion.refs_2_.refs_0_), channel_id=1, source_target_pairs={{0,8},{2,10},{4,12},{6,14},{8,16},{10,18},{12,20},{14,22},{16,24},... | collective-permute-start | bytes 2359304 | tf_op jit(solution)/shard_map/ppermute | solution.py:465
  99.8 24.9 %collective-permute-start.12 = (bf16[128,1536]{1,0:T(8,128)(2,1)}, bf16[128,1536]{1,0:T(8,128)(2,1)}, u32[]{:S(2)}, u32[]{:S(2)}) collective-permute-start(bf16[128,1536]{1,0:T(8,128)(2,1)} %collective-permute-done.8.refs_9_.refs_17_), channel_id=1, source_target_pairs={{0,4},{2,6},{4,0},{6,2},{8,12},{10,14},{12,8},{14,10},{16,20},{18,... | collective-permute-start | bytes 1179656 | tf_op jit(solution)/shard_map/ppermute | solution.py:465
  105.6 21.1 %collective-permute-start.17 = (bf16[256,1536]{1,0:T(8,128)(2,1)S(1)}, bf16[256,1536]{1,0:T(8,128)(2,1)S(1)}, u32[]{:S(2)}, u32[]{:S(2)}) collective-permute-start(bf16[256,1536]{1,0:T(8,128)(2,1)S(1)} %multiply_convert_fusion.refs_2_.refs_0_), channel_id=1, source_target_pairs={{0,2},{2,0},{4,6},{6,4},{8,10},{10,8},{12,14},{14,12},{16,18},{18,... | collective-permute-start | bytes 2359304 | tf_op jit(solution)/shard_map/ppermute | solution.py:465
  106.2 23.2 %collective-permute-start.21 = (bf16[256,1536]{1,0:T(8,128)(2,1)S(1)}, bf16[256,1536]{1,0:T(8,128)(2,1)S(1)}, u32[]{:S(2)}, u32[]{:S(2)}) collective-permute-start(bf16[256,1536]{1,0:T(8,128)(2,1)S(1)} %multiply_convert_fusion.refs_2_.refs_0_), channel_id=1, source_target_pairs={{0,4},{2,6},{4,0},{6,2},{8,12},{10,14},{12,8},{14,10},{16,20},{18,... | collective-permute-start | bytes 2359304 | tf_op jit(solution)/shard_map/ppermute | solution.py:465
  125.2 22.6 %collective-permute-start.27 = (bf16[256,1536]{1,0:T(8,128)(2,1)}, bf16[256,1536]{1,0:T(8,128)(2,1)}, u32[]{:S(2)}, u32[]{:S(2)}) collective-permute-start(bf16[256,1536]{1,0:T(8,128)(2,1)} %collective-permute-done.4.refs_2_.refs_5_), channel_id=1, source_target_pairs={{0,8},{2,10},{4,12},{6,14},{8,16},{10,18},{12,20},{14,22},{16,24},... | collective-permute-start | bytes 2359304 | tf_op jit(solution)/shard_map/ppermute | solution.py:465
  125.2 75.7 %collective-permute-start.9 = (bf16[256,1536]{1,0:T(8,128)(2,1)}, bf16[256,1536]{1,0:T(8,128)(2,1)}, u32[]{:S(2)}, u32[]{:S(2)}) collective-permute-start(bf16[256,1536]{1,0:T(8,128)(2,1)} %collective-permute-done.4.refs_2_.refs_5_), channel_id=1, source_target_pairs={{0,2},{2,0},{4,6},{6,4},{8,10},{10,8},{12,14},{14,12},{16,18},{18,... | collective-permute-start | bytes 2359304 | tf_op jit(solution)/shard_map/ppermute | solution.py:465
  126.7 101.6 %collective-permute-start.33 = (bf16[512,1536]{1,0:T(8,128)(2,1)}, bf16[512,1536]{1,0:T(8,128)(2,1)}, u32[]{:S(2)}, u32[]{:S(2)}) collective-permute-start(bf16[512,1536]{1,0:T(8,128)(2,1)} %collective-permute-done.26.refs_7_.refs_15_), channel_id=1, source_target_pairs={{0,8},{2,10},{4,12},{6,14},{8,16},{10,18},{12,20},{14,22},{16,24},... | collective-permute-start | bytes 4718600 | tf_op jit(solution)/shard_map/ppermute | solution.py:465
  130.2 50.3 %collective-permute-start.24 = (bf16[128,1536]{1,0:T(8,128)(2,1)}, bf16[128,1536]{1,0:T(8,128)(2,1)}, u32[]{:S(2)}, u32[]{:S(2)}) collective-permute-start(bf16[128,1536]{1,0:T(8,128)(2,1)} %slice.226), channel_id=1, source_target_pairs={{0,2},{2,0},{4,6},{6,4},{8,10},{10,8},{12,14},{14,12},{16,18},{18,... | collective-permute-start | bytes 1179656 | tf_op jit(solution)/shard_map/ppermute | solution.py:465
  143.7 36.9 %collective-permute-start.22 = (bf16[128,1536]{1,0:T(8,128)(2,1)}, bf16[128,1536]{1,0:T(8,128)(2,1)}, u32[]{:S(2)}, u32[]{:S(2)}) collective-permute-start(bf16[128,1536]{1,0:T(8,128)(2,1)} %slice.223), channel_id=1, source_target_pairs={{0,4},{2,6},{4,0},{6,2},{8,12},{10,14},{12,8},{14,10},{16,20},{18,... | collective-permute-start | bytes 1179656 | tf_op jit(solution)/shard_map/ppermute | solution.py:465
  147.8 57.6 %collective-permute-start.30 = (bf16[256,1536]{1,0:T(8,128)(2,1)}, bf16[256,1536]{1,0:T(8,128)(2,1)S(1)}, u32[]{:S(2)}, u32[]{:S(2)}) collective-permute-start(bf16[256,1536]{1,0:T(8,128)(2,1)} %collective-permute-done.27.refs_2_.refs_0_), channel_id=1, source_target_pairs={{0,4},{2,6},{4,0},{6,2},{8,12},{10,14},{12,8},{14,10},{16,20},{18,... | collective-permute-start | bytes 2359304 | tf_op jit(solution)/shard_map/ppermute | solution.py:465
  150.1 30.4 %all-to-all-start = ((s32[16,1,256]{2,1,0:T(1,128)}), s32[16,1,256]{2,1,0:T(1,128)S(1)}, u32[]{:S(2)}, u32[]{:S(2)}) async-start(s32[16,1,256]{2,1,0:T(1,128)} %broadcast_in_dim.97), calls=%async_computation | async-start | bytes 32768 | tf_op jit(solution)/shard_map/all_to_all | solution.py:673
  153.6 572.7 %reduce-scatter.4.cloned.1.call-start = ((), (), s32[]{:S(2)}) async-start(), calls=%async_computation.8 | async-start | bytes 6684672 | tf_op jit(solution)/shard_map/reduce_scatter | solution.py:772
  200.9 27.4 %collective-permute-start.29 = (bf16[256,1536]{1,0:T(8,128)(2,1)}, bf16[256,1536]{1,0:T(8,128)(2,1)S(1)}, u32[]{:S(2)}, u32[]{:S(2)}) collective-permute-start(bf16[256,1536]{1,0:T(8,128)(2,1)} %collective-permute-done.27.refs_2_.refs_0_), channel_id=1, source_target_pairs={{0,2},{2,0},{4,6},{6,4},{8,10},{10,8},{12,14},{14,12},{16,18},{18,... | collective-permute-start | bytes 2359304 | tf_op jit(solution)/shard_map/ppermute | solution.py:465
  201.5 26.9 %collective-permute-start.28 = (bf16[256,1536]{1,0:T(8,128)(2,1)}, bf16[256,1536]{1,0:T(8,128)(2,1)}, u32[]{:S(2)}, u32[]{:S(2)}) collective-permute-start(bf16[256,1536]{1,0:T(8,128)(2,1)} %collective-permute-done.27.refs_2_.refs_0_), channel_id=1, source_target_pairs={{0,8},{2,10},{4,12},{6,14},{8,16},{10,18},{12,20},{14,22},{16,24},... | collective-permute-start | bytes 2359304 | tf_op jit(solution)/shard_map/ppermute | solution.py:465
  202.1 25.1 %collective-permute-start.25 = (bf16[128,1536]{1,0:T(8,128)(2,1)S(1)}, bf16[128,1536]{1,0:T(8,128)(2,1)}, u32[]{:S(2)}, u32[]{:S(2)}) collective-permute-start(bf16[128,1536]{1,0:T(8,128)(2,1)S(1)} %slice.225), channel_id=1, source_target_pairs={{0,2},{2,0},{4,6},{6,4},{8,10},{10,8},{12,14},{14,12},{16,18},{18,... | collective-permute-start | bytes 1179656 | tf_op jit(solution)/shard_map/ppermute | solution.py:465
  205.5 25.1 %collective-permute-start.23 = (bf16[128,1536]{1,0:T(8,128)(2,1)}, bf16[128,1536]{1,0:T(8,128)(2,1)}, u32[]{:S(2)}, u32[]{:S(2)}) collective-permute-start(bf16[128,1536]{1,0:T(8,128)(2,1)} %slice.222), channel_id=1, source_target_pairs={{0,4},{2,6},{4,0},{6,2},{8,12},{10,14},{12,8},{14,10},{16,20},{18,... | collective-permute-start | bytes 1179656 | tf_op jit(solution)/shard_map/ppermute | solution.py:465
  227.2 23.1 %collective-permute-start.32 = (bf16[128,1536]{1,0:T(8,128)(2,1)}, bf16[128,1536]{1,0:T(8,128)(2,1)S(1)}, u32[]{:S(2)}, u32[]{:S(2)}) collective-permute-start(bf16[128,1536]{1,0:T(8,128)(2,1)} %slice.230), channel_id=1, source_target_pairs={{0,2},{2,0},{4,6},{6,4},{8,10},{10,8},{12,14},{14,12},{16,18},{18,... | collective-permute-start | bytes 1179656 | tf_op jit(solution)/shard_map/ppermute | solution.py:465
  228.4 38.2 %collective-permute-start.37 = (bf16[256,1536]{1,0:T(8,128)(2,1)}, bf16[256,1536]{1,0:T(8,128)(2,1)}, u32[]{:S(2)}, u32[]{:S(2)}) collective-permute-start(bf16[256,1536]{1,0:T(8,128)(2,1)} %collective-permute-done.28.refs_2_.refs_5_), channel_id=1, source_target_pairs={{0,2},{2,0},{4,6},{6,4},{8,10},{10,8},{12,14},{14,12},{16,18},{18,... | collective-permute-start | bytes 2359304 | tf_op jit(solution)/shard_map/ppermute | solution.py:465
  230.0 37.7 %collective-permute-start.36 = (bf16[256,1536]{1,0:T(8,128)(2,1)}, bf16[256,1536]{1,0:T(8,128)(2,1)}, u32[]{:S(2)}, u32[]{:S(2)}) collective-permute-start(bf16[256,1536]{1,0:T(8,128)(2,1)} %collective-permute-done.28.refs_2_.refs_5_), channel_id=1, source_target_pairs={{0,4},{2,6},{4,0},{6,2},{8,12},{10,14},{12,8},{14,10},{16,20},{18,... | collective-permute-start | bytes 2359304 | tf_op jit(solution)/shard_map/ppermute | solution.py:465
  250.3 40.3 %collective-permute-start.40 = (bf16[256,1536]{1,0:T(8,128)(2,1)}, bf16[256,1536]{1,0:T(8,128)(2,1)}, u32[]{:S(2)}, u32[]{:S(2)}) collective-permute-start(bf16[256,1536]{1,0:T(8,128)(2,1)} %get-tuple-element.188), channel_id=1, source_target_pairs={{0,2},{2,0},{4,6},{6,4},{8,10},{10,8},{12,14},{14,12},{16,18},{18,... | collective-permute-start | bytes 2359304 | tf_op jit(solution)/shard_map/ppermute | solution.py:465
  262.8 29.3 %collective-permute-start.35 = (bf16[256,1536]{1,0:T(8,128)(2,1)}, bf16[256,1536]{1,0:T(8,128)(2,1)}, u32[]{:S(2)}, u32[]{:S(2)}) collective-permute-start(bf16[256,1536]{1,0:T(8,128)(2,1)} %get-tuple-element.181), channel_id=1, source_target_pairs={{0,4},{2,6},{4,0},{6,2},{8,12},{10,14},{12,8},{14,10},{16,20},{18,... | collective-permute-start | bytes 2359304 | tf_op jit(solution)/shard_map/ppermute | solution.py:465
  264.8 35.8 %collective-permute-start.43 = (bf16[512,1536]{1,0:T(8,128)(2,1)}, bf16[512,1536]{1,0:T(8,128)(2,1)S(1)}, u32[]{:S(2)}, u32[]{:S(2)}) collective-permute-start(bf16[512,1536]{1,0:T(8,128)(2,1)} %collective-permute-done.33.refs_7_.refs_10_), channel_id=1, source_target_pairs={{0,8},{2,10},{4,12},{6,14},{8,16},{10,18},{12,20},{14,22},{16,24},... | collective-permute-start | bytes 4718600 | tf_op jit(solution)/shard_map/ppermute | solution.py:465
  268.7 27.3 %collective-permute-start.38 = (bf16[128,1536]{1,0:T(8,128)(2,1)S(1)}, bf16[128,1536]{1,0:T(8,128)(2,1)S(1)}, u32[]{:S(2)}, u32[]{:S(2)}) collective-permute-start(bf16[128,1536]{1,0:T(8,128)(2,1)S(1)} %slice.233), channel_id=1, source_target_pairs={{0,2},{2,0},{4,6},{6,4},{8,10},{10,8},{12,14},{14,12},{16,18},{18,... | collective-permute-start | bytes 1179656 | tf_op jit(solution)/shard_map/ppermute | solution.py:465
  270.3 27.0 %collective-permute-start.41 = (bf16[128,1536]{1,0:T(8,128)(2,1)S(1)}, bf16[128,1536]{1,0:T(8,128)(2,1)}, u32[]{:S(2)}, u32[]{:S(2)}) collective-permute-start(bf16[128,1536]{1,0:T(8,128)(2,1)S(1)} %slice.236), channel_id=1, source_target_pairs={{0,4},{2,6},{4,0},{6,2},{8,12},{10,14},{12,8},{14,10},{16,20},{18,... | collective-permute-start | bytes 1179656 | tf_op jit(solution)/shard_map/ppermute | solution.py:465
  292.1 48.7 %collective-permute-start.47 = (bf16[256,1536]{1,0:T(8,128)(2,1)}, bf16[256,1536]{1,0:T(8,128)(2,1)}, u32[]{:S(2)}, u32[]{:S(2)}) collective-permute-start(bf16[256,1536]{1,0:T(8,128)(2,1)} %get-tuple-element.202), channel_id=1, source_target_pairs={{0,4},{2,6},{4,0},{6,2},{8,12},{10,14},{12,8},{14,10},{16,20},{18,... | collective-permute-start | bytes 2359304 | tf_op jit(solution)/shard_map/ppermute | solution.py:465
  296.8 41.9 %collective-permute-start.39 = (bf16[128,1536]{1,0:T(8,128)(2,1)}, bf16[128,1536]{1,0:T(8,128)(2,1)}, u32[]{:S(2)}, u32[]{:S(2)}) collective-permute-start(bf16[128,1536]{1,0:T(8,128)(2,1)} %slice.232), channel_id=1, source_target_pairs={{0,2},{2,0},{4,6},{6,4},{8,10},{10,8},{12,14},{14,12},{16,18},{18,... | collective-permute-start | bytes 1179656 | tf_op jit(solution)/shard_map/ppermute | solution.py:465
  297.3 41.5 %collective-permute-start.42 = (bf16[128,1536]{1,0:T(8,128)(2,1)S(1)}, bf16[128,1536]{1,0:T(8,128)(2,1)}, u32[]{:S(2)}, u32[]{:S(2)}) collective-permute-start(bf16[128,1536]{1,0:T(8,128)(2,1)S(1)} %slice.235), channel_id=1, source_target_pairs={{0,4},{2,6},{4,0},{6,2},{8,12},{10,14},{12,8},{14,10},{16,20},{18,... | collective-permute-start | bytes 1179656 | tf_op jit(solution)/shard_map/ppermute | solution.py:465
  297.8 44.4 %collective-permute-start.48 = (bf16[256,1536]{1,0:T(8,128)(2,1)}, bf16[256,1536]{1,0:T(8,128)(2,1)}, u32[]{:S(2)}, u32[]{:S(2)}) collective-permute-start(bf16[256,1536]{1,0:T(8,128)(2,1)} %get-tuple-element.204), channel_id=1, source_target_pairs={{0,2},{2,0},{4,6},{6,4},{8,10},{10,8},{12,14},{14,12},{16,18},{18,... | collective-permute-start | bytes 2359304 | tf_op jit(solution)/shard_map/ppermute | solution.py:465
  300.6 60.4 %collective-permute-start.34 = (bf16[512,1536]{1,0:T(8,128)(2,1)}, bf16[512,1536]{1,0:T(8,128)(2,1)S(1)}, u32[]{:S(2)}, u32[]{:S(2)}) collective-permute-start(bf16[512,1536]{1,0:T(8,128)(2,1)} %get-tuple-element.177), channel_id=1, source_target_pairs={{0,8},{2,10},{4,12},{6,14},{8,16},{10,18},{12,20},{14,22},{16,24},... | collective-permute-start | bytes 4718600 | tf_op jit(solution)/shard_map/ppermute | solution.py:465
  338.7 25.3 %collective-permute-start.52 = (bf16[256,1536]{1,0:T(8,128)(2,1)S(1)}, bf16[256,1536]{1,0:T(8,128)(2,1)S(1)}, u32[]{:S(2)}, u32[]{:S(2)}) collective-permute-start(bf16[256,1536]{1,0:T(8,128)(2,1)S(1)} %copy-done.88), channel_id=1, source_target_pairs={{0,4},{2,6},{4,0},{6,2},{8,12},{10,14},{12,8},{14,10},{16,20},{18,... | collective-permute-start | bytes 2359304 | tf_op jit(solution)/shard_map/ppermute | solution.py:465
  340.3 23.5 %collective-permute-start.51 = (bf16[256,1536]{1,0:T(8,128)(2,1)S(1)}, bf16[256,1536]{1,0:T(8,128)(2,1)S(1)}, u32[]{:S(2)}, u32[]{:S(2)}) collective-permute-start(bf16[256,1536]{1,0:T(8,128)(2,1)S(1)} %copy-done.89), channel_id=1, source_target_pairs={{0,2},{2,0},{4,6},{6,4},{8,10},{10,8},{12,14},{14,12},{16,18},{18,... | collective-permute-start | bytes 2359304 | tf_op jit(solution)/shard_map/ppermute | solution.py:465
  361.0 29.9 %collective-permute-start.61 = (bf16[256,1536]{1,0:T(8,128)(2,1)S(1)}, bf16[256,1536]{1,0:T(8,128)(2,1)}, u32[]{:S(2)}, u32[]{:S(2)}) collective-permute-start(bf16[256,1536]{1,0:T(8,128)(2,1)S(1)} %pad_maximum_fusion.5), channel_id=1, source_target_pairs={{0,16},{2,18},{4,20},{6,22},{8,24},{10,26},{12,28},{14,30},{16,0},... | collective-permute-start | bytes 2359304 | tf_op jit(solution)/shard_map/ppermute | solution.py:465
  404.8 328.6 %reduce-scatter.6.cloned.1.call-start = ((), (), s32[]{:S(2)}) async-start(), calls=%async_computation.9 | async-start | bytes 9437184 | tf_op jit(solution)/shard_map/reduce_scatter | solution.py:828
  431.1 311.9 %reduce-scatter.8.cloned.1.call-start = ((), (), s32[]{:S(2)}) async-start(), calls=%async_computation.10 | async-start | bytes 4718592 | tf_op jit(solution)/shard_map/reduce_scatter | solution.py:829
  434.4 34.2 %collective-permute-start.44 = (bf16[256,1536]{1,0:T(8,128)(2,1)}, bf16[256,1536]{1,0:T(8,128)(2,1)S(1)}, u32[]{:S(2)}, u32[]{:S(2)}) collective-permute-start(bf16[256,1536]{1,0:T(8,128)(2,1)} %pad_maximum_fusion.3), channel_id=1, source_target_pairs={{0,24},{2,26},{4,28},{6,30},{8,0},{10,2},{12,4},{14,6},{16,8},{18,... | collective-permute-start | bytes 2359304 | tf_op jit(solution)/shard_map/ppermute | solution.py:465
  438.1 31.5 %collective-permute-start.50 = (bf16[256,1536]{1,0:T(8,128)(2,1)}, bf16[256,1536]{1,0:T(8,128)(2,1)}, u32[]{:S(2)}, u32[]{:S(2)}) collective-permute-start(bf16[256,1536]{1,0:T(8,128)(2,1)} %get-tuple-element.206), channel_id=1, source_target_pairs={{0,2},{2,0},{4,6},{6,4},{8,10},{10,8},{12,14},{14,12},{16,18},{18,... | collective-permute-start | bytes 2359304 | tf_op jit(solution)/shard_map/ppermute | solution.py:465
  439.6 32.8 %collective-permute-start.57 = (bf16[256,1536]{1,0:T(8,128)(2,1)}, bf16[256,1536]{1,0:T(8,128)(2,1)S(1)}, u32[]{:S(2)}, u32[]{:S(2)}) collective-permute-start(bf16[256,1536]{1,0:T(8,128)(2,1)} %get-tuple-element.229), channel_id=1, source_target_pairs={{0,4},{2,6},{4,0},{6,2},{8,12},{10,14},{12,8},{14,10},{16,20},{18,... | collective-permute-start | bytes 2359304 | tf_op jit(solution)/shard_map/ppermute | solution.py:465
  468.7 33.2 %collective-permute-start.45 = (bf16[512,1536]{1,0:T(8,128)(2,1)S(1)}, bf16[512,1536]{1,0:T(8,128)(2,1)S(1)}, u32[]{:S(2)}, u32[]{:S(2)}) collective-permute-start(bf16[512,1536]{1,0:T(8,128)(2,1)S(1)} %add_convert_fusion.2), channel_id=1, source_target_pairs={{0,8},{2,10},{4,12},{6,14},{8,16},{10,18},{12,20},{14,22},{16,24},... | collective-permute-start | bytes 4718600 | tf_op jit(solution)/shard_map/ppermute | solution.py:465
  503.4 45.9 %collective-permute-start.46 = (bf16[512,1536]{1,0:T(8,128)(2,1)}, bf16[512,1536]{1,0:T(8,128)(2,1)}, u32[]{:S(2)}, u32[]{:S(2)}) collective-permute-start(bf16[512,1536]{1,0:T(8,128)(2,1)} %add_convert_fusion.1), channel_id=1, source_target_pairs={{0,8},{2,10},{4,12},{6,14},{8,16},{10,18},{12,20},{14,22},{16,24},... | collective-permute-start | bytes 4718600 | tf_op jit(solution)/shard_map/ppermute | solution.py:465
  533.0 21.9 %collective-permute-start.65 = (bf16[256,1536]{1,0:T(8,128)(2,1)S(1)}, bf16[256,1536]{1,0:T(8,128)(2,1)S(1)}, u32[]{:S(2)}, u32[]{:S(2)}) collective-permute-start(bf16[256,1536]{1,0:T(8,128)(2,1)S(1)} %constant_dynamic-slice_fusion.14), channel_id=1, source_target_pairs={{0,1},{1,0},{2,3},{3,2},{4,5},{5,4},{6,7},{7,6},{8,9},{9,8},{10,11... | collective-permute-start | bytes 2359304 | tf_op jit(solution)/shard_map/ppermute | solution.py:486
  551.2 20.7 %collective-permute-start.55 = (bf16[256,1536]{1,0:T(8,128)(2,1)S(1)}, bf16[256,1536]{1,0:T(8,128)(2,1)S(1)}, u32[]{:S(2)}, u32[]{:S(2)}) collective-permute-start(bf16[256,1536]{1,0:T(8,128)(2,1)S(1)} %slice.238), channel_id=1, source_target_pairs={{0,4},{2,6},{4,0},{6,2},{8,12},{10,14},{12,8},{14,10},{16,20},{18,... | collective-permute-start | bytes 2359304 | tf_op jit(solution)/shard_map/ppermute | solution.py:465
  552.8 21.0 %collective-permute-start.67 = (bf16[4,2,96,640]{3,2,0,1:T(8,128)(2,1)S(1)}, bf16[4,2,96,640]{3,2,0,1:T(8,128)(2,1)S(1)}, u32[]{:S(2)}, u32[]{:S(2)}) collective-permute-start(bf16[4,2,96,640]{3,2,0,1:T(8,128)(2,1)S(1)} %bitcast.211), channel_id=1, source_target_pairs={{0,2},{2,0},{4,6},{6,4},{8,10},{10,8},{12,14},{14,12},{16,18},{18,... | collective-permute-start | bytes 2949128 | tf_op jit(solution)/shard_map/ppermute | solution.py:465
  553.9 36.8 %collective-permute-start.70 = (bf16[4,2,96,640]{3,2,1,0:T(8,128)(2,1)S(1)}, bf16[4,2,96,640]{3,2,1,0:T(8,128)(2,1)S(1)}, u32[]{:S(2)}, u32[]{:S(2)}) collective-permute-start(bf16[4,2,96,640]{3,2,1,0:T(8,128)(2,1)S(1)} %dynamic-slice_bitcast_fusion), channel_id=1, source_target_pairs={{0,4},{2,6},{4,0},{6,2},{8,12},{10,14},{12,8},{14,10},{16,20},{18,... | collective-permute-start | bytes 2949128 | tf_op jit(solution)/shard_map/ppermute | solution.py:465
  556.1 37.7 %collective-permute-start.69 = (f32[18,1536]{1,0:T(8,128)S(1)}, f32[18,1536]{1,0:T(8,128)S(1)}, u32[]{:S(2)}, u32[]{:S(2)}) collective-permute-start(f32[18,1536]{1,0:T(8,128)S(1)} %pad_maximum_fusion.8), channel_id=1, source_target_pairs={{0,1},{1,0},{2,3},{3,2},{4,5},{5,4},{6,7},{7,6},{8,9},{9,8},{10,11... | collective-permute-start | bytes 331784 | tf_op jit(solution)/shard_map/ppermute | solution.py:486
  574.8 27.9 %collective-permute-start.84 = (bf16[4,96,640]{2,1,0:T(8,128)(2,1)}, bf16[4,96,640]{2,1,0:T(8,128)(2,1)}, u32[]{:S(2)}, u32[]{:S(2)}) collective-permute-start(bf16[4,96,640]{2,1,0:T(8,128)(2,1)} %dynamic-slice_bitcast_fusion.2), channel_id=1, source_target_pairs={{0,4},{2,6},{4,0},{6,2},{8,12},{10,14},{12,8},{14,10},{16,20},{18,... | collective-permute-start | bytes 1474568 | tf_op jit(solution)/shard_map/ppermute | solution.py:465
  608.7 25.3 %collective-permute-start.87 = (bf16[96,1280]{1,0:T(8,128)(2,1)S(1)}, bf16[96,1280]{1,0:T(8,128)(2,1)S(1)}, u32[]{:S(2)}, u32[]{:S(2)}) collective-permute-start(bf16[96,1280]{1,0:T(8,128)(2,1)S(1)} %get-tuple-element.309), channel_id=1, source_target_pairs={{0,16},{2,18},{4,20},{6,22},{8,24},{10,26},{12,28},{14,30},{16,0},... | collective-permute-start | bytes 737288 | tf_op jit(solution)/shard_map/ppermute | solution.py:481
  608.8 25.2 %collective-permute-start.88 = (bf16[96,1280]{1,0:T(8,128)(2,1)S(1)}, bf16[96,1280]{1,0:T(8,128)(2,1)S(1)}, u32[]{:S(2)}, u32[]{:S(2)}) collective-permute-start(bf16[96,1280]{1,0:T(8,128)(2,1)S(1)} %get-tuple-element.310), channel_id=1, source_target_pairs={{0,8},{2,10},{4,12},{6,14},{8,16},{10,18},{12,20},{14,22},{16,24},... | collective-permute-start | bytes 737288 | tf_op jit(solution)/shard_map/ppermute | solution.py:481
  616.5 23.0 %collective-permute-start.73 = (bf16[4,48,896]{2,1,0:T(8,128)(2,1)S(1)}, bf16[4,48,896]{2,1,0:T(8,128)(2,1)S(1)}, u32[]{:S(2)}, u32[]{:S(2)}) collective-permute-start(bf16[4,48,896]{2,1,0:T(8,128)(2,1)S(1)} %dynamic-slice_bitcast_fusion.3), channel_id=1, source_target_pairs={{0,2},{2,0},{4,6},{6,4},{8,10},{10,8},{12,14},{14,12},{16,18},{18,... | collective-permute-start | bytes 1032200 | tf_op jit(solution)/shard_map/ppermute | solution.py:465
  617.9 21.7 %collective-permute-start.72 = (bf16[4,48,896]{2,1,0:T(8,128)(2,1)S(1)}, bf16[4,48,896]{2,1,0:T(8,128)(2,1)S(1)}, u32[]{:S(2)}, u32[]{:S(2)}) collective-permute-start(bf16[4,48,896]{2,1,0:T(8,128)(2,1)S(1)} %dynamic-slice_bitcast_fusion.4), channel_id=1, source_target_pairs={{0,4},{2,6},{4,0},{6,2},{8,12},{10,14},{12,8},{14,10},{16,20},{18,... | collective-permute-start | bytes 1032200 | tf_op jit(solution)/shard_map/ppermute | solution.py:465
  641.7 21.7 %collective-permute-start.75 = (bf16[48,1792]{1,0:T(8,128)(2,1)S(1)}, bf16[48,1792]{1,0:T(8,128)(2,1)S(1)}, u32[]{:S(2)}, u32[]{:S(2)}) collective-permute-start(bf16[48,1792]{1,0:T(8,128)(2,1)S(1)} %get-tuple-element.326), channel_id=1, source_target_pairs={{0,16},{2,18},{4,20},{6,22},{8,24},{10,26},{12,28},{14,30},{16,0},... | collective-permute-start | bytes 516104 | tf_op jit(solution)/shard_map/ppermute | solution.py:481
  641.7 21.7 %collective-permute-start.76 = (bf16[48,1792]{1,0:T(8,128)(2,1)S(1)}, bf16[48,1792]{1,0:T(8,128)(2,1)S(1)}, u32[]{:S(2)}, u32[]{:S(2)}) collective-permute-start(bf16[48,1792]{1,0:T(8,128)(2,1)S(1)} %get-tuple-element.327), channel_id=1, source_target_pairs={{0,8},{2,10},{4,12},{6,14},{8,16},{10,18},{12,20},{14,22},{16,24},... | collective-permute-start | bytes 516104 | tf_op jit(solution)/shard_map/ppermute | solution.py:481
  669.6 21.9 %collective-permute-start.93 = (bf16[4,96,640]{2,1,0:T(8,128)(2,1)S(1)}, bf16[4,96,640]{2,1,0:T(8,128)(2,1)S(1)}, u32[]{:S(2)}, u32[]{:S(2)}) collective-permute-start(bf16[4,96,640]{2,1,0:T(8,128)(2,1)S(1)} %get-tuple-element.270), channel_id=1, source_target_pairs={{0,2},{2,0},{4,6},{6,4},{8,10},{10,8},{12,14},{14,12},{16,18},{18,... | collective-permute-start | bytes 1474568 | tf_op jit(solution)/shard_map/ppermute | solution.py:465
  692.6 24.7 %collective-permute-start.95 = (bf16[4,2,96,640]{3,2,0,1:T(8,128)(2,1)}, bf16[4,2,96,640]{3,2,0,1:T(8,128)(2,1)}, u32[]{:S(2)}, u32[]{:S(2)}) collective-permute-start(bf16[4,2,96,640]{3,2,0,1:T(8,128)(2,1)} %maximum_select_fusion.10), channel_id=1, source_target_pairs={{0,4},{2,6},{4,0},{6,2},{8,12},{10,14},{12,8},{14,10},{16,20},{18,... | collective-permute-start | bytes 2949128 | tf_op jit(solution)/shard_map/ppermute | solution.py:465
  693.1 26.3 %collective-permute-start.94 = (bf16[4,2,96,640]{3,2,0,1:T(8,128)(2,1)}, bf16[4,2,96,640]{3,2,0,1:T(8,128)(2,1)}, u32[]{:S(2)}, u32[]{:S(2)}) collective-permute-start(bf16[4,2,96,640]{3,2,0,1:T(8,128)(2,1)} %maximum_select_fusion.8), channel_id=1, source_target_pairs={{0,2},{2,0},{4,6},{6,4},{8,10},{10,8},{12,14},{14,12},{16,18},{18,... | collective-permute-start | bytes 2949128 | tf_op jit(solution)/shard_map/ppermute | solution.py:465
  (131 other events, 2043.3 us)
Sparse Core Ops, SparseCore 0:
  9.6 12.4 all-gather.3
  47.2 9.5 all-gather.5
  100.5 9.7 all-gather.7
  405.0 160.4 reduce-scatter.3
  567.6 13.2 reduce-scatter.5
  583.7 12.0 reduce-scatter.7

commit v3 on v2

--- a/solution.py
+++ b/solution.py
@@ -56,11 +56,11 @@
 def routed_kernel(tables, fresh, *refs):
     counts = [len(table) for table in tables]
     groups, at = [], 2
-    for size in (counts[0], counts[1], 1, 1, 1, 1, 1, 0 if fresh else 1, counts[2], 1, 1, 1, 1, 1, 6):
+    for size in (counts[0], counts[1], 1, 1, 1, 1, 1, 0 if fresh else 1, counts[2], 1, 1, 1, 1, 6):
         groups.append(refs[at : at + size])
         at += size
     numbers, bits = refs[0], refs[1]
-    hn, dy, (seed,), (router,), (wg,), (wu,), (wd,), _, dx, (wide,), (mix,), *rest = groups
+    hn, dy, (seed,), (router,), (wg,), (wu,), (wd,), _, dx, (mix,), *rest = groups
     (dgate,), (pre,), (act,), scratch = rest
     hbuf, dbuf, xbuf, mbuf, in_sem, out_sem = scratch
     where = [places_of(table) for table in tables]
@@ -87,10 +87,7 @@
             copies.append(
                 pltpu.make_async_copy(xbuf.at[at, span], target, out_sem.at[at, i])
             )
-            target = wide.at[pl.ds(s * rows, rows)]
-            if i == 1:
-                at_row = pl.multiple_of((numbers[p] // 2) * rows, rows)
-                target = mix.at[pl.ds(at_row, rows)]
+            target = mix.at[pl.ds(pl.multiple_of(numbers[p] * rows, rows), rows)]
             copies.append(
                 pltpu.make_async_copy(mbuf.at[at, span], target, out_sem.at[at, 2 + i])
             )
@@ -187,8 +184,7 @@
 
     out = jax.ShapeDtypeStruct
     outs = [out((len(table) * rows, model), BF16) for table in tables[2]]
-    outs.append(out((4 * rows, model), BF16))
-    outs.append(out((bits.shape[0] // 2 * rows, model), BF16))
+    outs.append(out((bits.shape[0] * rows, model), BF16))
     mix = [] if mix is None else [mix]
     before = 2 + len(hn) + len(dy)
     got = pl.pallas_call(
@@ -453,11 +449,11 @@
         self.z, self.y, self.x = me // 4, (me // 2) % 2, me % 2
         self.t = lax.axis_index("tensor")
         self.sent = {"x": [], "y": [], "z": []}
-        self.after = None
+        self.after = self.single = None
 
     def send(self, axis, array, pairs):
         sent = self.sent[axis]
-        first = sent[-2:-1]
+        first = sent[-1:] if axis == self.single else sent[-2:-1]
         if self.after is not None:
             first.append(self.after)
         if first:
@@ -531,10 +527,9 @@
         yield one
         keep_one, one = split(one, self.y, 1)
         keep_two, two = split(two, self.x, 1)
-        got = self.by_y(one), self.by_x(two)
-        one, two = add(keep_one, got[0]), add(keep_two, got[1])
+        one, two = add(keep_one, self.by_y(one)), add(keep_two, self.by_x(two))
         both = jnp.concatenate([one, two], axis=-1)
-        yield got[0]
+        yield
 
         def at(j):
             return lax.dynamic_index_in_dim(both, (self.z - j) % self.ring, 0, keepdims=False)
@@ -644,6 +639,16 @@
     wu = lax.all_gather(w_up[0], "tensor")
     wd = lax.all_gather(w_down[0], "tensor")
 
+    named = jnp.any(
+        places.own_half(routes)[:, :, None] == jnp.arange(experts, dtype=jnp.int32), axis=1
+    )
+    bits = jnp.sum(
+        jnp.where(named, jnp.left_shift(1, jnp.arange(experts, dtype=jnp.int32)), 0), axis=1
+    )
+    bits = lax.all_to_all(
+        jnp.broadcast_to(bits[None], (count, half)), "dp", split_axis=0, concat_axis=0, tiled=True
+    ).reshape(2 * count, quarter)
+
     lengths = doc_lengths[0]
     index = jnp.arange(tokens, dtype=jnp.int32)
     ends = jnp.cumsum(lengths)
@@ -658,21 +663,13 @@
     normed, queries, keys, values, mixed_heads, sums, part = attend(
         layer_input, norm1_gain[None], w_query, w_key, w_value, w_out, *around
     )
+    part, bits = lax.optimization_barrier((part, bits))
     attention = places.sum_halves(part)
     inputs_half = places.own_half(layer_input).astype(F32)
     hidden = inputs_half + attention
     inverse_two = inverse_rms(hidden)
     normed_two = (hidden * inverse_two * gain_two).astype(BF16)
 
-    named = jnp.any(
-        places.own_half(routes)[:, :, None] == jnp.arange(experts, dtype=jnp.int32), axis=1
-    )
-    bits = jnp.sum(
-        jnp.where(named, jnp.left_shift(1, jnp.arange(experts, dtype=jnp.int32)), 0), axis=1
-    )
-    bits = lax.all_to_all(
-        jnp.broadcast_to(bits[None], (count, half)), "dp", split_axis=0, concat_axis=0, tiled=True
-    ).reshape(2 * count, quarter)
     router_rows = w_router.T
     expert = lax.axis_index("dp") // splits
     gate_grads = jnp.zeros((2 * count, quarter), F32)
@@ -683,15 +680,15 @@
     def run(j):
         numbers = jnp.stack([places.number(j, label) for label in LABELS] + [expert])
         dy_blocks.append((dy_first[j], *dy_second[j]))
-        mix, seed = results[-1][2:4] if results else (None, gate_grads)
+        mix, seed = results[-1][1:3] if results else (None, gate_grads)
         results.append(
             routed(
                 numbers.astype(jnp.int32), bits, hn_blocks[j], dy_blocks[j], mix, seed, router_rows,
                 wg, wu, wd, tables,
             )
         )
-        places.after = results[-1][3]
-        kept.append(results[-1][4:6])
+        places.after = results[-1][2]
+        kept.append(results[-1][3:5])
 
     def near(j):
         hn_blocks[j] = places.spread_near(ring_blocks[j])
@@ -716,7 +713,7 @@
         return value if running is None else add(places.by_z(running), value)
 
     def grads_of(blocks, before):
-        per = 2 if ring < 8 else 4
+        per = 4
         for at in range(0, len(blocks), per):
             span = blocks[at : at + per]
             before = expert_grads(
@@ -741,38 +738,32 @@
             near(j + 2)
         if j + 1 < ring:
             far(j + 1)
-        if j == 3:
-            first = places.by_z(results[1][1])
         if j > 2:
+            places.single = "z"
             back_near(j - 2)
             back_ring(j - 2)
         if j > 1:
             back_far(j - 1)
         run(j)
     last = ring - 1
-    places.after = None
     back_far(last)
     if last > 1:
         back_near(last - 1)
         back_ring(last - 1)
-    kept[: ring // 2] = lax.optimization_barrier((kept[: ring // 2], results[last][3]))[0]
-    expert_sums = grads_of(range(ring // 2), ())
+    places.after = None
+    kept = lax.optimization_barrier((kept, results[last][2]))[0]
+    expert_sums = grads_of(range(ring), ())
     places.after = expert_sums[1]
     back_near(last)
+    back_far(0)
+    places.after = back[0]
+    back_ring(last)
     places.after = None
-    for j in range(2, last):
-        first = places.by_z(add(first, results[j][1]))
-    back_ring(last)
-    moved = first
-    back_far(0)
-    kept[ring // 2 :] = lax.optimization_barrier((kept[ring // 2 :], back[last]))[0]
-    expert_sums = grads_of(range(ring // 2, ring), expert_sums)
     back_near(0)
-    second = lax.optimization_barrier((results[-1][2], back[last]))[0]
-    second = lax.psum_scatter(second, "dp", scatter_dimension=0, tiled=True)
+    mixture = lax.optimization_barrier((results[-1][1], back[last]))[0]
     normed_grad = sum(part.astype(F32) for part in back)
     gate_grads = lax.all_to_all(
-        results[-1][3].reshape(count, half), "dp", split_axis=0, concat_axis=0, tiled=True
+        results[-1][2].reshape(count, half), "dp", split_axis=0, concat_axis=0, tiled=True
     )
     gate_grads = jnp.sum(gate_grads.reshape(experts, splits, half), axis=1).T
 
@@ -785,20 +776,15 @@
     grad_gain_two = jnp.sum(normed_grad * hidden * inverse_two, axis=0)
     hidden_grad = dy.astype(F32) + norm_back(hidden, inverse_two, gain_two, normed_grad)
     hidden_low = places.both_halves(hidden_grad.astype(BF16))
-    hidden_low = lax.optimization_barrier((hidden_low, moved, expert_sums[1]))[0]
-    moved = places.by_z(add(moved, results[last][1]))
-    first = add(moved, results[0][1])
+    mixture = lax.psum_scatter(mixture, "dp", scatter_dimension=0, tiled=True)
+    mixture = mixture.astype(F32)
     grad_out = dot(mixed_heads, hidden_low, TN).astype(BF16)
 
     grad_heads_w, part = attend_back(
         hidden_low, w_query, w_key, w_value, w_out, *around, normed, queries, keys, values, sums
     )
     grad_heads_w = places.sum_all(grad_heads_w)
-    places.after = moved
-    next(grad_heads_w)
-    places.after = None
-    first = places.collect_far(first[:half], first[half:], "xy")
-    first = places.collect_near(first, "xy")
+    begun = next(grad_heads_w)
     normed_grad_one = places.sum_halves(part)
     inverse_half = inverse_rms(inputs_half)
     grad_gain_one = jnp.sum(normed_grad_one * inputs_half * inverse_half, axis=0)
@@ -818,7 +804,6 @@
     next(grad_out)
     next(grad_heads_w)
     next(grad_out)
-    mixture = jnp.concatenate([first, second], axis=0).astype(F32)
     grad_heads_w = next(grad_heads_w).astype(F32)
     grad_out = next(grad_out).astype(F32)
     small = grad_out[:, columns:].reshape(-1)[: (experts + 2) * model].reshape(-1, model)

time: 760 us -> 732 us (0.963)
  waiting for transfers between devices: 349 us -> 318 us
  starting transfers between devices: 110 us -> 122 us
  Pallas kernels: 159 us -> 149 us
    ppermute x78 -> x73, waiting for transfers between devices: 281 us -> 241 us  [send(): got = lax.ppermute(array, 'dp', pairs)]
    all_to_all x1, waiting for transfers between devices: 26.1 us -> 0.01 us  [on_device(): lax.all_to_all(jnp.broadcast_to(bits[None], (count, half)), 'dp', split_a...]
    ppermute x12, waiting for transfers between devices: 40.5 us -> 66.6 us  [by_ring(): lax.ppermute(array, 'dp', [(i, (i + 4 * step) % self.count) for i in rang...]
    pallas_call x2 -> x1, Pallas kernels: 38.3 us -> 29.3 us  [expert_grads(): pl.pallas_call(functools.partial(expert_grads_kernel, tables, not before)...]
    ppermute x78 -> x73, starting transfers between devices: 83.3 us -> 90.4 us  [send(): got = lax.ppermute(array, 'dp', pairs)]
    convert_element_type x29 -> x24, other arithmetic: 20.5 us -> 16.4 us  [add(): return (left.astype(F32) + right.astype(F32)).astype(left.dtype)]
  transfers between devices with their start and end apart: 104 -> 99, of which waited for: 37 -> 37; matrix products, arithmetic and copies ran while one was open for 14% -> 14% of each run, Pallas kernels for 21% -> 21%
where the time goes in v3:
time: 732 us; the launch traced here: 721 us
  waiting for transfers between devices  318 us (43%)
  Pallas kernels  149 us (20%)
  starting transfers between devices  122 us (17%)
  local copies, waits for them, and re-layouts  56.9 us (8%)
  other arithmetic  53.8 us (7%)
  between operations  15.9 us (2%)
    ppermute x73, waiting for transfers between devices, send(): got = lax.ppermute(array, 'dp', pairs)  241 us
    ppermute x73, starting transfers between devices, send(): got = lax.ppermute(array, 'dp', pairs)  90.4 us
    pallas_call x4, Pallas kernels, routed(): pl.pallas_call(functools.partial(routed_kernel, tables, not mix), grid=(4...  78.7 us
    ppermute x12, waiting for transfers between devices, by_ring(): lax.ppermute(array, 'dp', [(i, (i + 4 * step) % self.count) for i in rang...  66.6 us
    pallas_call x1, Pallas kernels, expert_grads(): pl.pallas_call(functools.partial(expert_grads_kernel, tables, not before)...  29.3 us
    pallas_call x1, Pallas kernels, attend_back(): pl.pallas_call(attend_back_kernel, out_shape=[out((model, columns), BF16)...  24.4 us
    ppermute x12, starting transfers between devices, by_ring(): lax.ppermute(array, 'dp', [(i, (i + 4 * step) % self.count) for i in rang...  22.2 us
    pallas_call x1, Pallas kernels, attend(): pl.pallas_call(attend_kernel, out_shape=[out((tokens, model), BF16), out(...  17 us
  transfers between devices with their start and end apart: 99, of which 37 were waited for; matrix products, arithmetic and copies ran while one was open for 14% of the time, Pallas kernels for 21%

profile of v3, /device:TPU:0, one launch (start us, length us, event | category | flops | bytes accessed | tf_op | source)
XLA Modules:
  0.0 720.7 jit_solution(6175519680448312480)
XLA Ops:
  7.9 2.1 constant_dynamic-slice_fusion.15
  10.0 3.0 collective-permute-start.6
  15.2 5.0 all-to-all-start
  20.4 2.0 collective-permute-start.1
  22.8 9.6 %collective-permute-done.1.refs_8_.refs_26_ = bf16[128,1536]{1,0:T(8,128)(2,1)S(1)} collective-permute-done((bf16[128,1536]{1,0:T(8,128)(2,1)S(1)}, bf16[128,1536]{1,0:T(8,128)(2,1)S(1)}, u32[]{:S(2)}, u32[]{:S(2)}) %collective-permute-start.1) | collective-permute-done | bytes 393248 | tf_op jit(solution)/shard_map/ppermute | solution.py:461
  36.4 17.0 %attend.1 = (bf16[512,1536]{1,0:T(8,128)(2,1)}, bf16[512,768]{1,0:T(8,128)(2,1)}, bf16[512,256]{1,0:T(8,128)(2,1)}, bf16[512,256]{1,0:T(8,128)(2,1)}, bf16[512,7...) custom-call(bf16[512,1536]{1,0:T(8,128)(2,1)} %x.3, bf16[1,1536]{1,0:T(2,128)(2,1)} %broadcast_in_dim.87.gain, ...), custom_call_target="tpu_custom_call" | custom-call | bytes 1048576 | tf_op jit(solution)/shard_map/attend/pallas_call | solution.py:361
  61.5 14.1 %collective-permute-done.7 = bf16[128,1536]{1,0:T(8,128)(2,1)S(1)} collective-permute-done((bf16[128,1536]{1,0:T(8,128)(2,1)S(1)}, bf16[128,1536]{1,0:T(8,128)(2,1)S(1)}, u32[]{:S(2)}, u32[]{:S(2)}) %collective-permute-start.7) | collective-permute-done | bytes 393248 | tf_op jit(solution)/shard_map/ppermute | solution.py:461
  83.2 4.4 collective-permute-done.12.refs_9_.refs_27_
  89.3 5.0 collective-permute-done.22.refs_9_.refs_32_
  101.0 5.5 collective-permute-done.23.refs_9_.refs_37_
  108.1 4.5 collective-permute-done.13.refs_11_.refs_34_
  115.5 17.2 %collective-permute-done.4.refs_2_.refs_5_ = bf16[256,1536]{1,0:T(8,128)(2,1)S(1)} collective-permute-done((bf16[256,1536]{1,0:T(8,128)(2,1)S(1)}, bf16[256,1536]{1,0:T(8,128)(2,1)S(1)}, u32[]{:S(2)}, u32[]{:S(2)}) %collective-permute-start.4) | collective-permute-done | bytes 786464 | tf_op jit(solution)/shard_map/ppermute | solution.py:461
  135.6 2.0 collective-permute-start.35
  140.7 10.7 %collective-permute-done.28.refs_4_.refs_7_ = bf16[256,1536]{1,0:T(8,128)(2,1)S(1)} collective-permute-done((bf16[256,1536]{1,0:T(8,128)(2,1)}, bf16[256,1536]{1,0:T(8,128)(2,1)S(1)}, u32[]{:S(2)}, u32[]{:S(2)}) %collective-permute-start.28) | collective-permute-done | bytes 786464 | tf_op jit(solution)/shard_map/ppermute | solution.py:461
  152.9 4.8 collective-permute-done.9.refs_2_.refs_10_
  158.8 2.2 collective-permute-done.19.refs_6_.refs_4_
  161.0 2.8 collective-permute-done.18.refs_5_.refs_3_
  164.4 19.7 %routed_rows.4 = (bf16[256,1536]{1,0:T(8,128)(2,1)}, bf16[256,1536]{1,0:T(8,128)(2,1)}, bf16[256,1536]{1,0:T(8,128)(2,1)}, bf16[256,1536]{1,0:T(8,128)(2,1)}, bf...) custom-call(s32[9]{0:T(128)} %stack.312.refs_0_, ...), custom_call_target="tpu_custom_call", output_to_operand_aliasing={{5}: (12, {})} | custom-call | bytes 1048576 | tf_op jit(solution)/shard_map/routed_rows/pallas_call | solution.py:190
  184.1 2.0 collective-permute-start.21
  193.1 19.0 %collective-permute-done.32.refs_6_.refs_9_ = bf16[128,1536]{1,0:T(8,128)(2,1)S(1)} collective-permute-done((bf16[128,1536]{1,0:T(8,128)(2,1)S(1)}, bf16[128,1536]{1,0:T(8,128)(2,1)S(1)}, u32[]{:S(2)}, u32[]{:S(2)}) %collective-permute-start.32) | collective-permute-done | bytes 393248 | tf_op jit(solution)/shard_map/ppermute | solution.py:461
  217.0 19.6 %routed_rows.5 = (bf16[256,1536]{1,0:T(8,128)(2,1)}, bf16[256,1536]{1,0:T(8,128)(2,1)}, bf16[256,1536]{1,0:T(8,128)(2,1)}, bf16[256,1536]{1,0:T(8,128)(2,1)}, bf...) custom-call(s32[9]{0:T(128)} %stack.321.refs_0_, ...), custom_call_target="tpu_custom_call", output_to_operand_aliasing={{5}: (12, {}), {4}: (17, {})} | custom-call | bytes 1048576 | tf_op jit(solution)/shard_map/routed_rows/pallas_call | solution.py:190
  239.9 9.6 %collective-permute-done.37.refs_5_.refs_13_ = bf16[128,1536]{1,0:T(8,128)(2,1)S(1)} collective-permute-done((bf16[128,1536]{1,0:T(8,128)(2,1)S(1)}, bf16[128,1536]{1,0:T(8,128)(2,1)S(1)}, u32[]{:S(2)}, u32[]{:S(2)}) %collective-permute-start.37) | collective-permute-done | bytes 393248 | tf_op jit(solution)/shard_map/ppermute | solution.py:461
  256.3 19.7 %routed_rows.6 = (bf16[256,1536]{1,0:T(8,128)(2,1)}, bf16[256,1536]{1,0:T(8,128)(2,1)}, bf16[256,1536]{1,0:T(8,128)(2,1)}, bf16[256,1536]{1,0:T(8,128)(2,1)}, bf...) custom-call(s32[9]{0:T(128)} %stack.330.refs_0_, ...), custom_call_target="tpu_custom_call", output_to_operand_aliasing={{5}: (12, {}), {4}: (17, {})} | custom-call | bytes 1048576 | tf_op jit(solution)/shard_map/routed_rows/pallas_call | solution.py:190
  285.6 19.6 %routed_rows.7 = (bf16[256,1536]{1,0:T(8,128)(2,1)}, bf16[256,1536]{1,0:T(8,128)(2,1)}, bf16[256,1536]{1,0:T(8,128)(2,1)}, bf16[256,1536]{1,0:T(8,128)(2,1)}, bf...) custom-call(s32[9]{0:T(128)} %stack.303.refs_0_, ...), custom_call_target="tpu_custom_call", output_to_operand_aliasing={{5}: (12, {}), {4}: (17, {})} | custom-call | bytes 1048576 | tf_op jit(solution)/shard_map/routed_rows/pallas_call | solution.py:190
  305.2 29.3 %expert_grads.1 = (f32[2,1536,512]{2,1,0:T(8,128)}, f32[512,1536]{1,0:T(8,128)}) custom-call(bf16[256,1536]{1,0:T(8,128)(2,1)} %copy-done.3, bf16[256,1536]{1,0:T(8,128)(2,1)} %copy-done.18, bf16[256,1536]{1,0:T(8,128)(2,1)} %copy-done.19, bf16[128,1536]{1,0:T(8,128)(2,1)} %collective-permute-done.18.refs_5_.refs_3_, bf16[128,1536]{1,0:T(8,128)(2,1)} %copy-done.33, ...), custom_call_target="tpu_custom_call" | custom-call | bytes 1048576 | tf_op jit(solution)/shard_map/expert_grads/pallas_call | solution.py:284
  345.4 3.8 collective-permute-done.49
  354.4 3.2 collective-permute-done.51
  357.6 5.8 collective-permute-start.52
  368.9 5.9 collective-permute-done.45
  378.1 12.2 %collective-permute-done.52 = bf16[256,1536]{1,0:T(8,128)(2,1)} collective-permute-done((bf16[256,1536]{1,0:T(8,128)(2,1)S(1)}, bf16[256,1536]{1,0:T(8,128)(2,1)}, u32[]{:S(2)}, u32[]{:S(2)}) %collective-permute-start.52) | collective-permute-done | bytes 786464 | tf_op jit(solution)/shard_map/ppermute | solution.py:461
  390.3 14.1 %collective-permute-done.55 = bf16[256,1536]{1,0:T(8,128)(2,1)} collective-permute-done((bf16[256,1536]{1,0:T(8,128)(2,1)S(1)}, bf16[256,1536]{1,0:T(8,128)(2,1)}, u32[]{:S(2)}, u32[]{:S(2)}) %collective-permute-start.55) | collective-permute-done | bytes 786464 | tf_op jit(solution)/shard_map/ppermute | solution.py:461
  407.2 3.7 all-to-all-start.1
  411.1 7.1 all-to-all-done.1
  421.2 6.0 collective-permute-done.58
  427.3 2.7 multiply_reduce_fusion
  431.6 2.1 collective-permute-done.59
  439.5 24.4 %attend_back.1 = (bf16[1536,1280]{1,0:T(8,128)(2,1)}, bf16[512,1536]{1,0:T(8,128)(2,1)}) custom-call(bf16[512,1536]{1,0:T(8,128)(2,1)} %copy-done.13, bf16[1536,768]{1,0:T(8,128)(2,1)} %wq.3, bf16[1536,256]{1,0:T(8,128)(2,1)} %wk.3, bf16[1536,256]{1,0:T(8,128)(2,1)} %wv.3, bf16[768,1536]{1,0:T(8,128)(2,1)} %wo.3, f32[512,128]{1,0:T(8,128)} %get-tuple-element.309.cosine, ...), custom_call_target="tpu_custom_call" | custom-call | bytes 1048576 | tf_op jit(solution)/shard_map/attend_back/pallas_call | solution.py:428
  465.1 2.6 fusion.56
  473.2 26.1 %collective-permute-done.78 = bf16[4,2,96,640]{3,2,1,0:T(8,128)(2,1)S(1)} collective-permute-done((bf16[4,2,96,640]{3,2,1,0:T(8,128)(2,1)S(1)}, bf16[4,2,96,640]{3,2,1,0:T(8,128)(2,1)S(1)}, u32[]{:S(2)}, u32[]{:S(2)}) %collective-permute-start.78) | collective-permute-done | bytes 983072 | tf_op jit(solution)/shard_map/ppermute | solution.py:461
  510.9 9.9 %collective-permute-done.79 = bf16[4,96,640]{2,1,0:T(8,128)(2,1)} collective-permute-done((bf16[4,96,640]{2,1,0:T(8,128)(2,1)}, bf16[4,96,640]{2,1,0:T(8,128)(2,1)}, u32[]{:S(2)}, u32[]{:S(2)}) %collective-permute-start.79) | collective-permute-done | bytes 491552 | tf_op jit(solution)/shard_map/ppermute | solution.py:461
  523.4 1.9 collective-permute-start.81
  527.4 14.8 %collective-permute-done.64 = bf16[4,2,48,896]{3,2,1,0:T(8,128)(2,1)S(1)} collective-permute-done((bf16[4,2,48,896]{3,2,1,0:T(8,128)(2,1)S(1)}, bf16[4,2,48,896]{3,2,1,0:T(8,128)(2,1)S(1)}, u32[]{:S(2)}, u32[]{:S(2)}) %collective-permute-start.64) | collective-permute-done | bytes 688160 | tf_op jit(solution)/shard_map/ppermute | solution.py:461
  546.4 2.4 collective-permute-start.85
  548.8 1.9 collective-permute-start.84
  554.8 5.0 collective-permute-start.69
  559.8 25.6 %collective-permute-done.85 = bf16[96,1280]{1,0:T(8,128)(2,1)S(1)} collective-permute-done((bf16[96,1280]{1,0:T(8,128)(2,1)S(1)}, bf16[96,1280]{1,0:T(8,128)(2,1)S(1)}, u32[]{:S(2)}, u32[]{:S(2)}) %collective-permute-start.85) | collective-permute-done | bytes 245792 | tf_op jit(solution)/shard_map/ppermute | solution.py:477
  585.8 29.3 %collective-permute-done.68 = bf16[48,1792]{1,0:T(8,128)(2,1)S(1)} collective-permute-done((bf16[48,1792]{1,0:T(8,128)(2,1)S(1)}, bf16[48,1792]{1,0:T(8,128)(2,1)S(1)}, u32[]{:S(2)}, u32[]{:S(2)}) %collective-permute-start.68) | collective-permute-done | bytes 172064 | tf_op jit(solution)/shard_map/ppermute | solution.py:477
  615.3 4.7 collective-permute-start.71
  620.0 1.9 collective-permute-start.70
  622.2 2.0 collective-permute-start.87
  625.1 10.5 %collective-permute-done.71 = bf16[48,1792]{1,0:T(8,128)(2,1)S(1)} collective-permute-done((bf16[48,1792]{1,0:T(8,128)(2,1)S(1)}, bf16[48,1792]{1,0:T(8,128)(2,1)S(1)}, u32[]{:S(2)}, u32[]{:S(2)}) %collective-permute-start.71) | collective-permute-done | bytes 172064 | tf_op jit(solution)/shard_map/ppermute | solution.py:477
  636.0 2.0 collective-permute-start.73
  640.5 12.7 %collective-permute-done.74 = bf16[4,48,896]{2,1,0:T(8,128)(2,1)S(1)} collective-permute-done((bf16[4,48,896]{2,1,0:T(8,128)(2,1)S(1)}, bf16[4,48,896]{2,1,0:T(8,128)(2,1)S(1)}, u32[]{:S(2)}, u32[]{:S(2)}) %collective-permute-start.74) | collective-permute-done | bytes 344096 | tf_op jit(solution)/shard_map/ppermute | solution.py:461
  653.8 2.5 collective-permute-start.75
  661.2 10.5 %collective-permute-done.76 = bf16[4,2,48,896]{3,2,0,1:T(8,128)(2,1)S(1)} collective-permute-done((bf16[4,2,48,896]{3,2,0,1:T(8,128)(2,1)S(1)}, bf16[4,2,48,896]{3,2,0,1:T(8,128)(2,1)S(1)}, u32[]{:S(2)}, u32[]{:S(2)}) %collective-permute-start.76) | collective-permute-done | bytes 688160 | tf_op jit(solution)/shard_map/ppermute | solution.py:461
  676.0 2.0 maximum_convert_fusion.1
  678.1 2.8 slice.241
  680.9 6.5 collective-permute-done.90
  690.7 2.0 maximum_select_fusion
  694.2 2.5 slice.240
  696.7 4.6 fusion.6
  703.8 3.7 slice_bitcast_fusion
  707.5 3.0 maximum_select_fusion.4
  710.5 2.9 maximum_select_fusion.2
  (441 shorter events, 166.9 us)
Async XLA Ops:
  7.2 151.6 %all-gather.4.cloned.1.call-start = ((), (), s32[]{:S(2)}) async-start(), calls=%async_computation.5 | async-start | bytes 2359296 | tf_op jit(solution)/shard_map/all_gather | solution.py:638
  10.0 45.9 %collective-permute-start.6 = (bf16[256,1536]{1,0:T(8,128)(2,1)}, bf16[256,1536]{1,0:T(8,128)(2,1)S(1)}, u32[]{:S(2)}, u32[]{:S(2)}) collective-permute-start(bf16[256,1536]{1,0:T(8,128)(2,1)} %constant_dynamic-slice_fusion.15), channel_id=1, source_target_pairs={{0,4},{2,6},{4,0},{6,2},{8,12},{10,14},{12,8},{14,10},{16,20},{18,... | collective-permute-start | bytes 2359304 | tf_op jit(solution)/shard_map/ppermute | solution.py:461
  13.0 44.4 %collective-permute-start.5 = (bf16[256,1536]{1,0:T(8,128)(2,1)}, bf16[256,1536]{1,0:T(8,128)(2,1)}, u32[]{:S(2)}, u32[]{:S(2)}) collective-permute-start(bf16[256,1536]{1,0:T(8,128)(2,1)} %constant_dynamic-slice_fusion.15), channel_id=1, source_target_pairs={{0,2},{2,0},{4,6},{6,4},{8,10},{10,8},{12,14},{14,12},{16,18},{18,... | collective-permute-start | bytes 2359304 | tf_op jit(solution)/shard_map/ppermute | solution.py:461
  15.2 38.1 %all-to-all-start = ((s32[16,1,256]{2,1,0:T(1,128)}), s32[16,1,256]{2,1,0:T(1,128)S(1)}, u32[]{:S(2)}, u32[]{:S(2)}) async-start(s32[16,1,256]{2,1,0:T(1,128)} %broadcast_in_dim.97), calls=%async_computation | async-start | bytes 32768 | tf_op jit(solution)/shard_map/all_to_all | solution.py:648
  20.2 138.6 %all-gather.6.cloned.1.call-start = ((), (), s32[]{:S(2)}) async-start(), calls=%async_computation.6 | async-start | bytes 2359296 | tf_op jit(solution)/shard_map/all_gather | solution.py:639
  22.4 136.5 %all-gather.8.cloned.1.call-start = ((), (), s32[]{:S(2)}) async-start(), calls=%async_computation.7 | async-start | bytes 2359296 | tf_op jit(solution)/shard_map/all_gather | solution.py:640
  32.5 22.2 %collective-permute-start.2 = (bf16[128,1536]{1,0:T(8,128)(2,1)S(1)}, bf16[128,1536]{1,0:T(8,128)(2,1)}, u32[]{:S(2)}, u32[]{:S(2)}) collective-permute-start(bf16[128,1536]{1,0:T(8,128)(2,1)S(1)} %collective-permute-done.1.refs_8_.refs_26_), channel_id=1, source_target_pairs={{0,8},{2,10},{4,12},{6,14},{8,16},{10,18},{12,20},{14,22},{16,24},... | collective-permute-start | bytes 1179656 | tf_op jit(solution)/shard_map/ppermute | solution.py:461
  54.5 23.7 %collective-permute-start = (bf16[256,1536]{1,0:T(8,128)(2,1)S(1)}, bf16[256,1536]{1,0:T(8,128)(2,1)S(1)}, u32[]{:S(2)}, u32[]{:S(2)}) collective-permute-start(bf16[256,1536]{1,0:T(8,128)(2,1)S(1)} %constant_dynamic-slice_fusion.16), channel_id=1, source_target_pairs={{0,1},{1,0},{2,3},{3,2},{4,5},{5,4},{6,7},{7,6},{8,9},{9,8},{10,11... | collective-permute-start | bytes 2359304 | tf_op jit(solution)/shard_map/ppermute | solution.py:482
  54.6 34.6 %collective-permute-start.3 = (bf16[128,1536]{1,0:T(8,128)(2,1)}, bf16[128,1536]{1,0:T(8,128)(2,1)}, u32[]{:S(2)}, u32[]{:S(2)}) collective-permute-start(bf16[128,1536]{1,0:T(8,128)(2,1)} %collective-permute-done.2.refs_8_.refs_31_), channel_id=1, source_target_pairs={{0,8},{2,10},{4,12},{6,14},{8,16},{10,18},{12,20},{14,22},{16,24},... | collective-permute-start | bytes 1179656 | tf_op jit(solution)/shard_map/ppermute | solution.py:461
  55.9 25.1 %collective-permute-start.10 = (bf16[128,1536]{1,0:T(8,128)(2,1)S(1)}, bf16[128,1536]{1,0:T(8,128)(2,1)S(1)}, u32[]{:S(2)}, u32[]{:S(2)}) collective-permute-start(bf16[128,1536]{1,0:T(8,128)(2,1)S(1)} %collective-permute-done.1.refs_8_.refs_26_), channel_id=1, source_target_pairs={{0,4},{2,6},{4,0},{6,2},{8,12},{10,14},{12,8},{14,10},{16,20},{18,... | collective-permute-start | bytes 1179656 | tf_op jit(solution)/shard_map/ppermute | solution.py:461
  59.9 22.7 %collective-permute-start.20 = (bf16[128,1536]{1,0:T(8,128)(2,1)S(1)}, bf16[128,1536]{1,0:T(8,128)(2,1)S(1)}, u32[]{:S(2)}, u32[]{:S(2)}) collective-permute-start(bf16[128,1536]{1,0:T(8,128)(2,1)S(1)} %get-tuple-element.291.refs_10_.refs_23_), channel_id=1, source_target_pairs={{0,2},{2,0},{4,6},{6,4},{8,10},{10,8},{12,14},{14,12},{16,18},{18,... | collective-permute-start | bytes 1179656 | tf_op jit(solution)/shard_map/ppermute | solution.py:461
  78.3 56.8 %collective-permute-start.8 = (bf16[512,1536]{1,0:T(8,128)(2,1)}, bf16[512,1536]{1,0:T(8,128)(2,1)}, u32[]{:S(2)}, u32[]{:S(2)}) collective-permute-start(bf16[512,1536]{1,0:T(8,128)(2,1)} %pad_maximum_fusion.refs_7_.refs_20_), channel_id=1, source_target_pairs={{0,8},{2,10},{4,12},{6,14},{8,16},{10,18},{12,20},{14,22},{16,24},... | collective-permute-start | bytes 4718600 | tf_op jit(solution)/shard_map/ppermute | solution.py:461
  95.8 36.9 %collective-permute-start.4 = (bf16[256,1536]{1,0:T(8,128)(2,1)S(1)}, bf16[256,1536]{1,0:T(8,128)(2,1)S(1)}, u32[]{:S(2)}, u32[]{:S(2)}) collective-permute-start(bf16[256,1536]{1,0:T(8,128)(2,1)S(1)} %multiply_convert_fusion.refs_2_.refs_0_), channel_id=1, source_target_pairs={{0,8},{2,10},{4,12},{6,14},{8,16},{10,18},{12,20},{14,22},{16,24},... | collective-permute-start | bytes 2359304 | tf_op jit(solution)/shard_map/ppermute | solution.py:461
  106.6 27.0 %collective-permute-start.27 = (bf16[128,1536]{1,0:T(8,128)(2,1)S(1)}, bf16[128,1536]{1,0:T(8,128)(2,1)}, u32[]{:S(2)}, u32[]{:S(2)}) collective-permute-start(bf16[128,1536]{1,0:T(8,128)(2,1)S(1)} %collective-permute-done.23.refs_9_.refs_37_), channel_id=1, source_target_pairs={{0,4},{2,6},{4,0},{6,2},{8,12},{10,14},{12,8},{14,10},{16,20},{18,... | collective-permute-start | bytes 1179656 | tf_op jit(solution)/shard_map/ppermute | solution.py:461
  108.1 588.7 %reduce-scatter.4.cloned.1.call-start = ((), (), s32[]{:S(2)}) async-start(), calls=%async_computation.8 | async-start | bytes 13369344 | tf_op jit(solution)/shard_map/reduce_scatter | solution.py:779
  112.6 23.1 %collective-permute-start.14 = (bf16[256,1536]{1,0:T(8,128)(2,1)S(1)}, bf16[256,1536]{1,0:T(8,128)(2,1)S(1)}, u32[]{:S(2)}, u32[]{:S(2)}) collective-permute-start(bf16[256,1536]{1,0:T(8,128)(2,1)S(1)} %multiply_convert_fusion.refs_2_.refs_0_), channel_id=1, source_target_pairs={{0,2},{2,0},{4,6},{6,4},{8,10},{10,8},{12,14},{14,12},{16,18},{18,... | collective-permute-start | bytes 2359304 | tf_op jit(solution)/shard_map/ppermute | solution.py:461
  114.1 24.4 %collective-permute-start.17 = (bf16[256,1536]{1,0:T(8,128)(2,1)S(1)}, bf16[256,1536]{1,0:T(8,128)(2,1)S(1)}, u32[]{:S(2)}, u32[]{:S(2)}) collective-permute-start(bf16[256,1536]{1,0:T(8,128)(2,1)S(1)} %multiply_convert_fusion.refs_2_.refs_0_), channel_id=1, source_target_pairs={{0,4},{2,6},{4,0},{6,2},{8,12},{10,14},{12,8},{14,10},{16,20},{18,... | collective-permute-start | bytes 2359304 | tf_op jit(solution)/shard_map/ppermute | solution.py:461
  135.1 22.6 %collective-permute-start.9 = (bf16[256,1536]{1,0:T(8,128)(2,1)}, bf16[256,1536]{1,0:T(8,128)(2,1)}, u32[]{:S(2)}, u32[]{:S(2)}) collective-permute-start(bf16[256,1536]{1,0:T(8,128)(2,1)} %copy-done.26), channel_id=1, source_target_pairs={{0,8},{2,10},{4,12},{6,14},{8,16},{10,18},{12,20},{14,22},{16,24},... | collective-permute-start | bytes 2359304 | tf_op jit(solution)/shard_map/ppermute | solution.py:461
  135.1 51.0 %collective-permute-start.24 = (bf16[256,1536]{1,0:T(8,128)(2,1)}, bf16[256,1536]{1,0:T(8,128)(2,1)}, u32[]{:S(2)}, u32[]{:S(2)}) collective-permute-start(bf16[256,1536]{1,0:T(8,128)(2,1)} %copy-done.26), channel_id=1, source_target_pairs={{0,2},{2,0},{4,6},{6,4},{8,10},{10,8},{12,14},{14,12},{16,18},{18,... | collective-permute-start | bytes 2359304 | tf_op jit(solution)/shard_map/ppermute | solution.py:461
  135.6 80.6 %collective-permute-start.35 = (bf16[512,1536]{1,0:T(8,128)(2,1)}, bf16[512,1536]{1,0:T(8,128)(2,1)}, u32[]{:S(2)}, u32[]{:S(2)}) collective-permute-start(bf16[512,1536]{1,0:T(8,128)(2,1)} %collective-permute-done.8.refs_7_.refs_25_), channel_id=1, source_target_pairs={{0,8},{2,10},{4,12},{6,14},{8,16},{10,18},{12,20},{14,22},{16,24},... | collective-permute-start | bytes 4718600 | tf_op jit(solution)/shard_map/ppermute | solution.py:461
  139.3 21.7 %collective-permute-start.19 = (bf16[128,1536]{1,0:T(8,128)(2,1)}, bf16[128,1536]{1,0:T(8,128)(2,1)S(1)}, u32[]{:S(2)}, u32[]{:S(2)}) collective-permute-start(bf16[128,1536]{1,0:T(8,128)(2,1)} %slice.208), channel_id=1, source_target_pairs={{0,2},{2,0},{4,6},{6,4},{8,10},{10,8},{12,14},{14,12},{16,18},{18,... | collective-permute-start | bytes 1179656 | tf_op jit(solution)/shard_map/ppermute | solution.py:461
  157.7 32.3 %collective-permute-start.29 = (bf16[256,1536]{1,0:T(8,128)(2,1)}, bf16[256,1536]{1,0:T(8,128)(2,1)}, u32[]{:S(2)}, u32[]{:S(2)}) collective-permute-start(bf16[256,1536]{1,0:T(8,128)(2,1)} %collective-permute-done.9.refs_2_.refs_10_), channel_id=1, source_target_pairs={{0,4},{2,6},{4,0},{6,2},{8,12},{10,14},{12,8},{14,10},{16,20},{18,... | collective-permute-start | bytes 2359304 | tf_op jit(solution)/shard_map/ppermute | solution.py:461
  184.1 28.9 %collective-permute-start.21 = (bf16[256,1536]{1,0:T(8,128)(2,1)}, bf16[256,1536]{1,0:T(8,128)(2,1)}, u32[]{:S(2)}, u32[]{:S(2)}) collective-permute-start(bf16[256,1536]{1,0:T(8,128)(2,1)} %collective-permute-done.9.refs_2_.refs_10_), channel_id=1, source_target_pairs={{0,8},{2,10},{4,12},{6,14},{8,16},{10,18},{12,20},{14,22},{16,24},... | collective-permute-start | bytes 2359304 | tf_op jit(solution)/shard_map/ppermute | solution.py:461
  186.1 27.0 %collective-permute-start.25 = (bf16[256,1536]{1,0:T(8,128)(2,1)}, bf16[256,1536]{1,0:T(8,128)(2,1)S(1)}, u32[]{:S(2)}, u32[]{:S(2)}) collective-permute-start(bf16[256,1536]{1,0:T(8,128)(2,1)} %collective-permute-done.9.refs_2_.refs_10_), channel_id=1, source_target_pairs={{0,2},{2,0},{4,6},{6,4},{8,10},{10,8},{12,14},{14,12},{16,18},{18,... | collective-permute-start | bytes 2359304 | tf_op jit(solution)/shard_map/ppermute | solution.py:461
  186.4 25.7 %collective-permute-start.32 = (bf16[128,1536]{1,0:T(8,128)(2,1)S(1)}, bf16[128,1536]{1,0:T(8,128)(2,1)S(1)}, u32[]{:S(2)}, u32[]{:S(2)}) collective-permute-start(bf16[128,1536]{1,0:T(8,128)(2,1)S(1)} %slice.213), channel_id=1, source_target_pairs={{0,2},{2,0},{4,6},{6,4},{8,10},{10,8},{12,14},{14,12},{16,18},{18,... | collective-permute-start | bytes 1179656 | tf_op jit(solution)/shard_map/ppermute | solution.py:461
  190.0 26.3 %collective-permute-start.31 = (bf16[128,1536]{1,0:T(8,128)(2,1)}, bf16[128,1536]{1,0:T(8,128)(2,1)S(1)}, u32[]{:S(2)}, u32[]{:S(2)}) collective-permute-start(bf16[128,1536]{1,0:T(8,128)(2,1)} %slice.212), channel_id=1, source_target_pairs={{0,4},{2,6},{4,0},{6,2},{8,12},{10,14},{12,8},{14,10},{16,20},{18,... | collective-permute-start | bytes 1179656 | tf_op jit(solution)/shard_map/ppermute | solution.py:461
  212.1 24.5 %collective-permute-start.38 = (bf16[128,1536]{1,0:T(8,128)(2,1)}, bf16[128,1536]{1,0:T(8,128)(2,1)S(1)}, u32[]{:S(2)}, u32[]{:S(2)}) collective-permute-start(bf16[128,1536]{1,0:T(8,128)(2,1)} %slice.216), channel_id=1, source_target_pairs={{0,2},{2,0},{4,6},{6,4},{8,10},{10,8},{12,14},{14,12},{16,18},{18,... | collective-permute-start | bytes 1179656 | tf_op jit(solution)/shard_map/ppermute | solution.py:461
  213.0 39.4 %collective-permute-start.26 = (bf16[256,1536]{1,0:T(8,128)(2,1)}, bf16[256,1536]{1,0:T(8,128)(2,1)}, u32[]{:S(2)}, u32[]{:S(2)}) collective-permute-start(bf16[256,1536]{1,0:T(8,128)(2,1)} %collective-permute-done.21.refs_2_.refs_15_), channel_id=1, source_target_pairs={{0,2},{2,0},{4,6},{6,4},{8,10},{10,8},{12,14},{14,12},{16,18},{18,... | collective-permute-start | bytes 2359304 | tf_op jit(solution)/shard_map/ppermute | solution.py:461
  214.8 36.7 %collective-permute-start.30 = (bf16[256,1536]{1,0:T(8,128)(2,1)}, bf16[256,1536]{1,0:T(8,128)(2,1)}, u32[]{:S(2)}, u32[]{:S(2)}) collective-permute-start(bf16[256,1536]{1,0:T(8,128)(2,1)} %collective-permute-done.21.refs_2_.refs_15_), channel_id=1, source_target_pairs={{0,4},{2,6},{4,0},{6,2},{8,12},{10,14},{12,8},{14,10},{16,20},{18,... | collective-permute-start | bytes 2359304 | tf_op jit(solution)/shard_map/ppermute | solution.py:461
  236.7 40.7 %collective-permute-start.39 = (bf16[256,1536]{1,0:T(8,128)(2,1)}, bf16[256,1536]{1,0:T(8,128)(2,1)}, u32[]{:S(2)}, u32[]{:S(2)}) collective-permute-start(bf16[256,1536]{1,0:T(8,128)(2,1)} %get-tuple-element.179), channel_id=1, source_target_pairs={{0,2},{2,0},{4,6},{6,4},{8,10},{10,8},{12,14},{14,12},{16,18},{18,... | collective-permute-start | bytes 2359304 | tf_op jit(solution)/shard_map/ppermute | solution.py:461
  238.0 46.4 %collective-permute-start.36 = (bf16[512,1536]{1,0:T(8,128)(2,1)}, bf16[512,1536]{1,0:T(8,128)(2,1)S(1)}, u32[]{:S(2)}, u32[]{:S(2)}) collective-permute-start(bf16[512,1536]{1,0:T(8,128)(2,1)} %collective-permute-done.35.refs_7_.refs_30_), channel_id=1, source_target_pairs={{0,8},{2,10},{4,12},{6,14},{8,16},{10,18},{12,20},{14,22},{16,24},... | collective-permute-start | bytes 4718600 | tf_op jit(solution)/shard_map/ppermute | solution.py:461
  249.4 30.8 %collective-permute-start.42 = (bf16[256,1536]{1,0:T(8,128)(2,1)}, bf16[256,1536]{1,0:T(8,128)(2,1)}, u32[]{:S(2)}, u32[]{:S(2)}) collective-permute-start(bf16[256,1536]{1,0:T(8,128)(2,1)} %get-tuple-element.186), channel_id=1, source_target_pairs={{0,4},{2,6},{4,0},{6,2},{8,12},{10,14},{12,8},{14,10},{16,20},{18,... | collective-permute-start | bytes 2359304 | tf_op jit(solution)/shard_map/ppermute | solution.py:461
  253.5 25.3 %collective-permute-start.33 = (bf16[128,1536]{1,0:T(8,128)(2,1)S(1)}, bf16[128,1536]{1,0:T(8,128)(2,1)S(1)}, u32[]{:S(2)}, u32[]{:S(2)}) collective-permute-start(bf16[128,1536]{1,0:T(8,128)(2,1)S(1)} %slice.211), channel_id=1, source_target_pairs={{0,4},{2,6},{4,0},{6,2},{8,12},{10,14},{12,8},{14,10},{16,20},{18,... | collective-permute-start | bytes 1179656 | tf_op jit(solution)/shard_map/ppermute | solution.py:461
  255.0 26.7 %collective-permute-start.34 = (bf16[128,1536]{1,0:T(8,128)(2,1)S(1)}, bf16[128,1536]{1,0:T(8,128)(2,1)S(1)}, u32[]{:S(2)}, u32[]{:S(2)}) collective-permute-start(bf16[128,1536]{1,0:T(8,128)(2,1)S(1)} %slice.214), channel_id=1, source_target_pairs={{0,2},{2,0},{4,6},{6,4},{8,10},{10,8},{12,14},{14,12},{16,18},{18,... | collective-permute-start | bytes 1179656 | tf_op jit(solution)/shard_map/ppermute | solution.py:461
  278.8 55.7 %collective-permute-start.40 = (bf16[128,1536]{1,0:T(8,128)(2,1)S(1)}, bf16[128,1536]{1,0:T(8,128)(2,1)}, u32[]{:S(2)}, u32[]{:S(2)}) collective-permute-start(bf16[128,1536]{1,0:T(8,128)(2,1)S(1)} %slice.217), channel_id=1, source_target_pairs={{0,4},{2,6},{4,0},{6,2},{8,12},{10,14},{12,8},{14,10},{16,20},{18,... | collective-permute-start | bytes 1179656 | tf_op jit(solution)/shard_map/ppermute | solution.py:461
  279.5 56.2 %collective-permute-start.48 = (bf16[256,1536]{1,0:T(8,128)(2,1)}, bf16[256,1536]{1,0:T(8,128)(2,1)S(1)}, u32[]{:S(2)}, u32[]{:S(2)}) collective-permute-start(bf16[256,1536]{1,0:T(8,128)(2,1)} %get-tuple-element.213), channel_id=1, source_target_pairs={{0,2},{2,0},{4,6},{6,4},{8,10},{10,8},{12,14},{14,12},{16,18},{18,... | collective-permute-start | bytes 2359304 | tf_op jit(solution)/shard_map/ppermute | solution.py:461
  281.7 56.9 %collective-permute-start.43 = (bf16[128,1536]{1,0:T(8,128)(2,1)S(1)}, bf16[128,1536]{1,0:T(8,128)(2,1)}, u32[]{:S(2)}, u32[]{:S(2)}) collective-permute-start(bf16[128,1536]{1,0:T(8,128)(2,1)S(1)} %slice.220), channel_id=1, source_target_pairs={{0,2},{2,0},{4,6},{6,4},{8,10},{10,8},{12,14},{14,12},{16,18},{18,... | collective-permute-start | bytes 1179656 | tf_op jit(solution)/shard_map/ppermute | solution.py:461
  283.0 53.0 %collective-permute-start.47 = (bf16[256,1536]{1,0:T(8,128)(2,1)}, bf16[256,1536]{1,0:T(8,128)(2,1)S(1)}, u32[]{:S(2)}, u32[]{:S(2)}) collective-permute-start(bf16[256,1536]{1,0:T(8,128)(2,1)} %get-tuple-element.211), channel_id=1, source_target_pairs={{0,4},{2,6},{4,0},{6,2},{8,12},{10,14},{12,8},{14,10},{16,20},{18,... | collective-permute-start | bytes 2359304 | tf_op jit(solution)/shard_map/ppermute | solution.py:461
  342.5 22.3 %collective-permute-start.44 = (bf16[256,1536]{1,0:T(8,128)(2,1)}, bf16[256,1536]{1,0:T(8,128)(2,1)}, u32[]{:S(2)}, u32[]{:S(2)}) collective-permute-start(bf16[256,1536]{1,0:T(8,128)(2,1)} %get-tuple-element.188), channel_id=1, source_target_pairs={{0,2},{2,0},{4,6},{6,4},{8,10},{10,8},{12,14},{14,12},{16,18},{18,... | collective-permute-start | bytes 2359304 | tf_op jit(solution)/shard_map/ppermute | solution.py:461
  344.0 19.4 %collective-permute-start.41 = (bf16[256,1536]{1,0:T(8,128)(2,1)}, bf16[256,1536]{1,0:T(8,128)(2,1)}, u32[]{:S(2)}, u32[]{:S(2)}) collective-permute-start(bf16[256,1536]{1,0:T(8,128)(2,1)} %get-tuple-element.182), channel_id=1, source_target_pairs={{0,4},{2,6},{4,0},{6,2},{8,12},{10,14},{12,8},{14,10},{16,20},{18,... | collective-permute-start | bytes 2359304 | tf_op jit(solution)/shard_map/ppermute | solution.py:461
  350.1 25.8 %collective-permute-start.53 = (bf16[256,1536]{1,0:T(8,128)(2,1)}, bf16[256,1536]{1,0:T(8,128)(2,1)S(1)}, u32[]{:S(2)}, u32[]{:S(2)}) collective-permute-start(bf16[256,1536]{1,0:T(8,128)(2,1)} %get-tuple-element.221), channel_id=1, source_target_pairs={{0,4},{2,6},{4,0},{6,2},{8,12},{10,14},{12,8},{14,10},{16,20},{18,... | collective-permute-start | bytes 2359304 | tf_op jit(solution)/shard_map/ppermute | solution.py:461
  350.8 25.5 %collective-permute-start.54 = (bf16[256,1536]{1,0:T(8,128)(2,1)}, bf16[256,1536]{1,0:T(8,128)(2,1)S(1)}, u32[]{:S(2)}, u32[]{:S(2)}) collective-permute-start(bf16[256,1536]{1,0:T(8,128)(2,1)} %get-tuple-element.224), channel_id=1, source_target_pairs={{0,2},{2,0},{4,6},{6,4},{8,10},{10,8},{12,14},{14,12},{16,18},{18,... | collective-permute-start | bytes 2359304 | tf_op jit(solution)/shard_map/ppermute | solution.py:461
  357.6 32.7 %collective-permute-start.52 = (bf16[256,1536]{1,0:T(8,128)(2,1)S(1)}, bf16[256,1536]{1,0:T(8,128)(2,1)}, u32[]{:S(2)}, u32[]{:S(2)}) collective-permute-start(bf16[256,1536]{1,0:T(8,128)(2,1)S(1)} %pad_maximum_fusion.4), channel_id=1, source_target_pairs={{0,16},{2,18},{4,20},{6,22},{8,24},{10,26},{12,28},{14,30},{16,0},... | collective-permute-start | bytes 2359304 | tf_op jit(solution)/shard_map/ppermute | solution.py:461
  404.4 299.4 %reduce-scatter.6.cloned.1.call-start = ((), (), s32[]{:S(2)}) async-start(), calls=%async_computation.9 | async-start | bytes 9437184 | tf_op jit(solution)/shard_map/reduce_scatter | solution.py:813
  410.9 302.5 %reduce-scatter.8.cloned.1.call-start = ((), (), s32[]{:S(2)}) async-start(), calls=%async_computation.10 | async-start | bytes 4718592 | tf_op jit(solution)/shard_map/reduce_scatter | solution.py:814
  438.4 31.8 %collective-permute-start.62 = (bf16[4,2,48,896]{3,2,0,1:T(8,128)(2,1)S(1)}, bf16[4,2,48,896]{3,2,0,1:T(8,128)(2,1)S(1)}, u32[]{:S(2)}, u32[]{:S(2)}) collective-permute-start(bf16[4,2,48,896]{3,2,0,1:T(8,128)(2,1)S(1)} %bitcast.213), channel_id=1, source_target_pairs={{0,2},{2,0},{4,6},{6,4},{8,10},{10,8},{12,14},{14,12},{16,18},{18,... | collective-permute-start | bytes 2064392 | tf_op jit(solution)/shard_map/ppermute | solution.py:461
  467.9 31.4 %collective-permute-start.78 = (bf16[4,2,96,640]{3,2,1,0:T(8,128)(2,1)S(1)}, bf16[4,2,96,640]{3,2,1,0:T(8,128)(2,1)S(1)}, u32[]{:S(2)}, u32[]{:S(2)}) collective-permute-start(bf16[4,2,96,640]{3,2,1,0:T(8,128)(2,1)S(1)} %dynamic-slice_bitcast_fusion), channel_id=1, source_target_pairs={{0,4},{2,6},{4,0},{6,2},{8,12},{10,14},{12,8},{14,10},{16,20},{18,... | collective-permute-start | bytes 2949128 | tf_op jit(solution)/shard_map/ppermute | solution.py:461
  469.4 31.0 %collective-permute-start.77 = (bf16[4,2,96,640]{3,2,0,1:T(8,128)(2,1)S(1)}, bf16[4,2,96,640]{3,2,0,1:T(8,128)(2,1)S(1)}, u32[]{:S(2)}, u32[]{:S(2)}) collective-permute-start(bf16[4,2,96,640]{3,2,0,1:T(8,128)(2,1)S(1)} %bitcast.211), channel_id=1, source_target_pairs={{0,2},{2,0},{4,6},{6,4},{8,10},{10,8},{12,14},{14,12},{16,18},{18,... | collective-permute-start | bytes 2949128 | tf_op jit(solution)/shard_map/ppermute | solution.py:461
  473.1 29.6 %collective-permute-start.63 = (f32[18,1536]{1,0:T(8,128)S(1)}, f32[18,1536]{1,0:T(8,128)S(1)}, u32[]{:S(2)}, u32[]{:S(2)}) collective-permute-start(f32[18,1536]{1,0:T(8,128)S(1)} %pad_maximum_fusion.8), channel_id=1, source_target_pairs={{0,1},{1,0},{2,3},{3,2},{4,5},{5,4},{6,7},{7,6},{8,9},{9,8},{10,11... | collective-permute-start | bytes 331784 | tf_op jit(solution)/shard_map/ppermute | solution.py:482
  501.4 19.4 %collective-permute-start.79 = (bf16[4,96,640]{2,1,0:T(8,128)(2,1)}, bf16[4,96,640]{2,1,0:T(8,128)(2,1)}, u32[]{:S(2)}, u32[]{:S(2)}) collective-permute-start(bf16[4,96,640]{2,1,0:T(8,128)(2,1)} %dynamic-slice_bitcast_fusion.2), channel_id=1, source_target_pairs={{0,4},{2,6},{4,0},{6,2},{8,12},{10,14},{12,8},{14,10},{16,20},{18,... | collective-permute-start | bytes 1474568 | tf_op jit(solution)/shard_map/ppermute | solution.py:461
  502.0 20.0 %collective-permute-start.80 = (bf16[4,96,640]{2,1,0:T(8,128)(2,1)}, bf16[4,96,640]{2,1,0:T(8,128)(2,1)}, u32[]{:S(2)}, u32[]{:S(2)}) collective-permute-start(bf16[4,96,640]{2,1,0:T(8,128)(2,1)} %dynamic-slice_bitcast_fusion.1), channel_id=1, source_target_pairs={{0,2},{2,0},{4,6},{6,4},{8,10},{10,8},{12,14},{14,12},{16,18},{18,... | collective-permute-start | bytes 1474568 | tf_op jit(solution)/shard_map/ppermute | solution.py:461
  509.5 32.6 %collective-permute-start.64 = (bf16[4,2,48,896]{3,2,1,0:T(8,128)(2,1)S(1)}, bf16[4,2,48,896]{3,2,1,0:T(8,128)(2,1)S(1)}, u32[]{:S(2)}, u32[]{:S(2)}) collective-permute-start(bf16[4,2,48,896]{3,2,1,0:T(8,128)(2,1)S(1)} %fusion.17), channel_id=1, source_target_pairs={{0,4},{2,6},{4,0},{6,2},{8,12},{10,14},{12,8},{14,10},{16,20},{18,... | collective-permute-start | bytes 2064392 | tf_op jit(solution)/shard_map/ppermute | solution.py:461
  523.4 21.2 %collective-permute-start.81 = (bf16[96,1280]{1,0:T(8,128)(2,1)S(1)}, bf16[96,1280]{1,0:T(8,128)(2,1)S(1)}, u32[]{:S(2)}, u32[]{:S(2)}) collective-permute-start(bf16[96,1280]{1,0:T(8,128)(2,1)S(1)} %get-tuple-element.288), channel_id=1, source_target_pairs={{0,24},{2,26},{4,28},{6,30},{8,0},{10,2},{12,4},{14,6},{16,8},{18,... | collective-permute-start | bytes 737288 | tf_op jit(solution)/shard_map/ppermute | solution.py:477
  525.3 20.4 %collective-permute-start.82 = (bf16[96,1280]{1,0:T(8,128)(2,1)S(1)}, bf16[96,1280]{1,0:T(8,128)(2,1)S(1)}, u32[]{:S(2)}, u32[]{:S(2)}) collective-permute-start(bf16[96,1280]{1,0:T(8,128)(2,1)S(1)} %get-tuple-element.289), channel_id=1, source_target_pairs={{0,16},{2,18},{4,20},{6,22},{8,24},{10,26},{12,28},{14,30},{16,0},... | collective-permute-start | bytes 737288 | tf_op jit(solution)/shard_map/ppermute | solution.py:477
  525.5 20.2 %collective-permute-start.83 = (bf16[96,1280]{1,0:T(8,128)(2,1)S(1)}, bf16[96,1280]{1,0:T(8,128)(2,1)S(1)}, u32[]{:S(2)}, u32[]{:S(2)}) collective-permute-start(bf16[96,1280]{1,0:T(8,128)(2,1)S(1)} %get-tuple-element.290), channel_id=1, source_target_pairs={{0,8},{2,10},{4,12},{6,14},{8,16},{10,18},{12,20},{14,22},{16,24},... | collective-permute-start | bytes 737288 | tf_op jit(solution)/shard_map/ppermute | solution.py:477
  546.4 39.0 %collective-permute-start.85 = (bf16[96,1280]{1,0:T(8,128)(2,1)S(1)}, bf16[96,1280]{1,0:T(8,128)(2,1)S(1)}, u32[]{:S(2)}, u32[]{:S(2)}) collective-permute-start(bf16[96,1280]{1,0:T(8,128)(2,1)S(1)} %fusion.22), channel_id=1, source_target_pairs={{0,16},{2,18},{4,20},{6,22},{8,24},{10,26},{12,28},{14,30},{16,0},... | collective-permute-start | bytes 737288 | tf_op jit(solution)/shard_map/ppermute | solution.py:477
  548.8 36.6 %collective-permute-start.84 = (bf16[96,1280]{1,0:T(8,128)(2,1)S(1)}, bf16[96,1280]{1,0:T(8,128)(2,1)S(1)}, u32[]{:S(2)}, u32[]{:S(2)}) collective-permute-start(bf16[96,1280]{1,0:T(8,128)(2,1)S(1)} %fusion.22), channel_id=1, source_target_pairs={{0,8},{2,10},{4,12},{6,14},{8,16},{10,18},{12,20},{14,22},{16,24},... | collective-permute-start | bytes 737288 | tf_op jit(solution)/shard_map/ppermute | solution.py:477
  553.2 32.6 %collective-permute-start.67 = (bf16[48,1792]{1,0:T(8,128)(2,1)S(1)}, bf16[48,1792]{1,0:T(8,128)(2,1)S(1)}, u32[]{:S(2)}, u32[]{:S(2)}) collective-permute-start(bf16[48,1792]{1,0:T(8,128)(2,1)S(1)} %get-tuple-element.305), channel_id=1, source_target_pairs={{0,24},{2,26},{4,28},{6,30},{8,0},{10,2},{12,4},{14,6},{16,8},{18,... | collective-permute-start | bytes 516104 | tf_op jit(solution)/shard_map/ppermute | solution.py:477
  554.6 60.5 %collective-permute-start.68 = (bf16[48,1792]{1,0:T(8,128)(2,1)S(1)}, bf16[48,1792]{1,0:T(8,128)(2,1)S(1)}, u32[]{:S(2)}, u32[]{:S(2)}) collective-permute-start(bf16[48,1792]{1,0:T(8,128)(2,1)S(1)} %get-tuple-element.306), channel_id=1, source_target_pairs={{0,16},{2,18},{4,20},{6,22},{8,24},{10,26},{12,28},{14,30},{16,0},... | collective-permute-start | bytes 516104 | tf_op jit(solution)/shard_map/ppermute | solution.py:477
  554.8 60.3 %collective-permute-start.69 = (bf16[48,1792]{1,0:T(8,128)(2,1)S(1)}, bf16[48,1792]{1,0:T(8,128)(2,1)S(1)}, u32[]{:S(2)}, u32[]{:S(2)}) collective-permute-start(bf16[48,1792]{1,0:T(8,128)(2,1)S(1)} %get-tuple-element.307), channel_id=1, source_target_pairs={{0,8},{2,10},{4,12},{6,14},{8,16},{10,18},{12,20},{14,22},{16,24},... | collective-permute-start | bytes 516104 | tf_op jit(solution)/shard_map/ppermute | solution.py:477
  615.3 20.3 %collective-permute-start.71 = (bf16[48,1792]{1,0:T(8,128)(2,1)S(1)}, bf16[48,1792]{1,0:T(8,128)(2,1)S(1)}, u32[]{:S(2)}, u32[]{:S(2)}) collective-permute-start(bf16[48,1792]{1,0:T(8,128)(2,1)S(1)} %fusion.25), channel_id=1, source_target_pairs={{0,16},{2,18},{4,20},{6,22},{8,24},{10,26},{12,28},{14,30},{16,0},... | collective-permute-start | bytes 516104 | tf_op jit(solution)/shard_map/ppermute | solution.py:477
  624.2 32.1 %collective-permute-start.88 = (bf16[4,96,640]{2,1,0:T(8,128)(2,1)S(1)}, bf16[4,96,640]{2,1,0:T(8,128)(2,1)S(1)}, u32[]{:S(2)}, u32[]{:S(2)}) collective-permute-start(bf16[4,96,640]{2,1,0:T(8,128)(2,1)S(1)} %get-tuple-element.250), channel_id=1, source_target_pairs={{0,2},{2,0},{4,6},{6,4},{8,10},{10,8},{12,14},{14,12},{16,18},{18,... | collective-permute-start | bytes 1474568 | tf_op jit(solution)/shard_map/ppermute | solution.py:461
  657.5 29.9 %collective-permute-start.90 = (bf16[4,2,96,640]{3,2,0,1:T(8,128)(2,1)}, bf16[4,2,96,640]{3,2,0,1:T(8,128)(2,1)}, u32[]{:S(2)}, u32[]{:S(2)}) collective-permute-start(bf16[4,2,96,640]{3,2,0,1:T(8,128)(2,1)} %maximum_select_fusion.10), channel_id=1, source_target_pairs={{0,4},{2,6},{4,0},{6,2},{8,12},{10,14},{12,8},{14,10},{16,20},{18,... | collective-permute-start | bytes 2949128 | tf_op jit(solution)/shard_map/ppermute | solution.py:461
  657.5 32.0 %collective-permute-start.89 = (bf16[4,2,96,640]{3,2,0,1:T(8,128)(2,1)}, bf16[4,2,96,640]{3,2,0,1:T(8,128)(2,1)}, u32[]{:S(2)}, u32[]{:S(2)}) collective-permute-start(bf16[4,2,96,640]{3,2,0,1:T(8,128)(2,1)} %maximum_select_fusion.8), channel_id=1, source_target_pairs={{0,2},{2,0},{4,6},{6,4},{8,10},{10,8},{12,14},{14,12},{16,18},{18,... | collective-permute-start | bytes 2949128 | tf_op jit(solution)/shard_map/ppermute | solution.py:461
  (108 other events, 1499.0 us)
Sparse Core Ops, SparseCore 0:
  9.6 12.4 all-gather.3
  23.7 10.9 all-gather.5
  108.2 9.8 all-gather.7
  404.5 259.4 reduce-scatter.3
  666.3 13.9 reduce-scatter.5
  683.0 12.0 reduce-scatter.7

commit v4 on v3

--- a/solution.py
+++ b/solution.py
@@ -756,11 +756,12 @@
     places.after = expert_sums[1]
     back_near(last)
     back_far(0)
+    near_last = back[last]
     places.after = back[0]
     back_ring(last)
     places.after = None
     back_near(0)
-    mixture = lax.optimization_barrier((results[-1][1], back[last]))[0]
+    mixture = lax.optimization_barrier((results[-1][1], near_last))[0]
     normed_grad = sum(part.astype(F32) for part in back)
     gate_grads = lax.all_to_all(
         results[-1][2].reshape(count, half), "dp", split_axis=0, concat_axis=0, tiled=True

time: 732 us -> 794 us (1.085)
  waiting for transfers between devices: 318 us -> 361 us
  starting transfers between devices: 122 us -> 141 us
    ppermute x73, waiting for transfers between devices: 241 us -> 311 us  [send(): got = lax.ppermute(array, 'dp', pairs)]
    ppermute x12, waiting for transfers between devices: 66.6 us -> 47.1 us  [by_ring(): lax.ppermute(array, 'dp', [(i, (i + 4 * step) % self.count) for i in rang...]
    ppermute x12, starting transfers between devices: 22.2 us -> 35.5 us  [by_ring(): lax.ppermute(array, 'dp', [(i, (i + 4 * step) % self.count) for i in rang...]
  transfers between devices with their start and end apart: 99 -> 99, of which waited for: 37 -> 36; matrix products, arithmetic and copies ran while one was open for 14% -> 13% of each run, Pallas kernels for 21% -> 19%
where the time goes in v4:
time: 794 us; the launch traced here: 781 us
  waiting for transfers between devices  361 us (45%)
  Pallas kernels  149 us (19%)
  starting transfers between devices  141 us (18%)
  local copies, waits for them, and re-layouts  57.3 us (7%)
  other arithmetic  52.9 us (7%)
  between operations  15.8 us (2%)
    ppermute x73, waiting for transfers between devices, send(): got = lax.ppermute(array, 'dp', pairs)  311 us
    ppermute x73, starting transfers between devices, send(): got = lax.ppermute(array, 'dp', pairs)  94.1 us
    pallas_call x4, Pallas kernels, routed(): pl.pallas_call(functools.partial(routed_kernel, tables, not mix), grid=(4...  78.8 us
    ppermute x12, waiting for transfers between devices, by_ring(): lax.ppermute(array, 'dp', [(i, (i + 4 * step) % self.count) for i in rang...  47.1 us
    ppermute x12, starting transfers between devices, by_ring(): lax.ppermute(array, 'dp', [(i, (i + 4 * step) % self.count) for i in rang...  35.5 us
    pallas_call x1, Pallas kernels, expert_grads(): pl.pallas_call(functools.partial(expert_grads_kernel, tables, not before)...  29.3 us
    pallas_call x1, Pallas kernels, attend_back(): pl.pallas_call(attend_back_kernel, out_shape=[out((model, columns), BF16)...  24.4 us
    pallas_call x1, Pallas kernels, attend(): pl.pallas_call(attend_kernel, out_shape=[out((tokens, model), BF16), out(...  17 us
  transfers between devices with their start and end apart: 99, of which 36 were waited for; matrix products, arithmetic and copies ran while one was open for 13% of the time, Pallas kernels for 19%

profile of v4, /device:TPU:0, one launch (start us, length us, event | category | flops | bytes accessed | tf_op | source)
XLA Modules:
  0.0 781.3 jit_solution(1943165612264261774)
XLA Ops:
  7.9 2.1 constant_dynamic-slice_fusion.15
  10.0 3.0 collective-permute-start.6
  15.2 5.0 all-to-all-start
  20.4 2.0 collective-permute-start.1
  22.8 9.6 %collective-permute-done.1.refs_8_.refs_26_ = bf16[128,1536]{1,0:T(8,128)(2,1)S(1)} collective-permute-done((bf16[128,1536]{1,0:T(8,128)(2,1)S(1)}, bf16[128,1536]{1,0:T(8,128)(2,1)S(1)}, u32[]{:S(2)}, u32[]{:S(2)}) %collective-permute-start.1) | collective-permute-done | bytes 393248 | tf_op jit(solution)/shard_map/ppermute | solution.py:461
  36.4 17.0 %attend.1 = (bf16[512,1536]{1,0:T(8,128)(2,1)}, bf16[512,768]{1,0:T(8,128)(2,1)}, bf16[512,256]{1,0:T(8,128)(2,1)}, bf16[512,256]{1,0:T(8,128)(2,1)}, bf16[512,7...) custom-call(bf16[512,1536]{1,0:T(8,128)(2,1)} %x.3, bf16[1,1536]{1,0:T(2,128)(2,1)} %broadcast_in_dim.87.gain, ...), custom_call_target="tpu_custom_call" | custom-call | bytes 1048576 | tf_op jit(solution)/shard_map/attend/pallas_call | solution.py:361
  57.4 1.9 fusion.58
  61.5 14.0 %collective-permute-done.7 = bf16[128,1536]{1,0:T(8,128)(2,1)S(1)} collective-permute-done((bf16[128,1536]{1,0:T(8,128)(2,1)S(1)}, bf16[128,1536]{1,0:T(8,128)(2,1)S(1)}, u32[]{:S(2)}, u32[]{:S(2)}) %collective-permute-start.7) | collective-permute-done | bytes 393248 | tf_op jit(solution)/shard_map/ppermute | solution.py:461
  83.1 4.5 collective-permute-done.12.refs_9_.refs_27_
  89.3 5.0 collective-permute-done.22.refs_9_.refs_32_
  101.0 5.7 collective-permute-done.23.refs_9_.refs_37_
  108.2 4.5 collective-permute-done.13.refs_11_.refs_34_
  115.6 17.1 %collective-permute-done.4.refs_2_.refs_5_ = bf16[256,1536]{1,0:T(8,128)(2,1)S(1)} collective-permute-done((bf16[256,1536]{1,0:T(8,128)(2,1)S(1)}, bf16[256,1536]{1,0:T(8,128)(2,1)S(1)}, u32[]{:S(2)}, u32[]{:S(2)}) %collective-permute-start.4) | collective-permute-done | bytes 786464 | tf_op jit(solution)/shard_map/ppermute | solution.py:461
  135.6 2.0 collective-permute-start.35
  140.7 10.7 %collective-permute-done.28.refs_4_.refs_7_ = bf16[256,1536]{1,0:T(8,128)(2,1)S(1)} collective-permute-done((bf16[256,1536]{1,0:T(8,128)(2,1)}, bf16[256,1536]{1,0:T(8,128)(2,1)S(1)}, u32[]{:S(2)}, u32[]{:S(2)}) %collective-permute-start.28) | collective-permute-done | bytes 786464 | tf_op jit(solution)/shard_map/ppermute | solution.py:461
  152.9 4.8 collective-permute-done.9.refs_2_.refs_10_
  158.9 2.1 collective-permute-done.19.refs_6_.refs_4_
  161.0 2.7 collective-permute-done.18.refs_5_.refs_3_
  164.4 19.7 %routed_rows.4 = (bf16[256,1536]{1,0:T(8,128)(2,1)}, bf16[256,1536]{1,0:T(8,128)(2,1)}, bf16[256,1536]{1,0:T(8,128)(2,1)}, bf16[256,1536]{1,0:T(8,128)(2,1)}, bf...) custom-call(s32[9]{0:T(128)} %stack.312.refs_0_, ...), custom_call_target="tpu_custom_call", output_to_operand_aliasing={{5}: (12, {})} | custom-call | bytes 1048576 | tf_op jit(solution)/shard_map/routed_rows/pallas_call | solution.py:190
  193.1 17.0 %collective-permute-done.32.refs_6_.refs_9_ = bf16[128,1536]{1,0:T(8,128)(2,1)S(1)} collective-permute-done((bf16[128,1536]{1,0:T(8,128)(2,1)S(1)}, bf16[128,1536]{1,0:T(8,128)(2,1)S(1)}, u32[]{:S(2)}, u32[]{:S(2)}) %collective-permute-start.32) | collective-permute-done | bytes 393248 | tf_op jit(solution)/shard_map/ppermute | solution.py:461
  215.3 19.7 %routed_rows.5 = (bf16[256,1536]{1,0:T(8,128)(2,1)}, bf16[256,1536]{1,0:T(8,128)(2,1)}, bf16[256,1536]{1,0:T(8,128)(2,1)}, bf16[256,1536]{1,0:T(8,128)(2,1)}, bf...) custom-call(s32[9]{0:T(128)} %stack.321.refs_0_, ...), custom_call_target="tpu_custom_call", output_to_operand_aliasing={{5}: (12, {}), {4}: (17, {})} | custom-call | bytes 1048576 | tf_op jit(solution)/shard_map/routed_rows/pallas_call | solution.py:190
  236.3 2.0 collective-permute-start.36
  239.4 11.2 %collective-permute-done.37.refs_5_.refs_13_ = bf16[128,1536]{1,0:T(8,128)(2,1)S(1)} collective-permute-done((bf16[128,1536]{1,0:T(8,128)(2,1)}, bf16[128,1536]{1,0:T(8,128)(2,1)S(1)}, u32[]{:S(2)}, u32[]{:S(2)}) %collective-permute-start.37) | collective-permute-done | bytes 393248 | tf_op jit(solution)/shard_map/ppermute | solution.py:461
  257.0 19.7 %routed_rows.6 = (bf16[256,1536]{1,0:T(8,128)(2,1)}, bf16[256,1536]{1,0:T(8,128)(2,1)}, bf16[256,1536]{1,0:T(8,128)(2,1)}, bf16[256,1536]{1,0:T(8,128)(2,1)}, bf...) custom-call(s32[9]{0:T(128)} %stack.330.refs_0_, ...), custom_call_target="tpu_custom_call", output_to_operand_aliasing={{5}: (12, {}), {4}: (17, {})} | custom-call | bytes 1048576 | tf_op jit(solution)/shard_map/routed_rows/pallas_call | solution.py:190
  282.1 19.7 %routed_rows.7 = (bf16[256,1536]{1,0:T(8,128)(2,1)}, bf16[256,1536]{1,0:T(8,128)(2,1)}, bf16[256,1536]{1,0:T(8,128)(2,1)}, bf16[256,1536]{1,0:T(8,128)(2,1)}, bf...) custom-call(s32[9]{0:T(128)} %stack.303.refs_0_, ...), custom_call_target="tpu_custom_call", output_to_operand_aliasing={{5}: (12, {}), {4}: (17, {})} | custom-call | bytes 1048576 | tf_op jit(solution)/shard_map/routed_rows/pallas_call | solution.py:190
  306.4 7.1 collective-permute-done.43
  314.3 29.3 %expert_grads.1 = (f32[2,1536,512]{2,1,0:T(8,128)}, f32[512,1536]{1,0:T(8,128)}) custom-call(bf16[256,1536]{1,0:T(8,128)(2,1)} %copy-done.3, bf16[256,1536]{1,0:T(8,128)(2,1)} %copy-done.18, bf16[256,1536]{1,0:T(8,128)(2,1)} %copy-done.19, bf16[128,1536]{1,0:T(8,128)(2,1)} %collective-permute-done.18.refs_5_.refs_3_, bf16[128,1536]{1,0:T(8,128)(2,1)} %copy-done.37, ...), custom_call_target="tpu_custom_call" | custom-call | bytes 1048576 | tf_op jit(solution)/shard_map/expert_grads/pallas_call | solution.py:284
  347.3 4.5 collective-permute-done.45
  351.9 3.5 collective-permute-done.46
  358.6 4.6 all-to-all-start.1
  364.4 16.2 %collective-permute-done.49 = bf16[256,1536]{1,0:T(8,128)(2,1)} collective-permute-done((bf16[256,1536]{1,0:T(8,128)(2,1)}, bf16[256,1536]{1,0:T(8,128)(2,1)}, u32[]{:S(2)}, u32[]{:S(2)}) %collective-permute-start.49) | collective-permute-done | bytes 786464 | tf_op jit(solution)/shard_map/ppermute | solution.py:461
  385.9 2.2 collective-permute-start.50
  390.2 9.5 %collective-permute-done.50 = bf16[128,1536]{1,0:T(8,128)(2,1)} collective-permute-done((bf16[128,1536]{1,0:T(8,128)(2,1)}, bf16[128,1536]{1,0:T(8,128)(2,1)}, u32[]{:S(2)}, u32[]{:S(2)}) %collective-permute-start.50) | collective-permute-done | bytes 393248 | tf_op jit(solution)/shard_map/ppermute | solution.py:461
  404.1 18.0 %collective-permute-done.56 = bf16[256,1536]{1,0:T(8,128)(2,1)} collective-permute-done((bf16[256,1536]{1,0:T(8,128)(2,1)}, bf16[256,1536]{1,0:T(8,128)(2,1)}, u32[]{:S(2)}, u32[]{:S(2)}) %collective-permute-start.56) | collective-permute-done | bytes 786464 | tf_op jit(solution)/shard_map/ppermute | solution.py:461
  422.1 16.3 %collective-permute-start.57 = (bf16[256,1536]{1,0:T(8,128)(2,1)S(1)}, bf16[256,1536]{1,0:T(8,128)(2,1)S(1)}, u32[]{:S(2)}, u32[]{:S(2)}) collective-permute-start(bf16[256,1536]{1,0:T(8,128)(2,1)S(1)} %pad_maximum_fusion.5), channel_id=1, source_target_pairs={{0,16},{2,18},{4,20},{6,22},{8,24},{10,26},{12,28},{14,30},{16,0},... | collective-permute-start | bytes 2359304 | tf_op jit(solution)/shard_map/ppermute | solution.py:461
  440.4 47.9 %collective-permute-done.57 = bf16[256,1536]{1,0:T(8,128)(2,1)S(1)} collective-permute-done((bf16[256,1536]{1,0:T(8,128)(2,1)S(1)}, bf16[256,1536]{1,0:T(8,128)(2,1)S(1)}, u32[]{:S(2)}, u32[]{:S(2)}) %collective-permute-start.57) | collective-permute-done | bytes 786464 | tf_op jit(solution)/shard_map/ppermute | solution.py:461
  488.9 13.5 %collective-permute-done.58 = bf16[256,1536]{1,0:T(8,128)(2,1)S(1)} collective-permute-done((bf16[256,1536]{1,0:T(8,128)(2,1)S(1)}, bf16[256,1536]{1,0:T(8,128)(2,1)S(1)}, u32[]{:S(2)}, u32[]{:S(2)}) %collective-permute-start.58) | collective-permute-done | bytes 786464 | tf_op jit(solution)/shard_map/ppermute | solution.py:461
  502.5 2.1 multiply_reduce_fusion
  506.1 2.1 collective-permute-done.59
  514.2 24.4 %attend_back.1 = (bf16[1536,1280]{1,0:T(8,128)(2,1)}, bf16[512,1536]{1,0:T(8,128)(2,1)}) custom-call(bf16[512,1536]{1,0:T(8,128)(2,1)} %copy-done.13, bf16[1536,768]{1,0:T(8,128)(2,1)} %wq.3, bf16[1536,256]{1,0:T(8,128)(2,1)} %wk.3, bf16[1536,256]{1,0:T(8,128)(2,1)} %wv.3, bf16[768,1536]{1,0:T(8,128)(2,1)} %wo.3, f32[512,128]{1,0:T(8,128)} %get-tuple-element.309.cosine, ...), custom_call_target="tpu_custom_call" | custom-call | bytes 1048576 | tf_op jit(solution)/shard_map/attend_back/pallas_call | solution.py:428
  539.8 3.3 fusion.56
  547.7 27.0 %collective-permute-done.78 = bf16[4,2,96,640]{3,2,1,0:T(8,128)(2,1)S(1)} collective-permute-done((bf16[4,2,96,640]{3,2,1,0:T(8,128)(2,1)S(1)}, bf16[4,2,96,640]{3,2,1,0:T(8,128)(2,1)S(1)}, u32[]{:S(2)}, u32[]{:S(2)}) %collective-permute-start.78) | collective-permute-done | bytes 983072 | tf_op jit(solution)/shard_map/ppermute | solution.py:461
  587.3 13.7 %collective-permute-done.79 = bf16[4,96,640]{2,1,0:T(8,128)(2,1)} collective-permute-done((bf16[4,96,640]{2,1,0:T(8,128)(2,1)}, bf16[4,96,640]{2,1,0:T(8,128)(2,1)}, u32[]{:S(2)}, u32[]{:S(2)}) %collective-permute-start.79) | collective-permute-done | bytes 491552 | tf_op jit(solution)/shard_map/ppermute | solution.py:461
  603.7 2.1 collective-permute-start.81
  606.4 12.5 %collective-permute-done.64 = bf16[4,2,48,896]{3,2,1,0:T(8,128)(2,1)S(1)} collective-permute-done((bf16[4,2,48,896]{3,2,1,0:T(8,128)(2,1)S(1)}, bf16[4,2,48,896]{3,2,1,0:T(8,128)(2,1)S(1)}, u32[]{:S(2)}, u32[]{:S(2)}) %collective-permute-start.64) | collective-permute-done | bytes 688160 | tf_op jit(solution)/shard_map/ppermute | solution.py:461
  619.9 16.8 %collective-permute-done.82 = bf16[96,1280]{1,0:T(8,128)(2,1)S(1)} collective-permute-done((bf16[96,1280]{1,0:T(8,128)(2,1)S(1)}, bf16[96,1280]{1,0:T(8,128)(2,1)S(1)}, u32[]{:S(2)}, u32[]{:S(2)}) %collective-permute-start.82) | collective-permute-done | bytes 245792 | tf_op jit(solution)/shard_map/ppermute | solution.py:477
  637.1 14.4 %collective-permute-start.85 = (bf16[96,1280]{1,0:T(8,128)(2,1)S(1)}, bf16[96,1280]{1,0:T(8,128)(2,1)S(1)}, u32[]{:S(2)}, u32[]{:S(2)}) collective-permute-start(bf16[96,1280]{1,0:T(8,128)(2,1)S(1)} %fusion.22), channel_id=1, source_target_pairs={{0,16},{2,18},{4,20},{6,22},{8,24},{10,26},{12,28},{14,30},{16,0},... | collective-permute-start | bytes 737288 | tf_op jit(solution)/shard_map/ppermute | solution.py:477
  651.5 1.9 collective-permute-start.84
  653.7 1.9 collective-permute-start.67
  655.7 12.2 %collective-permute-start.69 = (bf16[48,1792]{1,0:T(8,128)(2,1)S(1)}, bf16[48,1792]{1,0:T(8,128)(2,1)S(1)}, u32[]{:S(2)}, u32[]{:S(2)}) collective-permute-start(bf16[48,1792]{1,0:T(8,128)(2,1)S(1)} %get-tuple-element.307), channel_id=1, source_target_pairs={{0,8},{2,10},{4,12},{6,14},{8,16},{10,18},{12,20},{14,22},{16,24},... | collective-permute-start | bytes 516104 | tf_op jit(solution)/shard_map/ppermute | solution.py:477
  667.9 13.6 %collective-permute-done.85 = bf16[96,1280]{1,0:T(8,128)(2,1)S(1)} collective-permute-done((bf16[96,1280]{1,0:T(8,128)(2,1)S(1)}, bf16[96,1280]{1,0:T(8,128)(2,1)S(1)}, u32[]{:S(2)}, u32[]{:S(2)}) %collective-permute-start.85) | collective-permute-done | bytes 245792 | tf_op jit(solution)/shard_map/ppermute | solution.py:477
  681.8 6.3 collective-permute-done.68
  688.4 1.9 collective-permute-start.70
  691.9 2.9 collective-permute-done.72
  694.7 7.5 collective-permute-done.71
  706.3 5.5 collective-permute-done.74
  719.9 10.5 %collective-permute-done.76 = bf16[4,2,48,896]{3,2,0,1:T(8,128)(2,1)S(1)} collective-permute-done((bf16[4,2,48,896]{3,2,0,1:T(8,128)(2,1)S(1)}, bf16[4,2,48,896]{3,2,0,1:T(8,128)(2,1)S(1)}, u32[]{:S(2)}, u32[]{:S(2)}) %collective-permute-start.76) | collective-permute-done | bytes 688160 | tf_op jit(solution)/shard_map/ppermute | solution.py:461
  736.7 2.8 slice.241
  739.5 9.1 %collective-permute-done.90 = bf16[4,2,96,640]{3,2,0,1:T(8,128)(2,1)} collective-permute-done((bf16[4,2,96,640]{3,2,0,1:T(8,128)(2,1)}, bf16[4,2,96,640]{3,2,0,1:T(8,128)(2,1)}, u32[]{:S(2)}, u32[]{:S(2)}) %collective-permute-start.90) | collective-permute-done | bytes 983072 | tf_op jit(solution)/shard_map/ppermute | solution.py:461
  755.1 2.5 slice.240
  757.6 4.6 fusion.6
  764.6 3.7 slice_bitcast_fusion
  768.4 3.0 maximum_select_fusion.4
  771.3 2.9 maximum_select_fusion.2
  (461 shorter events, 159.1 us)
Async XLA Ops:
  7.2 151.7 %all-gather.4.cloned.1.call-start = ((), (), s32[]{:S(2)}) async-start(), calls=%async_computation.5 | async-start | bytes 2359296 | tf_op jit(solution)/shard_map/all_gather | solution.py:638
  10.0 45.9 %collective-permute-start.6 = (bf16[256,1536]{1,0:T(8,128)(2,1)}, bf16[256,1536]{1,0:T(8,128)(2,1)S(1)}, u32[]{:S(2)}, u32[]{:S(2)}) collective-permute-start(bf16[256,1536]{1,0:T(8,128)(2,1)} %constant_dynamic-slice_fusion.15), channel_id=1, source_target_pairs={{0,4},{2,6},{4,0},{6,2},{8,12},{10,14},{12,8},{14,10},{16,20},{18,... | collective-permute-start | bytes 2359304 | tf_op jit(solution)/shard_map/ppermute | solution.py:461
  13.0 44.4 %collective-permute-start.5 = (bf16[256,1536]{1,0:T(8,128)(2,1)}, bf16[256,1536]{1,0:T(8,128)(2,1)}, u32[]{:S(2)}, u32[]{:S(2)}) collective-permute-start(bf16[256,1536]{1,0:T(8,128)(2,1)} %constant_dynamic-slice_fusion.15), channel_id=1, source_target_pairs={{0,2},{2,0},{4,6},{6,4},{8,10},{10,8},{12,14},{14,12},{16,18},{18,... | collective-permute-start | bytes 2359304 | tf_op jit(solution)/shard_map/ppermute | solution.py:461
  15.2 38.1 %all-to-all-start = ((s32[16,1,256]{2,1,0:T(1,128)}), s32[16,1,256]{2,1,0:T(1,128)S(1)}, u32[]{:S(2)}, u32[]{:S(2)}) async-start(s32[16,1,256]{2,1,0:T(1,128)} %broadcast_in_dim.97), calls=%async_computation | async-start | bytes 32768 | tf_op jit(solution)/shard_map/all_to_all | solution.py:648
  20.2 138.7 %all-gather.6.cloned.1.call-start = ((), (), s32[]{:S(2)}) async-start(), calls=%async_computation.6 | async-start | bytes 2359296 | tf_op jit(solution)/shard_map/all_gather | solution.py:639
  22.4 136.5 %all-gather.8.cloned.1.call-start = ((), (), s32[]{:S(2)}) async-start(), calls=%async_computation.7 | async-start | bytes 2359296 | tf_op jit(solution)/shard_map/all_gather | solution.py:640
  54.5 23.7 %collective-permute-start = (bf16[256,1536]{1,0:T(8,128)(2,1)S(1)}, bf16[256,1536]{1,0:T(8,128)(2,1)S(1)}, u32[]{:S(2)}, u32[]{:S(2)}) collective-permute-start(bf16[256,1536]{1,0:T(8,128)(2,1)S(1)} %constant_dynamic-slice_fusion.16), channel_id=1, source_target_pairs={{0,1},{1,0},{2,3},{3,2},{4,5},{5,4},{6,7},{7,6},{8,9},{9,8},{10,11... | collective-permute-start | bytes 2359304 | tf_op jit(solution)/shard_map/ppermute | solution.py:482
  54.6 34.7 %collective-permute-start.3 = (bf16[128,1536]{1,0:T(8,128)(2,1)}, bf16[128,1536]{1,0:T(8,128)(2,1)}, u32[]{:S(2)}, u32[]{:S(2)}) collective-permute-start(bf16[128,1536]{1,0:T(8,128)(2,1)} %collective-permute-done.2.refs_8_.refs_31_), channel_id=1, source_target_pairs={{0,8},{2,10},{4,12},{6,14},{8,16},{10,18},{12,20},{14,22},{16,24},... | collective-permute-start | bytes 1179656 | tf_op jit(solution)/shard_map/ppermute | solution.py:461
  55.9 25.1 %collective-permute-start.10 = (bf16[128,1536]{1,0:T(8,128)(2,1)S(1)}, bf16[128,1536]{1,0:T(8,128)(2,1)S(1)}, u32[]{:S(2)}, u32[]{:S(2)}) collective-permute-start(bf16[128,1536]{1,0:T(8,128)(2,1)S(1)} %collective-permute-done.1.refs_8_.refs_26_), channel_id=1, source_target_pairs={{0,4},{2,6},{4,0},{6,2},{8,12},{10,14},{12,8},{14,10},{16,20},{18,... | collective-permute-start | bytes 1179656 | tf_op jit(solution)/shard_map/ppermute | solution.py:461
  60.0 22.6 %collective-permute-start.20 = (bf16[128,1536]{1,0:T(8,128)(2,1)S(1)}, bf16[128,1536]{1,0:T(8,128)(2,1)S(1)}, u32[]{:S(2)}, u32[]{:S(2)}) collective-permute-start(bf16[128,1536]{1,0:T(8,128)(2,1)S(1)} %get-tuple-element.291.refs_10_.refs_23_), channel_id=1, source_target_pairs={{0,2},{2,0},{4,6},{6,4},{8,10},{10,8},{12,14},{14,12},{16,18},{18,... | collective-permute-start | bytes 1179656 | tf_op jit(solution)/shard_map/ppermute | solution.py:461
  78.3 56.8 %collective-permute-start.8 = (bf16[512,1536]{1,0:T(8,128)(2,1)}, bf16[512,1536]{1,0:T(8,128)(2,1)}, u32[]{:S(2)}, u32[]{:S(2)}) collective-permute-start(bf16[512,1536]{1,0:T(8,128)(2,1)} %pad_maximum_fusion.refs_7_.refs_20_), channel_id=1, source_target_pairs={{0,8},{2,10},{4,12},{6,14},{8,16},{10,18},{12,20},{14,22},{16,24},... | collective-permute-start | bytes 4718600 | tf_op jit(solution)/shard_map/ppermute | solution.py:461
  95.9 36.8 %collective-permute-start.4 = (bf16[256,1536]{1,0:T(8,128)(2,1)S(1)}, bf16[256,1536]{1,0:T(8,128)(2,1)S(1)}, u32[]{:S(2)}, u32[]{:S(2)}) collective-permute-start(bf16[256,1536]{1,0:T(8,128)(2,1)S(1)} %multiply_convert_fusion.refs_2_.refs_0_), channel_id=1, source_target_pairs={{0,8},{2,10},{4,12},{6,14},{8,16},{10,18},{12,20},{14,22},{16,24},... | collective-permute-start | bytes 2359304 | tf_op jit(solution)/shard_map/ppermute | solution.py:461
  106.7 26.9 %collective-permute-start.27 = (bf16[128,1536]{1,0:T(8,128)(2,1)S(1)}, bf16[128,1536]{1,0:T(8,128)(2,1)}, u32[]{:S(2)}, u32[]{:S(2)}) collective-permute-start(bf16[128,1536]{1,0:T(8,128)(2,1)S(1)} %collective-permute-done.23.refs_9_.refs_37_), channel_id=1, source_target_pairs={{0,4},{2,6},{4,0},{6,2},{8,12},{10,14},{12,8},{14,10},{16,20},{18,... | collective-permute-start | bytes 1179656 | tf_op jit(solution)/shard_map/ppermute | solution.py:461
  108.2 649.4 %reduce-scatter.4.cloned.1.call-start = ((), (), s32[]{:S(2)}) async-start(), calls=%async_computation.8 | async-start | bytes 13369344 | tf_op jit(solution)/shard_map/reduce_scatter | solution.py:780
  112.7 23.0 %collective-permute-start.14 = (bf16[256,1536]{1,0:T(8,128)(2,1)S(1)}, bf16[256,1536]{1,0:T(8,128)(2,1)S(1)}, u32[]{:S(2)}, u32[]{:S(2)}) collective-permute-start(bf16[256,1536]{1,0:T(8,128)(2,1)S(1)} %multiply_convert_fusion.refs_2_.refs_0_), channel_id=1, source_target_pairs={{0,2},{2,0},{4,6},{6,4},{8,10},{10,8},{12,14},{14,12},{16,18},{18,... | collective-permute-start | bytes 2359304 | tf_op jit(solution)/shard_map/ppermute | solution.py:461
  114.1 24.3 %collective-permute-start.17 = (bf16[256,1536]{1,0:T(8,128)(2,1)S(1)}, bf16[256,1536]{1,0:T(8,128)(2,1)S(1)}, u32[]{:S(2)}, u32[]{:S(2)}) collective-permute-start(bf16[256,1536]{1,0:T(8,128)(2,1)S(1)} %multiply_convert_fusion.refs_2_.refs_0_), channel_id=1, source_target_pairs={{0,4},{2,6},{4,0},{6,2},{8,12},{10,14},{12,8},{14,10},{16,20},{18,... | collective-permute-start | bytes 2359304 | tf_op jit(solution)/shard_map/ppermute | solution.py:461
  135.1 22.6 %collective-permute-start.9 = (bf16[256,1536]{1,0:T(8,128)(2,1)}, bf16[256,1536]{1,0:T(8,128)(2,1)}, u32[]{:S(2)}, u32[]{:S(2)}) collective-permute-start(bf16[256,1536]{1,0:T(8,128)(2,1)} %copy-done.26), channel_id=1, source_target_pairs={{0,8},{2,10},{4,12},{6,14},{8,16},{10,18},{12,20},{14,22},{16,24},... | collective-permute-start | bytes 2359304 | tf_op jit(solution)/shard_map/ppermute | solution.py:461
  135.1 49.0 %collective-permute-start.24 = (bf16[256,1536]{1,0:T(8,128)(2,1)}, bf16[256,1536]{1,0:T(8,128)(2,1)}, u32[]{:S(2)}, u32[]{:S(2)}) collective-permute-start(bf16[256,1536]{1,0:T(8,128)(2,1)} %copy-done.26), channel_id=1, source_target_pairs={{0,2},{2,0},{4,6},{6,4},{8,10},{10,8},{12,14},{14,12},{16,18},{18,... | collective-permute-start | bytes 2359304 | tf_op jit(solution)/shard_map/ppermute | solution.py:461
  135.6 79.6 %collective-permute-start.35 = (bf16[512,1536]{1,0:T(8,128)(2,1)}, bf16[512,1536]{1,0:T(8,128)(2,1)}, u32[]{:S(2)}, u32[]{:S(2)}) collective-permute-start(bf16[512,1536]{1,0:T(8,128)(2,1)} %collective-permute-done.8.refs_7_.refs_25_), channel_id=1, source_target_pairs={{0,8},{2,10},{4,12},{6,14},{8,16},{10,18},{12,20},{14,22},{16,24},... | collective-permute-start | bytes 4718600 | tf_op jit(solution)/shard_map/ppermute | solution.py:461
  157.7 32.3 %collective-permute-start.29 = (bf16[256,1536]{1,0:T(8,128)(2,1)}, bf16[256,1536]{1,0:T(8,128)(2,1)}, u32[]{:S(2)}, u32[]{:S(2)}) collective-permute-start(bf16[256,1536]{1,0:T(8,128)(2,1)} %collective-permute-done.9.refs_2_.refs_10_), channel_id=1, source_target_pairs={{0,4},{2,6},{4,0},{6,2},{8,12},{10,14},{12,8},{14,10},{16,20},{18,... | collective-permute-start | bytes 2359304 | tf_op jit(solution)/shard_map/ppermute | solution.py:461
  184.1 27.3 %collective-permute-start.25 = (bf16[256,1536]{1,0:T(8,128)(2,1)}, bf16[256,1536]{1,0:T(8,128)(2,1)S(1)}, u32[]{:S(2)}, u32[]{:S(2)}) collective-permute-start(bf16[256,1536]{1,0:T(8,128)(2,1)} %collective-permute-done.9.refs_2_.refs_10_), channel_id=1, source_target_pairs={{0,2},{2,0},{4,6},{6,4},{8,10},{10,8},{12,14},{14,12},{16,18},{18,... | collective-permute-start | bytes 2359304 | tf_op jit(solution)/shard_map/ppermute | solution.py:461
  184.7 27.6 %collective-permute-start.21 = (bf16[256,1536]{1,0:T(8,128)(2,1)}, bf16[256,1536]{1,0:T(8,128)(2,1)}, u32[]{:S(2)}, u32[]{:S(2)}) collective-permute-start(bf16[256,1536]{1,0:T(8,128)(2,1)} %collective-permute-done.9.refs_2_.refs_10_), channel_id=1, source_target_pairs={{0,8},{2,10},{4,12},{6,14},{8,16},{10,18},{12,20},{14,22},{16,24},... | collective-permute-start | bytes 2359304 | tf_op jit(solution)/shard_map/ppermute | solution.py:461
  186.4 23.7 %collective-permute-start.32 = (bf16[128,1536]{1,0:T(8,128)(2,1)S(1)}, bf16[128,1536]{1,0:T(8,128)(2,1)S(1)}, u32[]{:S(2)}, u32[]{:S(2)}) collective-permute-start(bf16[128,1536]{1,0:T(8,128)(2,1)S(1)} %slice.213), channel_id=1, source_target_pairs={{0,2},{2,0},{4,6},{6,4},{8,10},{10,8},{12,14},{14,12},{16,18},{18,... | collective-permute-start | bytes 1179656 | tf_op jit(solution)/shard_map/ppermute | solution.py:461
  210.1 24.8 %collective-permute-start.38 = (bf16[128,1536]{1,0:T(8,128)(2,1)}, bf16[128,1536]{1,0:T(8,128)(2,1)S(1)}, u32[]{:S(2)}, u32[]{:S(2)}) collective-permute-start(bf16[128,1536]{1,0:T(8,128)(2,1)} %slice.216), channel_id=1, source_target_pairs={{0,2},{2,0},{4,6},{6,4},{8,10},{10,8},{12,14},{14,12},{16,18},{18,... | collective-permute-start | bytes 1179656 | tf_op jit(solution)/shard_map/ppermute | solution.py:461
  212.3 38.7 %collective-permute-start.30 = (bf16[256,1536]{1,0:T(8,128)(2,1)}, bf16[256,1536]{1,0:T(8,128)(2,1)}, u32[]{:S(2)}, u32[]{:S(2)}) collective-permute-start(bf16[256,1536]{1,0:T(8,128)(2,1)} %collective-permute-done.21.refs_2_.refs_15_), channel_id=1, source_target_pairs={{0,4},{2,6},{4,0},{6,2},{8,12},{10,14},{12,8},{14,10},{16,20},{18,... | collective-permute-start | bytes 2359304 | tf_op jit(solution)/shard_map/ppermute | solution.py:461
  213.8 39.0 %collective-permute-start.26 = (bf16[256,1536]{1,0:T(8,128)(2,1)}, bf16[256,1536]{1,0:T(8,128)(2,1)}, u32[]{:S(2)}, u32[]{:S(2)}) collective-permute-start(bf16[256,1536]{1,0:T(8,128)(2,1)} %collective-permute-done.21.refs_2_.refs_15_), channel_id=1, source_target_pairs={{0,2},{2,0},{4,6},{6,4},{8,10},{10,8},{12,14},{14,12},{16,18},{18,... | collective-permute-start | bytes 2359304 | tf_op jit(solution)/shard_map/ppermute | solution.py:461
  235.7 41.0 %collective-permute-start.39 = (bf16[256,1536]{1,0:T(8,128)(2,1)}, bf16[256,1536]{1,0:T(8,128)(2,1)}, u32[]{:S(2)}, u32[]{:S(2)}) collective-permute-start(bf16[256,1536]{1,0:T(8,128)(2,1)} %get-tuple-element.179), channel_id=1, source_target_pairs={{0,2},{2,0},{4,6},{6,4},{8,10},{10,8},{12,14},{14,12},{16,18},{18,... | collective-permute-start | bytes 2359304 | tf_op jit(solution)/shard_map/ppermute | solution.py:461
  236.3 44.7 %collective-permute-start.36 = (bf16[512,1536]{1,0:T(8,128)(2,1)}, bf16[512,1536]{1,0:T(8,128)(2,1)S(1)}, u32[]{:S(2)}, u32[]{:S(2)}) collective-permute-start(bf16[512,1536]{1,0:T(8,128)(2,1)} %collective-permute-done.35.refs_7_.refs_30_), channel_id=1, source_target_pairs={{0,8},{2,10},{4,12},{6,14},{8,16},{10,18},{12,20},{14,22},{16,24},... | collective-permute-start | bytes 4718600 | tf_op jit(solution)/shard_map/ppermute | solution.py:461
  250.6 52.7 %collective-permute-start.42 = (bf16[256,1536]{1,0:T(8,128)(2,1)}, bf16[256,1536]{1,0:T(8,128)(2,1)}, u32[]{:S(2)}, u32[]{:S(2)}) collective-permute-start(bf16[256,1536]{1,0:T(8,128)(2,1)} %get-tuple-element.186), channel_id=1, source_target_pairs={{0,4},{2,6},{4,0},{6,2},{8,12},{10,14},{12,8},{14,10},{16,20},{18,... | collective-permute-start | bytes 2359304 | tf_op jit(solution)/shard_map/ppermute | solution.py:461
  253.8 25.2 %collective-permute-start.33 = (bf16[128,1536]{1,0:T(8,128)(2,1)S(1)}, bf16[128,1536]{1,0:T(8,128)(2,1)}, u32[]{:S(2)}, u32[]{:S(2)}) collective-permute-start(bf16[128,1536]{1,0:T(8,128)(2,1)S(1)} %slice.211), channel_id=1, source_target_pairs={{0,4},{2,6},{4,0},{6,2},{8,12},{10,14},{12,8},{14,10},{16,20},{18,... | collective-permute-start | bytes 1179656 | tf_op jit(solution)/shard_map/ppermute | solution.py:461
  255.5 25.5 %collective-permute-start.34 = (bf16[128,1536]{1,0:T(8,128)(2,1)}, bf16[128,1536]{1,0:T(8,128)(2,1)}, u32[]{:S(2)}, u32[]{:S(2)}) collective-permute-start(bf16[128,1536]{1,0:T(8,128)(2,1)} %slice.214), channel_id=1, source_target_pairs={{0,2},{2,0},{4,6},{6,4},{8,10},{10,8},{12,14},{14,12},{16,18},{18,... | collective-permute-start | bytes 1179656 | tf_op jit(solution)/shard_map/ppermute | solution.py:461
  279.0 22.8 %collective-permute-start.40 = (bf16[128,1536]{1,0:T(8,128)(2,1)S(1)}, bf16[128,1536]{1,0:T(8,128)(2,1)}, u32[]{:S(2)}, u32[]{:S(2)}) collective-permute-start(bf16[128,1536]{1,0:T(8,128)(2,1)S(1)} %slice.217), channel_id=1, source_target_pairs={{0,4},{2,6},{4,0},{6,2},{8,12},{10,14},{12,8},{14,10},{16,20},{18,... | collective-permute-start | bytes 1179656 | tf_op jit(solution)/shard_map/ppermute | solution.py:461
  301.9 41.7 %collective-permute-start.41 = (bf16[256,1536]{1,0:T(8,128)(2,1)}, bf16[256,1536]{1,0:T(8,128)(2,1)S(1)}, u32[]{:S(2)}, u32[]{:S(2)}) collective-permute-start(bf16[256,1536]{1,0:T(8,128)(2,1)} %get-tuple-element.182), channel_id=1, source_target_pairs={{0,4},{2,6},{4,0},{6,2},{8,12},{10,14},{12,8},{14,10},{16,20},{18,... | collective-permute-start | bytes 2359304 | tf_op jit(solution)/shard_map/ppermute | solution.py:461
  313.5 30.3 %collective-permute-start.44 = (bf16[256,1536]{1,0:T(8,128)(2,1)S(1)}, bf16[256,1536]{1,0:T(8,128)(2,1)}, u32[]{:S(2)}, u32[]{:S(2)}) collective-permute-start(bf16[256,1536]{1,0:T(8,128)(2,1)S(1)} %copy-done.81), channel_id=1, source_target_pairs={{0,2},{2,0},{4,6},{6,4},{8,10},{10,8},{12,14},{14,12},{16,18},{18,... | collective-permute-start | bytes 2359304 | tf_op jit(solution)/shard_map/ppermute | solution.py:461
  356.4 408.3 %reduce-scatter.6.cloned.1.call-start = ((), (), s32[]{:S(2)}) async-start(), calls=%async_computation.9 | async-start | bytes 9437184 | tf_op jit(solution)/shard_map/reduce_scatter | solution.py:814
  357.0 23.6 %collective-permute-start.49 = (bf16[256,1536]{1,0:T(8,128)(2,1)}, bf16[256,1536]{1,0:T(8,128)(2,1)}, u32[]{:S(2)}, u32[]{:S(2)}) collective-permute-start(bf16[256,1536]{1,0:T(8,128)(2,1)} %get-tuple-element.216), channel_id=1, source_target_pairs={{0,4},{2,6},{4,0},{6,2},{8,12},{10,14},{12,8},{14,10},{16,20},{18,... | collective-permute-start | bytes 2359304 | tf_op jit(solution)/shard_map/ppermute | solution.py:461
  357.9 25.7 %collective-permute-start.48 = (bf16[256,1536]{1,0:T(8,128)(2,1)}, bf16[256,1536]{1,0:T(8,128)(2,1)}, u32[]{:S(2)}, u32[]{:S(2)}) collective-permute-start(bf16[256,1536]{1,0:T(8,128)(2,1)} %get-tuple-element.214), channel_id=1, source_target_pairs={{0,2},{2,0},{4,6},{6,4},{8,10},{10,8},{12,14},{14,12},{16,18},{18,... | collective-permute-start | bytes 2359304 | tf_op jit(solution)/shard_map/ppermute | solution.py:461
  358.6 31.6 %all-to-all-start.1 = ((f32[16,1,256]{2,1,0:T(1,128)}), f32[16,1,256]{2,1,0:T(1,128)S(1)}, u32[]{:S(2)}, u32[]{:S(2)}) async-start(f32[16,1,256]{2,1,0:T(1,128)} %bitcast.41), calls=%async_computation.2 | async-start | bytes 32768 | tf_op jit(solution)/shard_map/all_to_all | solution.py:766
  363.2 411.1 %reduce-scatter.8.cloned.1.call-start = ((), (), s32[]{:S(2)}) async-start(), calls=%async_computation.10 | async-start | bytes 4718592 | tf_op jit(solution)/shard_map/reduce_scatter | solution.py:815
  389.3 32.7 %collective-permute-start.56 = (bf16[256,1536]{1,0:T(8,128)(2,1)}, bf16[256,1536]{1,0:T(8,128)(2,1)}, u32[]{:S(2)}, u32[]{:S(2)}) collective-permute-start(bf16[256,1536]{1,0:T(8,128)(2,1)} %pad_maximum_fusion.4), channel_id=1, source_target_pairs={{0,24},{2,26},{4,28},{6,30},{8,0},{10,2},{12,4},{14,6},{16,8},{18,... | collective-permute-start | bytes 2359304 | tf_op jit(solution)/shard_map/ppermute | solution.py:461
  399.8 40.2 %collective-permute-start.54 = (bf16[256,1536]{1,0:T(8,128)(2,1)}, bf16[256,1536]{1,0:T(8,128)(2,1)S(1)}, u32[]{:S(2)}, u32[]{:S(2)}) collective-permute-start(bf16[256,1536]{1,0:T(8,128)(2,1)} %get-tuple-element.224), channel_id=1, source_target_pairs={{0,2},{2,0},{4,6},{6,4},{8,10},{10,8},{12,14},{14,12},{16,18},{18,... | collective-permute-start | bytes 2359304 | tf_op jit(solution)/shard_map/ppermute | solution.py:461
  401.3 37.1 %collective-permute-start.51 = (bf16[256,1536]{1,0:T(8,128)(2,1)}, bf16[256,1536]{1,0:T(8,128)(2,1)S(1)}, u32[]{:S(2)}, u32[]{:S(2)}) collective-permute-start(bf16[256,1536]{1,0:T(8,128)(2,1)} %get-tuple-element.218), channel_id=1, source_target_pairs={{0,4},{2,6},{4,0},{6,2},{8,12},{10,14},{12,8},{14,10},{16,20},{18,... | collective-permute-start | bytes 2359304 | tf_op jit(solution)/shard_map/ppermute | solution.py:461
  422.1 66.2 %collective-permute-start.57 = (bf16[256,1536]{1,0:T(8,128)(2,1)S(1)}, bf16[256,1536]{1,0:T(8,128)(2,1)S(1)}, u32[]{:S(2)}, u32[]{:S(2)}) collective-permute-start(bf16[256,1536]{1,0:T(8,128)(2,1)S(1)} %pad_maximum_fusion.5), channel_id=1, source_target_pairs={{0,16},{2,18},{4,20},{6,22},{8,24},{10,26},{12,28},{14,30},{16,0},... | collective-permute-start | bytes 2359304 | tf_op jit(solution)/shard_map/ppermute | solution.py:461
  438.6 50.0 %collective-permute-start.52 = (bf16[128,1536]{1,0:T(8,128)(2,1)S(1)}, bf16[128,1536]{1,0:T(8,128)(2,1)S(1)}, u32[]{:S(2)}, u32[]{:S(2)}) collective-permute-start(bf16[128,1536]{1,0:T(8,128)(2,1)S(1)} %slice.225), channel_id=1, source_target_pairs={{0,2},{2,0},{4,6},{6,4},{8,10},{10,8},{12,14},{14,12},{16,18},{18,... | collective-permute-start | bytes 1179656 | tf_op jit(solution)/shard_map/ppermute | solution.py:461
  440.3 48.5 %collective-permute-start.55 = (bf16[128,1536]{1,0:T(8,128)(2,1)S(1)}, bf16[128,1536]{1,0:T(8,128)(2,1)S(1)}, u32[]{:S(2)}, u32[]{:S(2)}) collective-permute-start(bf16[128,1536]{1,0:T(8,128)(2,1)S(1)} %slice.228), channel_id=1, source_target_pairs={{0,4},{2,6},{4,0},{6,2},{8,12},{10,14},{12,8},{14,10},{16,20},{18,... | collective-permute-start | bytes 1179656 | tf_op jit(solution)/shard_map/ppermute | solution.py:461
  512.9 31.3 %collective-permute-start.62 = (bf16[4,2,48,896]{3,2,0,1:T(8,128)(2,1)S(1)}, bf16[4,2,48,896]{3,2,0,1:T(8,128)(2,1)S(1)}, u32[]{:S(2)}, u32[]{:S(2)}) collective-permute-start(bf16[4,2,48,896]{3,2,0,1:T(8,128)(2,1)S(1)} %bitcast.215), channel_id=1, source_target_pairs={{0,2},{2,0},{4,6},{6,4},{8,10},{10,8},{12,14},{14,12},{16,18},{18,... | collective-permute-start | bytes 2064392 | tf_op jit(solution)/shard_map/ppermute | solution.py:461
  543.2 31.5 %collective-permute-start.78 = (bf16[4,2,96,640]{3,2,1,0:T(8,128)(2,1)S(1)}, bf16[4,2,96,640]{3,2,1,0:T(8,128)(2,1)S(1)}, u32[]{:S(2)}, u32[]{:S(2)}) collective-permute-start(bf16[4,2,96,640]{3,2,1,0:T(8,128)(2,1)S(1)} %dynamic-slice_bitcast_fusion), channel_id=1, source_target_pairs={{0,4},{2,6},{4,0},{6,2},{8,12},{10,14},{12,8},{14,10},{16,20},{18,... | collective-permute-start | bytes 2949128 | tf_op jit(solution)/shard_map/ppermute | solution.py:461
  543.7 32.1 %collective-permute-start.77 = (bf16[4,2,96,640]{3,2,0,1:T(8,128)(2,1)S(1)}, bf16[4,2,96,640]{3,2,0,1:T(8,128)(2,1)S(1)}, u32[]{:S(2)}, u32[]{:S(2)}) collective-permute-start(bf16[4,2,96,640]{3,2,0,1:T(8,128)(2,1)S(1)} %bitcast.213), channel_id=1, source_target_pairs={{0,2},{2,0},{4,6},{6,4},{8,10},{10,8},{12,14},{14,12},{16,18},{18,... | collective-permute-start | bytes 2949128 | tf_op jit(solution)/shard_map/ppermute | solution.py:461
  547.1 31.7 %collective-permute-start.63 = (f32[18,1536]{1,0:T(8,128)S(1)}, f32[18,1536]{1,0:T(8,128)S(1)}, u32[]{:S(2)}, u32[]{:S(2)}) collective-permute-start(f32[18,1536]{1,0:T(8,128)S(1)} %pad_maximum_fusion.8), channel_id=1, source_target_pairs={{0,1},{1,0},{2,3},{3,2},{4,5},{5,4},{6,7},{7,6},{8,9},{9,8},{10,11... | collective-permute-start | bytes 331784 | tf_op jit(solution)/shard_map/ppermute | solution.py:482
  576.9 24.2 %collective-permute-start.79 = (bf16[4,96,640]{2,1,0:T(8,128)(2,1)}, bf16[4,96,640]{2,1,0:T(8,128)(2,1)}, u32[]{:S(2)}, u32[]{:S(2)}) collective-permute-start(bf16[4,96,640]{2,1,0:T(8,128)(2,1)} %dynamic-slice_bitcast_fusion.2), channel_id=1, source_target_pairs={{0,4},{2,6},{4,0},{6,2},{8,12},{10,14},{12,8},{14,10},{16,20},{18,... | collective-permute-start | bytes 1474568 | tf_op jit(solution)/shard_map/ppermute | solution.py:461
  577.3 25.0 %collective-permute-start.80 = (bf16[4,96,640]{2,1,0:T(8,128)(2,1)}, bf16[4,96,640]{2,1,0:T(8,128)(2,1)}, u32[]{:S(2)}, u32[]{:S(2)}) collective-permute-start(bf16[4,96,640]{2,1,0:T(8,128)(2,1)} %dynamic-slice_bitcast_fusion.1), channel_id=1, source_target_pairs={{0,2},{2,0},{4,6},{6,4},{8,10},{10,8},{12,14},{14,12},{16,18},{18,... | collective-permute-start | bytes 1474568 | tf_op jit(solution)/shard_map/ppermute | solution.py:461
  585.8 33.1 %collective-permute-start.64 = (bf16[4,2,48,896]{3,2,1,0:T(8,128)(2,1)S(1)}, bf16[4,2,48,896]{3,2,1,0:T(8,128)(2,1)S(1)}, u32[]{:S(2)}, u32[]{:S(2)}) collective-permute-start(bf16[4,2,48,896]{3,2,1,0:T(8,128)(2,1)S(1)} %fusion.17), channel_id=1, source_target_pairs={{0,4},{2,6},{4,0},{6,2},{8,12},{10,14},{12,8},{14,10},{16,20},{18,... | collective-permute-start | bytes 2064392 | tf_op jit(solution)/shard_map/ppermute | solution.py:461
  605.7 31.0 %collective-permute-start.82 = (bf16[96,1280]{1,0:T(8,128)(2,1)S(1)}, bf16[96,1280]{1,0:T(8,128)(2,1)S(1)}, u32[]{:S(2)}, u32[]{:S(2)}) collective-permute-start(bf16[96,1280]{1,0:T(8,128)(2,1)S(1)} %get-tuple-element.289), channel_id=1, source_target_pairs={{0,16},{2,18},{4,20},{6,22},{8,24},{10,26},{12,28},{14,30},{16,0},... | collective-permute-start | bytes 737288 | tf_op jit(solution)/shard_map/ppermute | solution.py:477
  605.7 31.0 %collective-permute-start.83 = (bf16[96,1280]{1,0:T(8,128)(2,1)S(1)}, bf16[96,1280]{1,0:T(8,128)(2,1)S(1)}, u32[]{:S(2)}, u32[]{:S(2)}) collective-permute-start(bf16[96,1280]{1,0:T(8,128)(2,1)S(1)} %get-tuple-element.290), channel_id=1, source_target_pairs={{0,8},{2,10},{4,12},{6,14},{8,16},{10,18},{12,20},{14,22},{16,24},... | collective-permute-start | bytes 737288 | tf_op jit(solution)/shard_map/ppermute | solution.py:477
  619.2 34.3 %collective-permute-start.65 = (bf16[4,48,896]{2,1,0:T(8,128)(2,1)S(1)}, bf16[4,48,896]{2,1,0:T(8,128)(2,1)S(1)}, u32[]{:S(2)}, u32[]{:S(2)}) collective-permute-start(bf16[4,48,896]{2,1,0:T(8,128)(2,1)S(1)} %copy-done.62), channel_id=1, source_target_pairs={{0,4},{2,6},{4,0},{6,2},{8,12},{10,14},{12,8},{14,10},{16,20},{18,... | collective-permute-start | bytes 1032200 | tf_op jit(solution)/shard_map/ppermute | solution.py:461
  619.5 34.1 %collective-permute-start.66 = (bf16[4,48,896]{2,1,0:T(8,128)(2,1)S(1)}, bf16[4,48,896]{2,1,0:T(8,128)(2,1)S(1)}, u32[]{:S(2)}, u32[]{:S(2)}) collective-permute-start(bf16[4,48,896]{2,1,0:T(8,128)(2,1)S(1)} %dynamic-slice_bitcast_fusion.3), channel_id=1, source_target_pairs={{0,2},{2,0},{4,6},{6,4},{8,10},{10,8},{12,14},{14,12},{16,18},{18,... | collective-permute-start | bytes 1032200 | tf_op jit(solution)/shard_map/ppermute | solution.py:461
  637.1 44.3 %collective-permute-start.85 = (bf16[96,1280]{1,0:T(8,128)(2,1)S(1)}, bf16[96,1280]{1,0:T(8,128)(2,1)S(1)}, u32[]{:S(2)}, u32[]{:S(2)}) collective-permute-start(bf16[96,1280]{1,0:T(8,128)(2,1)S(1)} %fusion.22), channel_id=1, source_target_pairs={{0,16},{2,18},{4,20},{6,22},{8,24},{10,26},{12,28},{14,30},{16,0},... | collective-permute-start | bytes 737288 | tf_op jit(solution)/shard_map/ppermute | solution.py:477
  651.5 30.0 %collective-permute-start.84 = (bf16[96,1280]{1,0:T(8,128)(2,1)S(1)}, bf16[96,1280]{1,0:T(8,128)(2,1)S(1)}, u32[]{:S(2)}, u32[]{:S(2)}) collective-permute-start(bf16[96,1280]{1,0:T(8,128)(2,1)S(1)} %fusion.22), channel_id=1, source_target_pairs={{0,8},{2,10},{4,12},{6,14},{8,16},{10,18},{12,20},{14,22},{16,24},... | collective-permute-start | bytes 737288 | tf_op jit(solution)/shard_map/ppermute | solution.py:477
  653.7 28.1 %collective-permute-start.67 = (bf16[48,1792]{1,0:T(8,128)(2,1)S(1)}, bf16[48,1792]{1,0:T(8,128)(2,1)S(1)}, u32[]{:S(2)}, u32[]{:S(2)}) collective-permute-start(bf16[48,1792]{1,0:T(8,128)(2,1)S(1)} %get-tuple-element.305), channel_id=1, source_target_pairs={{0,24},{2,26},{4,28},{6,30},{8,0},{10,2},{12,4},{14,6},{16,8},{18,... | collective-permute-start | bytes 516104 | tf_op jit(solution)/shard_map/ppermute | solution.py:477
  655.7 32.4 %collective-permute-start.68 = (bf16[48,1792]{1,0:T(8,128)(2,1)S(1)}, bf16[48,1792]{1,0:T(8,128)(2,1)S(1)}, u32[]{:S(2)}, u32[]{:S(2)}) collective-permute-start(bf16[48,1792]{1,0:T(8,128)(2,1)S(1)} %get-tuple-element.306), channel_id=1, source_target_pairs={{0,16},{2,18},{4,20},{6,22},{8,24},{10,26},{12,28},{14,30},{16,0},... | collective-permute-start | bytes 516104 | tf_op jit(solution)/shard_map/ppermute | solution.py:477
  655.7 32.4 %collective-permute-start.69 = (bf16[48,1792]{1,0:T(8,128)(2,1)S(1)}, bf16[48,1792]{1,0:T(8,128)(2,1)S(1)}, u32[]{:S(2)}, u32[]{:S(2)}) collective-permute-start(bf16[48,1792]{1,0:T(8,128)(2,1)S(1)} %get-tuple-element.307), channel_id=1, source_target_pairs={{0,8},{2,10},{4,12},{6,14},{8,16},{10,18},{12,20},{14,22},{16,24},... | collective-permute-start | bytes 516104 | tf_op jit(solution)/shard_map/ppermute | solution.py:477
  690.7 23.8 %collective-permute-start.88 = (bf16[4,96,640]{2,1,0:T(8,128)(2,1)S(1)}, bf16[4,96,640]{2,1,0:T(8,128)(2,1)S(1)}, u32[]{:S(2)}, u32[]{:S(2)}) collective-permute-start(bf16[4,96,640]{2,1,0:T(8,128)(2,1)S(1)} %get-tuple-element.250), channel_id=1, source_target_pairs={{0,2},{2,0},{4,6},{6,4},{8,10},{10,8},{12,14},{14,12},{16,18},{18,... | collective-permute-start | bytes 1474568 | tf_op jit(solution)/shard_map/ppermute | solution.py:461
  715.6 32.9 %collective-permute-start.90 = (bf16[4,2,96,640]{3,2,0,1:T(8,128)(2,1)}, bf16[4,2,96,640]{3,2,0,1:T(8,128)(2,1)}, u32[]{:S(2)}, u32[]{:S(2)}) collective-permute-start(bf16[4,2,96,640]{3,2,0,1:T(8,128)(2,1)} %maximum_select_fusion.10), channel_id=1, source_target_pairs={{0,4},{2,6},{4,0},{6,2},{8,12},{10,14},{12,8},{14,10},{16,20},{18,... | collective-permute-start | bytes 2949128 | tf_op jit(solution)/shard_map/ppermute | solution.py:461
  717.1 33.6 %collective-permute-start.89 = (bf16[4,2,96,640]{3,2,0,1:T(8,128)(2,1)}, bf16[4,2,96,640]{3,2,0,1:T(8,128)(2,1)}, u32[]{:S(2)}, u32[]{:S(2)}) collective-permute-start(bf16[4,2,96,640]{3,2,0,1:T(8,128)(2,1)} %maximum_select_fusion.8), channel_id=1, source_target_pairs={{0,2},{2,0},{4,6},{6,4},{8,10},{10,8},{12,14},{14,12},{16,18},{18,... | collective-permute-start | bytes 2949128 | tf_op jit(solution)/shard_map/ppermute | solution.py:461
  (118 other events, 1523.5 us)
Sparse Core Ops, SparseCore 0:
  9.6 12.4 all-gather.3
  23.7 10.9 all-gather.5
  108.3 9.8 all-gather.7
  356.5 290.4 reduce-scatter.3
  649.3 15.2 reduce-scatter.5
  667.2 12.0 reduce-scatter.7
